TPU v7x, 256 devices: a whole 4x4x8 slice. The times are simulated.
256 devices in a mesh: segment: 2 (over x_lo), expert: 128 (over y, x_hi, z, core).
Axes of the slice: x: 4 (x_hi: 2, x_lo: 2; x = x_hi * 2 + x_lo), y: 4, z: 8, core: 2. Of those that a mesh axis runs over, the one named last changes fastest.
Arguments:
- boundary: bfloat16 [2, 8192, 2048], P('segment', 'expert'), may hold values from -6 to 6
- saved: bfloat16 [2, 8192, 2048], P('segment', 'expert'), may hold values from -6 to 6
- norm_gain: float32 [2, 2048], P('segment'), may hold values from 0.25 to 1.75
- gate_weight: bfloat16 [2, 128, 2048, 768], P('segment', 'expert'), may hold values from -0.125 to 0.125
- up_weight: bfloat16 [2, 128, 2048, 768], P('segment', 'expert'), may hold values from -0.125 to 0.125
- down_weight: bfloat16 [2, 128, 768, 2048], P('segment', 'expert'), may hold values from -0.21875 to 0.21875
- routes: int32 [2, 2, 8192, 8], P('segment', None, 'expert'), may hold values from 0 to 127, all different within a row; in each aligned block of 64 rows (0 to 63, 64 to 127, ..., all dimensions but the last counted through in order) at most 6 rows name the same one
- gate_codes: int32 [2, 2, 8192, 8], P('segment', None, 'expert'), may hold values from 1 to 16
Outputs:
- results: bfloat16 [2, 8192, 2048], P('segment', 'expert')
Inputs may be any that keep to these rules, and one draw needn't show every extreme that they name: `routes`: each row names 8 different experts. Among the rows of one index of expert (aligned blocks of 64 rows) no expert is named by more than 6 rows, a bound that some block reaches.
All inputs are finite; a program needn't handle non-finite values.
Results may differ from a plain program's by a relative error of at most 0.0075.
Values may be sent and summed in bfloat16 or wider, within the bound.
No kernel may reach another device: no remote copies, remote signals or barrier semaphores. Data moves between devices by JAX's collectives and lax.ppermute only.
A program may use at most 128 MiB of HBM per device.

v0:
```python
import functools

import jax
import jax.numpy as jnp
from jax import lax
from jax.experimental import pallas as pl
from jax.experimental.pallas import tpu as pltpu
from jax.sharding import Mesh
from jax.sharding import PartitionSpec as P

EXPERT = ("expert_0", "expert_1", "expert_2", "expert_3")
PLANE = ("expert_0", "expert_1", "expert_3")
RING = "expert_2"

CHUNKS = ((0, -1, 1, -2), (2, -3, 3, 4))
CAPACITY = 6

epsilon = 1e-06


def step_ring(block, step):
    count = lax.axis_size(RING)
    return lax.ppermute(block, RING, [(i, (i + step) % count) for i in range(count)])


def gather_near(own):
    blocks = {0: own}
    for distance in (1, 2):
        blocks[-distance] = step_ring(blocks[1 - distance], 1)
        blocks[distance] = step_ring(blocks[distance - 1], -1)
    return blocks


def gather_far(blocks):
    half = blocks[0].shape[0] // 2
    up, down = step_ring(blocks[-2], 1), step_ring(blocks[2], -1)
    last = jnp.concatenate((step_ring(up[:half], 1), step_ring(down[half:], -1)), axis=0)
    return {**blocks, -3: up, 3: down, 4: last}


def add(part, arrived):
    return (part.astype(jnp.float32) + arrived.astype(jnp.float32)).astype(jnp.bfloat16)


def sum_ring(parts):
    half = parts[4].shape[0] // 2
    up = step_ring(parts[4][:half], 1)
    down = step_ring(parts[4][half:], -1)
    up = jnp.concatenate((add(parts[3][:half], up), parts[3][half:]), axis=0)
    down = jnp.concatenate((parts[-3][:half], add(parts[-3][half:], down)), axis=0)
    for distance in (2, 1):
        up = add(parts[distance], step_ring(up, 1))
        down = add(parts[-distance], step_ring(down, -1))
    up, down = step_ring(up, 1), step_ring(down, -1)
    return sum(part.astype(jnp.float32) for part in (parts[0], up, down))


def exchange(rows):
    count = lax.axis_size(PLANE)
    parts = rows.reshape(count, -1, rows.shape[-1])
    moved = lax.all_to_all(parts, PLANE, split_axis=0, concat_axis=0, tiled=True)
    return moved.reshape(rows.shape)


def slots(ids, codes):
    width = ids.shape[1]
    tokens = 64
    blocks = width // tokens
    peers = lax.axis_size(PLANE)
    plane = lax.broadcasted_iota(jnp.int32, (peers, 1, 1), 0)
    named = ((plane // 2) * lax.axis_size(RING) + lax.axis_index(RING)) * 2 + plane % 2
    hit = ids[None] == named.astype(jnp.float32)
    member = jnp.sum(hit.astype(jnp.float32), axis=1)
    code = jnp.sum(jnp.where(hit, codes[None], 0.0), axis=1)
    row = lax.broadcasted_iota(jnp.int32, (width, width), 0)
    column = lax.broadcasted_iota(jnp.int32, (width, width), 1)
    earlier = ((row // tokens == column // tokens) & (row < column)).astype(jnp.bfloat16)
    rank = jnp.dot(member.astype(jnp.bfloat16), earlier, preferred_element_type=jnp.float32)
    block = lax.broadcasted_iota(jnp.int32, (1, width), 1) // tokens
    key = jnp.where(member > 0.0, (block * CAPACITY).astype(jnp.float32) + rank, -1.0)
    place = lax.broadcasted_iota(jnp.int32, (1, blocks * CAPACITY, 1), 1).astype(jnp.float32)
    found = key[:, None, :] == place
    picking = found.astype(jnp.bfloat16)
    weighing = jnp.where(found, code[:, None, :], 0.0).astype(jnp.bfloat16)
    return (picking.reshape(-1, width), weighing.reshape(-1, width))


def pick(picking, tokens):
    return jnp.dot(picking, tokens, preferred_element_type=jnp.float32).astype(jnp.bfloat16)


def combine(weighing, rows):
    return lax.dot_general(
        weighing, rows, (((0,), (0,)), ((), ())), preferred_element_type=jnp.float32
    ).astype(jnp.bfloat16)


def normalize(inputs, gain_row):
    widened = inputs.astype(jnp.float32)
    scaling = lax.rsqrt(jnp.mean(widened * widened, axis=-1, keepdims=True) + epsilon)
    return (widened, scaling, (widened * scaling * gain_row).astype(jnp.bfloat16))


def transposed(left, right):
    return lax.dot_general(
        left, right, (((1,), (1,)), ((), ())), preferred_element_type=jnp.float32
    )


def expert_kernel(
    first_at, second_at, forward_from, flag, first, second, w_gate, w_up, w_down, out, *scratch
):
    first_rows, second_rows, gate, up, down, made, done = scratch
    rows, width = first_rows.shape
    into = (
        (first.at[:, pl.ds(first_at * width, width)], first_rows),
        (second.at[:, pl.ds(second_at * width, width)], second_rows),
        (w_gate, gate),
        (w_up, up),
        (w_down, down),
    )
    copies = [
        pltpu.make_async_copy(source, target, done.at[i]) for i, (source, target) in enumerate(into)
    ]
    for copy in copies[:3]:
        copy.start()
    for copy in copies[:3]:
        copy.wait()
    for copy in copies[3:]:
        copy.start()
    forward = flag[0] == 1
    piece = width // 4
    given = [
        pltpu.make_async_copy(made.at[:, part], out.at[:, part], done.at[5 + i])
        for i, part in enumerate(pl.ds(i * piece, piece) for i in range(4))
    ]

    @pl.when(forward)
    def _():
        taken = (first_rows, second_rows)[forward_from][...]
        gate_part = jnp.dot(taken, gate[...], preferred_element_type=jnp.float32)
        copies[3].wait()
        up_part = jnp.dot(taken, up[...], preferred_element_type=jnp.float32)
        hidden = (gate_part * jax.nn.sigmoid(gate_part) * up_part).astype(jnp.bfloat16)
        copies[4].wait()
        for i, copy in enumerate(given):
            part = slice(i * piece, (i + 1) * piece)
            total = jnp.dot(hidden, down[:, part], preferred_element_type=jnp.float32)
            made[:, part] = total.astype(jnp.bfloat16)
            copy.start()

    @pl.when(jnp.logical_not(forward))
    def _():
        taken = first_rows[...]
        gate_part = jnp.dot(taken, gate[...], preferred_element_type=jnp.float32)
        copies[3].wait()
        up_part = jnp.dot(taken, up[...], preferred_element_type=jnp.float32)
        copies[4].wait()
        hidden_grad = transposed(second_rows[...], down[...])
        sigmoid_part = jax.nn.sigmoid(gate_part)
        activated = gate_part * sigmoid_part
        slope = sigmoid_part * (1.0 + gate_part * (1.0 - sigmoid_part))
        gate_grad = (hidden_grad * up_part * slope).astype(jnp.bfloat16)
        up_grad = (hidden_grad * activated).astype(jnp.bfloat16)
        for i, copy in enumerate(given):
            part = slice(i * piece, (i + 1) * piece)
            total = transposed(gate_grad, gate[part, :]) + transposed(up_grad, up[part, :])
            made[:, part] = total.astype(jnp.bfloat16)
            copy.start()

    for copy in given:
        copy.wait()


def apply_expert(flag, first, first_at, second, second_at, forward_from, weights):
    rows, (width, inner) = first.shape[0], weights[0].shape
    weights = [pltpu.with_memory_space_constraint(w, pltpu.HBM) for w in weights]
    return pl.pallas_call(
        functools.partial(expert_kernel, first_at, second_at, forward_from),
        in_specs=[pl.BlockSpec(memory_space=pltpu.SMEM)] + [pl.BlockSpec(memory_space=pl.ANY)] * 5,
        out_specs=pl.BlockSpec(memory_space=pl.ANY),
        out_shape=pltpu.HBM((rows, width), jnp.bfloat16),
        scratch_shapes=[pltpu.VMEM((rows, width), jnp.bfloat16)] * 2
        + [pltpu.VMEM(w.shape, w.dtype) for w in weights]
        + [pltpu.VMEM((rows, width), jnp.bfloat16), pltpu.SemaphoreType.DMA((9,))],
        cost_estimate=pl.CostEstimate(
            flops=10 * rows * width * inner,
            bytes_accessed=6 * width * (rows + inner),
            transcendentals=rows * inner,
        ),
        compiler_params=pltpu.CompilerParams(vmem_limit_bytes=48 * 1024 * 1024),
    )(flag, first, second, *weights)


def finish(widened, scaling, gain_row, upstream, summed, forward_flag):
    forward_out = widened + summed
    scaled = summed * gain_row
    inner_mean = jnp.mean(scaled * widened, axis=-1, keepdims=True)
    cubed = scaling * scaling * scaling
    backward_out = upstream.astype(jnp.float32) + scaling * scaled - widened * cubed * inner_mean
    return jnp.where(forward_flag, forward_out, backward_out).astype(jnp.bfloat16)


def stack(blocks, chunk):
    return jnp.concatenate([blocks[k] for k in chunk], axis=0)


def after(first, then):
    return lax.optimization_barrier((first, then))


def returned(outcomes, weighings, code_sum):
    near, far = outcomes
    far_back = exchange(far)
    far_back, near = after(far_back, near)
    near_back = exchange(near)
    parts = {}
    for chunk, back, weighing in zip(CHUNKS, (near_back, far_back), weighings):
        share = combine(weighing, back).reshape(len(chunk), -1, back.shape[-1])
        for i, k in enumerate(chunk):
            parts[k] = share[i]
    return sum_ring(parts) / code_sum


def body(boundary, saved, norm_gain, gate_weight, up_weight, down_weight, routes, gate_codes):
    first_segment = lax.axis_index("segment") == 0
    later_forward = jnp.logical_not(first_segment)
    width = boundary.shape[2]
    weights = (gate_weight[0, 0], up_weight[0, 0], down_weight[0, 0])
    gain_row = norm_gain[0]
    edge_rows = boundary[0]
    stored = saved[0]
    route_now = jnp.where(first_segment, routes[0, 0], routes[0, 1])
    codes_now = jnp.where(first_segment, gate_codes[0, 0], gate_codes[0, 1])
    route_next = jnp.where(first_segment, routes[0, 1], routes[0, 0])
    codes_next = jnp.where(first_segment, gate_codes[0, 1], gate_codes[0, 0])
    sum_now = jnp.sum(codes_now.astype(jnp.float32), axis=-1, keepdims=True)
    sum_next = jnp.sum(codes_next.astype(jnp.float32), axis=-1, keepdims=True)
    top = route_now.shape[1]
    info = jnp.concatenate((route_now, codes_now, route_next, codes_next), axis=1)
    info = jnp.pad(info.astype(jnp.bfloat16), ((0, 0), (0, 128 - 4 * top)))

    inputs_now = jnp.where(first_segment, edge_rows, stored)
    widened, scaling, normed = normalize(inputs_now, gain_row)
    stored_normed = normalize(stored, gain_row)[2]
    early_rows = jnp.where(first_segment, stored_normed, edge_rows)

    forward_first = first_segment.astype(jnp.int32).reshape(1)

    blocks = gather_near(jnp.concatenate((normed, early_rows, info), axis=1))
    pairs, place_next, weigh_now, weigh_next = [], [], [], []
    for chunk in CHUNKS:
        if pairs:
            blocks = gather_far(blocks)
        tokens = stack(blocks, chunk)
        told = jnp.transpose(tokens[:, 2 * width : 2 * width + 4 * top]).astype(jnp.float32)
        pick_now, by_now = slots(told[:top], told[top : 2 * top])
        pick_next, by_next = slots(told[2 * top : 3 * top], told[3 * top :])
        pick_early = jnp.where(first_segment, pick_next, pick_now)
        picked = jnp.concatenate(
            (
                pick(pick_now, tokens[:, :width]),
                pick(pick_early, tokens[:, width : 2 * width]),
            ),
            axis=1,
        )
        if pairs:
            pairs[-1], picked = after(pairs[-1], picked)
        else:
            picked, blocks = after(picked, blocks)
        pairs.append(exchange(picked))
        place_next.append(pick_next)
        weigh_now.append(by_now)
        weigh_next.append(by_next)
    outcomes = [apply_expert(forward_first, pair, 0, pair, 1, 0, weights) for pair in pairs]
    summed = returned(outcomes, weigh_now, sum_now)
    produced = finish(widened, scaling, gain_row, edge_rows, summed, first_segment)

    arrived = lax.ppermute(produced, "segment", [(0, 1), (1, 0)])
    inputs_next = jnp.where(first_segment, stored, arrived)
    widened_next, scaling_next, normed_next = normalize(inputs_next, gain_row)
    member_blocks = gather_far(gather_near(jnp.where(first_segment, arrived, normed_next)))
    landed = []
    for i, chunk in enumerate(CHUNKS):
        picked = pick(place_next[i], stack(member_blocks, chunk))
        if landed:
            landed[-1], picked = after(landed[-1], picked)
        landed.append(exchange(picked))
    outcomes = [
        apply_expert(1 - forward_first, pair, 1, rows, 0, 1, weights)
        for pair, rows in zip(pairs, landed)
    ]
    summed = returned(outcomes, weigh_next, sum_next)
    result = finish(widened_next, scaling_next, gain_row, arrived, summed, later_forward)
    return result[None]


def solution(mesh):
    finer = Mesh(
        mesh.devices.reshape(mesh.shape["segment"], 4, 2, 8, 2),
        ("segment", "expert_0", "expert_1", "expert_2", "expert_3"),
    )
    placed = (
        P("segment", EXPERT, None),
        P("segment", EXPERT, None),
        P("segment", None),
        P("segment", EXPERT, None, None),
        P("segment", EXPERT, None, None),
        P("segment", EXPERT, None, None),
        P("segment", None, EXPERT, None),
        P("segment", None, EXPERT, None),
    )
    return jax.shard_map(
        body, mesh=finer, in_specs=placed, out_specs=P("segment", EXPERT, None), check_vma=False
    )
```

profile of v0, /device:TPU:96, one launch (start us, length us, event | category | flops | bytes accessed | tf_op | source)
XLA Modules:
  0.0 412.1 jit_solution(8201943604749019761)
XLA Ops:
  5.8 3.2 collective-permute-start
  9.0 11.5 %collective-permute-done = bf16[64,4224]{1,0:T(8,128)(2,1)S(1)} collective-permute-done((bf16[64,4224]{1,0:T(8,128)(2,1)S(1)}, bf16[64,4224]{1,0:T(8,128)(2,1)S(1)}, u32[]{:S(2)}, u32[]{:S(2)}) %collective-permute-start) | collective-permute-done | bytes 540704 | tf_op jit(solution)/shard_map/ppermute | solution.py:23
  20.6 3.7 collective-permute-start.2
  24.8 10.1 %collective-permute-done.2 = bf16[64,4224]{1,0:T(8,128)(2,1)} collective-permute-done((bf16[64,4224]{1,0:T(8,128)(2,1)S(1)}, bf16[64,4224]{1,0:T(8,128)(2,1)}, u32[]{:S(2)}, u32[]{:S(2)}) %collective-permute-start.2) | collective-permute-done | bytes 540704 | tf_op jit(solution)/shard_map/ppermute | solution.py:23
  37.8 1.7 convolution_convert_fusion.4
  41.2 2.0 pad_maximum_fusion
  43.1 3.8 collective-permute-start.4
  46.9 7.0 %all-to-all-start = ((bf16[16,24,4096]{2,1,0:T(8,128)(2,1)}), bf16[16,24,4096]{2,1,0:T(8,128)(2,1)S(1)}, u32[]{:S(2)}, u32[]{:S(2)}) async-start(bf16[16,24,4096]{2,1,0:T(8,128)(2,1)} %bitcast.103), calls=%async_computation | async-start | bytes 6291456 | tf_op jit(solution)/shard_map/all_to_all | solution.py:61
  55.1 1.9 collective-permute-done.4
  58.0 3.8 collective-permute-start.6
  65.8 4.9 %collective-permute-done.7 = bf16[32,4224]{1,0:T(8,128)(2,1)S(1)} collective-permute-done((bf16[32,4224]{1,0:T(8,128)(2,1)S(1)}, bf16[32,4224]{1,0:T(8,128)(2,1)S(1)}, u32[]{:S(2)}, u32[]{:S(2)}) %collective-permute-start.7) | collective-permute-done | bytes 270368 | tf_op jit(solution)/shard_map/ppermute | solution.py:23
  78.7 1.8 convolution_convert_fusion.3
  80.5 1.8 convolution_convert_fusion.2
  82.3 2.0 pad_maximum_fusion.1
  84.3 10.2 %all-to-all-done = bf16[16,24,4096]{2,1,0:T(8,128)(2,1)S(1)} async-done(((bf16[16,24,4096]{2,1,0:T(8,128)(2,1)}), bf16[16,24,4096]{2,1,0:T(8,128)(2,1)S(1)}, u32[]{:S(2)}, u32[]{:S(2)}) %all-to-all-start) | async-done | bytes 3145760 | tf_op jit(solution)/shard_map/all_to_all | solution.py:61
  94.6 4.5 %all-to-all-start.1 = ((bf16[16,24,4096]{2,1,0:T(8,128)(2,1)}), bf16[16,24,4096]{2,1,0:T(8,128)(2,1)}, u32[]{:S(2)}, u32[]{:S(2)}) async-start(bf16[16,24,4096]{2,1,0:T(8,128)(2,1)} %bitcast.104), calls=%async_computation.1 | async-start | bytes 6291456 | tf_op jit(solution)/shard_map/all_to_all | solution.py:61
  99.1 40.6 %all-to-all-done.1 = bf16[16,24,4096]{2,1,0:T(8,128)(2,1)} async-done(((bf16[16,24,4096]{2,1,0:T(8,128)(2,1)}), bf16[16,24,4096]{2,1,0:T(8,128)(2,1)}, u32[]{:S(2)}, u32[]{:S(2)}) %all-to-all-start.1) | async-done | bytes 3145760 | tf_op jit(solution)/shard_map/all_to_all | solution.py:61
  139.7 8.9 %shard_map.82 = bf16[384,2048]{1,0:T(8,128)(2,1)} custom-call(s32[1]{0:T(128)} %bitcast.8.flag, bf16[384,4096]{1,0:T(8,128)(2,1)} %bitcast.17.first.second, bf16[384,4096]{1,0:T(8,128)(2,1)} %bitcast.17.first.second, bf16[2048,768]{1,0:T(8,128)(2,1)} %bitcast.117, bf16[2048,768]{1,0:T(8,128)(2,1)} %bitcast.121, bf16[768,2048]{1,0:T(8,128)(2,1)} %bitcast.125), custom_call_target="tpu_custom_call" | custom-call | flops 6039797760 | bytes 14155776 | tf_op jit(solution)/shard_map/pallas_call | solution.py:178
  148.5 4.4 %all-to-all-start.2 = ((bf16[16,24,2048]{2,1,0:T(8,128)(2,1)}), bf16[16,24,2048]{2,1,0:T(8,128)(2,1)}, u32[]{:S(2)}, u32[]{:S(2)}) async-start(bf16[16,24,2048]{2,1,0:T(8,128)(2,1)} %bitcast.109), calls=%async_computation.2 | async-start | bytes 3145728 | tf_op jit(solution)/shard_map/all_to_all | solution.py:61
  152.9 8.2 %shard_map.83 = bf16[384,2048]{1,0:T(8,128)(2,1)} custom-call(s32[1]{0:T(128)} %bitcast.8.flag, bf16[384,4096]{1,0:T(8,128)(2,1)S(1)} %bitcast.100, bf16[384,4096]{1,0:T(8,128)(2,1)S(1)} %bitcast.101, bf16[2048,768]{1,0:T(8,128)(2,1)} %bitcast.118, bf16[2048,768]{1,0:T(8,128)(2,1)} %bitcast.122, bf16[768,2048]{1,0:T(8,128)(2,1)} %bitcast.126), custom_call_target="tpu_custom_call" | custom-call | flops 6039797760 | bytes 14155776 | tf_op jit(solution)/shard_map/pallas_call | solution.py:178
  161.2 15.4 %all-to-all-done.2 = bf16[16,24,2048]{2,1,0:T(8,128)(2,1)} async-done(((bf16[16,24,2048]{2,1,0:T(8,128)(2,1)}), bf16[16,24,2048]{2,1,0:T(8,128)(2,1)}, u32[]{:S(2)}, u32[]{:S(2)}) %all-to-all-start.2) | async-done | bytes 1572896 | tf_op jit(solution)/shard_map/all_to_all | solution.py:61
  176.6 2.1 convolution_convert_fusion.7
  180.5 3.2 collective-permute-start.8
  183.8 4.4 %all-to-all-start.3 = ((bf16[16,24,2048]{2,1,0:T(8,128)(2,1)}), bf16[16,24,2048]{2,1,0:T(8,128)(2,1)}, u32[]{:S(2)}, u32[]{:S(2)}) async-start(bf16[16,24,2048]{2,1,0:T(8,128)(2,1)} %bitcast.106), calls=%async_computation.3 | async-start | bytes 3145728 | tf_op jit(solution)/shard_map/all_to_all | solution.py:61
  188.2 2.0 collective-permute-done.12
  194.7 4.0 collective-permute-done.9
  199.7 3.8 collective-permute-start.10
  203.5 8.4 %all-to-all-done.3 = bf16[16,24,2048]{2,1,0:T(8,128)(2,1)} async-done(((bf16[16,24,2048]{2,1,0:T(8,128)(2,1)}), bf16[16,24,2048]{2,1,0:T(8,128)(2,1)}, u32[]{:S(2)}, u32[]{:S(2)}) %all-to-all-start.3) | async-done | bytes 1572896 | tf_op jit(solution)/shard_map/all_to_all | solution.py:61
  211.9 2.2 fusion
  215.5 3.3 collective-permute-start.11
  218.8 6.0 %collective-permute-done.14 = bf16[64,2048]{1,0:T(8,128)(2,1)S(1)} collective-permute-done((bf16[64,2048]{1,0:T(8,128)(2,1)S(1)}, bf16[64,2048]{1,0:T(8,128)(2,1)S(1)}, u32[]{:S(2)}, u32[]{:S(2)}) %collective-permute-start.14) | collective-permute-done | bytes 262176 | tf_op jit(solution)/shard_map/ppermute | solution.py:23
  225.6 7.7 %collective-permute-done.15 = bf16[64,2048]{1,0:T(8,128)(2,1)S(1)} collective-permute-done((bf16[64,2048]{1,0:T(8,128)(2,1)S(1)}, bf16[64,2048]{1,0:T(8,128)(2,1)S(1)}, u32[]{:S(2)}, u32[]{:S(2)}) %collective-permute-start.15) | collective-permute-done | bytes 262176 | tf_op jit(solution)/shard_map/ppermute | solution.py:23
  234.1 3.9 collective-permute-start.16
  237.9 4.5 %collective-permute-done.16 = bf16[64,2048]{1,0:T(8,128)(2,1)S(1)} collective-permute-done((bf16[64,2048]{1,0:T(8,128)(2,1)S(1)}, bf16[64,2048]{1,0:T(8,128)(2,1)S(1)}, u32[]{:S(2)}, u32[]{:S(2)}) %collective-permute-start.16) | collective-permute-done | bytes 262176 | tf_op jit(solution)/shard_map/ppermute | solution.py:279
  243.5 2.0 collective-permute-start.18
  245.5 5.4 %collective-permute-done.17 = bf16[64,2048]{1,0:T(8,128)(2,1)S(1)} collective-permute-done((bf16[64,2048]{1,0:T(8,128)(2,1)S(1)}, bf16[64,2048]{1,0:T(8,128)(2,1)S(1)}, u32[]{:S(2)}, u32[]{:S(2)}) %collective-permute-start.17) | collective-permute-done | bytes 262176 | tf_op jit(solution)/shard_map/ppermute | solution.py:23
  251.2 1.7 collective-permute-start.20
  252.9 4.3 %collective-permute-done.19 = bf16[64,2048]{1,0:T(8,128)(2,1)S(1)} collective-permute-done((bf16[64,2048]{1,0:T(8,128)(2,1)S(1)}, bf16[64,2048]{1,0:T(8,128)(2,1)S(1)}, u32[]{:S(2)}, u32[]{:S(2)}) %collective-permute-start.19) | collective-permute-done | bytes 262176 | tf_op jit(solution)/shard_map/ppermute | solution.py:23
  257.3 2.8 convolution_convert_fusion.1
  260.1 5.4 %all-to-all-start.4 = ((bf16[16,24,2048]{2,1,0:T(8,128)(2,1)}), bf16[16,24,2048]{2,1,0:T(8,128)(2,1)}, u32[]{:S(2)}, u32[]{:S(2)}) async-start(bf16[16,24,2048]{2,1,0:T(8,128)(2,1)} %bitcast.107), calls=%async_computation.4 | async-start | bytes 3145728 | tf_op jit(solution)/shard_map/all_to_all | solution.py:61
  265.5 2.8 collective-permute-start.21
  269.3 5.3 %collective-permute-done.21 = bf16[64,2048]{1,0:T(8,128)(2,1)S(1)} collective-permute-done((bf16[64,2048]{1,0:T(8,128)(2,1)}, bf16[64,2048]{1,0:T(8,128)(2,1)S(1)}, u32[]{:S(2)}, u32[]{:S(2)}) %collective-permute-start.21) | collective-permute-done | bytes 262176 | tf_op jit(solution)/shard_map/ppermute | solution.py:23
  274.6 3.7 collective-permute-start.23
  278.6 2.2 collective-permute-done.23
  280.8 3.9 collective-permute-done.24
  284.7 1.8 convolution_convert_fusion
  286.5 2.7 all-to-all-done.4
  289.2 4.4 %all-to-all-start.5 = ((bf16[16,24,2048]{2,1,0:T(8,128)(2,1)}), bf16[16,24,2048]{2,1,0:T(8,128)(2,1)}, u32[]{:S(2)}, u32[]{:S(2)}) async-start(bf16[16,24,2048]{2,1,0:T(8,128)(2,1)} %bitcast.105), calls=%async_computation.5 | async-start | bytes 3145728 | tf_op jit(solution)/shard_map/all_to_all | solution.py:61
  293.6 23.7 %all-to-all-done.5 = bf16[16,24,2048]{2,1,0:T(8,128)(2,1)} async-done(((bf16[16,24,2048]{2,1,0:T(8,128)(2,1)}), bf16[16,24,2048]{2,1,0:T(8,128)(2,1)}, u32[]{:S(2)}, u32[]{:S(2)}) %all-to-all-start.5) | async-done | bytes 1572896 | tf_op jit(solution)/shard_map/all_to_all | solution.py:61
  317.3 11.8 %shard_map.84 = bf16[384,2048]{1,0:T(8,128)(2,1)} custom-call(s32[1]{0:T(128)S(6)} %sub.66.flag, bf16[384,4096]{1,0:T(8,128)(2,1)} %bitcast.17.first.second, bf16[384,2048]{1,0:T(8,128)(2,1)} %bitcast.29.second, bf16[2048,768]{1,0:T(8,128)(2,1)} %bitcast.119, bf16[2048,768]{1,0:T(8,128)(2,1)} %bitcast.123, bf16[768,2048]{1,0:T(8,128)(2,1)} %bitcast.127), custom_call_target="tpu_custom_call" | custom-call | flops 6039797760 | bytes 14155776 | tf_op jit(solution)/shard_map/pallas_call | solution.py:178
  329.1 4.4 %all-to-all-start.6 = ((bf16[16,24,2048]{2,1,0:T(8,128)(2,1)}), bf16[16,24,2048]{2,1,0:T(8,128)(2,1)}, u32[]{:S(2)}, u32[]{:S(2)}) async-start(bf16[16,24,2048]{2,1,0:T(8,128)(2,1)} %bitcast.108), calls=%async_computation.6 | async-start | bytes 3145728 | tf_op jit(solution)/shard_map/all_to_all | solution.py:61
  333.5 11.5 %shard_map.85 = bf16[384,2048]{1,0:T(8,128)(2,1)} custom-call(s32[1]{0:T(128)S(6)} %sub.66.flag, bf16[384,4096]{1,0:T(8,128)(2,1)S(1)} %bitcast.102, bf16[384,2048]{1,0:T(8,128)(2,1)} %bitcast.27.second, bf16[2048,768]{1,0:T(8,128)(2,1)} %bitcast.120, bf16[2048,768]{1,0:T(8,128)(2,1)} %bitcast.124, bf16[768,2048]{1,0:T(8,128)(2,1)} %bitcast.128), custom_call_target="tpu_custom_call" | custom-call | flops 6039797760 | bytes 14155776 | tf_op jit(solution)/shard_map/pallas_call | solution.py:178
  345.0 12.2 %all-to-all-done.6 = bf16[16,24,2048]{2,1,0:T(8,128)(2,1)} async-done(((bf16[16,24,2048]{2,1,0:T(8,128)(2,1)}), bf16[16,24,2048]{2,1,0:T(8,128)(2,1)}, u32[]{:S(2)}, u32[]{:S(2)}) %all-to-all-start.6) | async-done | bytes 1572896 | tf_op jit(solution)/shard_map/all_to_all | solution.py:61
  357.2 2.2 convolution_convert_fusion.6
  359.6 2.8 collective-permute-start.25
  362.3 3.7 all-to-all-start.7
  366.1 2.5 collective-permute-done.29
  371.1 1.6 collective-permute-start.30
  372.7 3.7 collective-permute-done.26
  376.5 3.8 collective-permute-start.27
  380.2 9.4 %all-to-all-done.7 = bf16[16,24,2048]{2,1,0:T(8,128)(2,1)S(1)} async-done(((bf16[16,24,2048]{2,1,0:T(8,128)(2,1)}), bf16[16,24,2048]{2,1,0:T(8,128)(2,1)S(1)}, u32[]{:S(2)}, u32[]{:S(2)}) %all-to-all-start.7) | async-done | bytes 1572896 | tf_op jit(solution)/shard_map/all_to_all | solution.py:61
  392.6 3.3 collective-permute-start.28
  395.9 6.0 %collective-permute-done.31 = bf16[64,2048]{1,0:T(8,128)(2,1)S(1)} collective-permute-done((bf16[64,2048]{1,0:T(8,128)(2,1)S(1)}, bf16[64,2048]{1,0:T(8,128)(2,1)S(1)}, u32[]{:S(2)}, u32[]{:S(2)}) %collective-permute-start.31) | collective-permute-done | bytes 262176 | tf_op jit(solution)/shard_map/ppermute | solution.py:23
  402.0 8.4 %collective-permute-done.32 = bf16[64,2048]{1,0:T(8,128)(2,1)S(1)} collective-permute-done((bf16[64,2048]{1,0:T(8,128)(2,1)S(1)}, bf16[64,2048]{1,0:T(8,128)(2,1)S(1)}, u32[]{:S(2)}, u32[]{:S(2)}) %collective-permute-start.32) | collective-permute-done | bytes 262176 | tf_op jit(solution)/shard_map/ppermute | solution.py:23
  (183 shorter events, 44.3 us)
Async XLA Ops:
  0.8 23.8 %copy-start.11 = (s32[1,1,64,8]{3,2,1,0:T(8,128)}, s32[1,1,64,8]{3,2,1,0:T(8,128)S(1)}, u32[]{:S(2)}) copy-start(s32[1,1,64,8]{3,2,1,0:T(8,128)S(1)} %copy.36) | copy-start | bytes 6148
  0.9 23.7 %copy-start.13 = (s32[1,1,64,8]{3,2,1,0:T(8,128)}, s32[1,1,64,8]{3,2,1,0:T(8,128)S(1)}, u32[]{:S(2)}) copy-start(s32[1,1,64,8]{3,2,1,0:T(8,128)S(1)} %copy.35) | copy-start | bytes 6148
  3.0 32.6 %copy-start.1 = (bf16[64,2048]{1,0:T(8,128)(2,1)}, bf16[64,2048]{1,0:T(8,128)(2,1)S(1)}, u32[]{:S(2)}) copy-start(bf16[64,2048]{1,0:T(8,128)(2,1)S(1)} %get-tuple-element.42) | copy-start | bytes 786436
  5.8 14.7 %collective-permute-start = (bf16[64,4224]{1,0:T(8,128)(2,1)S(1)}, bf16[64,4224]{1,0:T(8,128)(2,1)S(1)}, u32[]{:S(2)}, u32[]{:S(2)}) collective-permute-start(bf16[64,4224]{1,0:T(8,128)(2,1)S(1)} %pad_maximum_fusion.12), channel_id=1, source_target_pairs={{0,2},{2,4},{4,6},{6,8},{8,10},{10,12},{12,14},{14,0},{1,3},{3,5},... | collective-permute-start | bytes 1622024 | tf_op jit(solution)/shard_map/ppermute | solution.py:23
  9.0 15.4 %collective-permute-start.1 = (bf16[64,4224]{1,0:T(8,128)(2,1)S(1)}, bf16[64,4224]{1,0:T(8,128)(2,1)S(1)}, u32[]{:S(2)}, u32[]{:S(2)}) collective-permute-start(bf16[64,4224]{1,0:T(8,128)(2,1)S(1)} %pad_maximum_fusion.12), channel_id=1, source_target_pairs={{0,14},{2,0},{4,2},{6,4},{8,6},{10,8},{12,10},{14,12},{1,15},{3,1}... | collective-permute-start | bytes 1622024 | tf_op jit(solution)/shard_map/ppermute | solution.py:23
  20.6 16.7 %copy-start.8 = (bf16[64,4224]{1,0:T(8,128)(2,1)}, bf16[64,4224]{1,0:T(8,128)(2,1)S(1)}, u32[]{:S(2)}) copy-start(bf16[64,4224]{1,0:T(8,128)(2,1)S(1)} %collective-permute-done) | copy-start | bytes 1622020
  20.6 14.4 %collective-permute-start.2 = (bf16[64,4224]{1,0:T(8,128)(2,1)S(1)}, bf16[64,4224]{1,0:T(8,128)(2,1)}, u32[]{:S(2)}, u32[]{:S(2)}) collective-permute-start(bf16[64,4224]{1,0:T(8,128)(2,1)S(1)} %collective-permute-done), channel_id=1, source_target_pairs={{0,2},{2,4},{4,6},{6,8},{8,10},{10,12},{12,14},{14,0},{1,3},{3,5},... | collective-permute-start | bytes 1622024 | tf_op jit(solution)/shard_map/ppermute | solution.py:23
  24.4 12.9 %copy-start.34 = (pred[256]{0:T(512)(128)(4,1)}, pred[256]{0:T(512)(128)(4,1)S(1)}, u32[]{:S(2)}) copy-start(pred[256]{0:T(512)(128)(4,1)S(1)} %compare_and_fusion) | copy-start | bytes 772
  24.4 12.9 %copy-start.25 = (f32[16]{0:T(128)}, f32[16]{0:T(128)S(1)}, u32[]{:S(2)}) copy-start(f32[16]{0:T(128)S(1)} %fusion.90) | copy-start | bytes 196
  24.4 12.9 %copy-start.33 = (s32[256]{0:T(256)}, s32[256]{0:T(256)S(1)}, u32[]{:S(2)}) copy-start(s32[256]{0:T(256)S(1)} %fusion.88) | copy-start | bytes 3076
  24.4 12.9 %copy-start.27 = (s32[256]{0:T(256)}, s32[256]{0:T(256)S(1)}, u32[]{:S(2)}) copy-start(s32[256]{0:T(256)S(1)} %get-tuple-element.90) | copy-start | bytes 3076
  24.4 12.9 %copy-start.28 = (f32[256]{0:T(256)}, f32[256]{0:T(256)S(1)}, u32[]{:S(2)}) copy-start(f32[256]{0:T(256)S(1)} %get-tuple-element.91) | copy-start | bytes 3076
  24.5 18.7 %collective-permute-start.3 = (bf16[64,4224]{1,0:T(8,128)(2,1)S(1)}, bf16[64,4224]{1,0:T(8,128)(2,1)}, u32[]{:S(2)}, u32[]{:S(2)}) collective-permute-start(bf16[64,4224]{1,0:T(8,128)(2,1)S(1)} %collective-permute-done.1), channel_id=1, source_target_pairs={{0,14},{2,0},{4,2},{6,4},{8,6},{10,8},{12,10},{14,12},{1,15},{3,1}... | collective-permute-start | bytes 1622024 | tf_op jit(solution)/shard_map/ppermute | solution.py:23
  43.1 13.9 %collective-permute-start.4 = (bf16[64,4224]{1,0:T(8,128)(2,1)}, bf16[64,4224]{1,0:T(8,128)(2,1)}, u32[]{:S(2)}, u32[]{:S(2)}) collective-permute-start(bf16[64,4224]{1,0:T(8,128)(2,1)} %collective-permute-done.2), channel_id=1, source_target_pairs={{0,2},{2,4},{4,6},{6,8},{8,10},{10,12},{12,14},{14,0},{1,3},{3,5},... | collective-permute-start | bytes 1622024 | tf_op jit(solution)/shard_map/ppermute | solution.py:23
  46.9 14.8 %collective-permute-start.5 = (bf16[64,4224]{1,0:T(8,128)(2,1)}, bf16[64,4224]{1,0:T(8,128)(2,1)}, u32[]{:S(2)}, u32[]{:S(2)}) collective-permute-start(bf16[64,4224]{1,0:T(8,128)(2,1)} %collective-permute-done.3), channel_id=1, source_target_pairs={{0,14},{2,0},{4,2},{6,4},{8,6},{10,8},{12,10},{14,12},{1,15},{3,1}... | collective-permute-start | bytes 1622024 | tf_op jit(solution)/shard_map/ppermute | solution.py:23
  46.9 47.6 %all-to-all-start = ((bf16[16,24,4096]{2,1,0:T(8,128)(2,1)}), bf16[16,24,4096]{2,1,0:T(8,128)(2,1)S(1)}, u32[]{:S(2)}, u32[]{:S(2)}) async-start(bf16[16,24,4096]{2,1,0:T(8,128)(2,1)} %bitcast.103), calls=%async_computation | async-start | bytes 6291456 | tf_op jit(solution)/shard_map/all_to_all | solution.py:61
  58.0 7.7 %collective-permute-start.6 = (bf16[32,4224]{1,0:T(8,128)(2,1)S(1)}, bf16[32,4224]{1,0:T(8,128)(2,1)S(1)}, u32[]{:S(2)}, u32[]{:S(2)}) collective-permute-start(bf16[32,4224]{1,0:T(8,128)(2,1)S(1)} %slice.223), channel_id=1, source_target_pairs={{0,2},{2,4},{4,6},{6,8},{8,10},{10,12},{12,14},{14,0},{1,3},{3,5},... | collective-permute-start | bytes 811016 | tf_op jit(solution)/shard_map/ppermute | solution.py:23
  62.7 7.9 %collective-permute-start.7 = (bf16[32,4224]{1,0:T(8,128)(2,1)S(1)}, bf16[32,4224]{1,0:T(8,128)(2,1)S(1)}, u32[]{:S(2)}, u32[]{:S(2)}) collective-permute-start(bf16[32,4224]{1,0:T(8,128)(2,1)S(1)} %slice.224), channel_id=1, source_target_pairs={{0,14},{2,0},{4,2},{6,4},{8,6},{10,8},{12,10},{14,12},{1,15},{3,1}... | collective-permute-start | bytes 811016 | tf_op jit(solution)/shard_map/ppermute | solution.py:23
  94.6 45.1 %all-to-all-start.1 = ((bf16[16,24,4096]{2,1,0:T(8,128)(2,1)}), bf16[16,24,4096]{2,1,0:T(8,128)(2,1)}, u32[]{:S(2)}, u32[]{:S(2)}) async-start(bf16[16,24,4096]{2,1,0:T(8,128)(2,1)} %bitcast.104), calls=%async_computation.1 | async-start | bytes 6291456 | tf_op jit(solution)/shard_map/all_to_all | solution.py:61
  148.5 28.1 %all-to-all-start.2 = ((bf16[16,24,2048]{2,1,0:T(8,128)(2,1)}), bf16[16,24,2048]{2,1,0:T(8,128)(2,1)}, u32[]{:S(2)}, u32[]{:S(2)}) async-start(bf16[16,24,2048]{2,1,0:T(8,128)(2,1)} %bitcast.109), calls=%async_computation.2 | async-start | bytes 3145728 | tf_op jit(solution)/shard_map/all_to_all | solution.py:61
  180.5 7.7 %collective-permute-start.8 = (bf16[32,2048]{1,0:T(8,128)(2,1)}, bf16[32,2048]{1,0:T(8,128)(2,1)}, u32[]{:S(2)}, u32[]{:S(2)}) collective-permute-start(bf16[32,2048]{1,0:T(8,128)(2,1)} %get-tuple-element.55), channel_id=1, source_target_pairs={{0,2},{2,4},{4,6},{6,8},{8,10},{10,12},{12,14},{14,0},{1,3},{3,5},... | collective-permute-start | bytes 393224 | tf_op jit(solution)/shard_map/ppermute | solution.py:23
  183.8 6.5 %collective-permute-start.12 = (bf16[32,2048]{1,0:T(8,128)(2,1)}, bf16[32,2048]{1,0:T(8,128)(2,1)}, u32[]{:S(2)}, u32[]{:S(2)}) collective-permute-start(bf16[32,2048]{1,0:T(8,128)(2,1)} %get-tuple-element.56), channel_id=1, source_target_pairs={{0,14},{2,0},{4,2},{6,4},{8,6},{10,8},{12,10},{14,12},{1,15},{3,1}... | collective-permute-start | bytes 393224 | tf_op jit(solution)/shard_map/ppermute | solution.py:23
  183.8 28.1 %all-to-all-start.3 = ((bf16[16,24,2048]{2,1,0:T(8,128)(2,1)}), bf16[16,24,2048]{2,1,0:T(8,128)(2,1)}, u32[]{:S(2)}, u32[]{:S(2)}) async-start(bf16[16,24,2048]{2,1,0:T(8,128)(2,1)} %bitcast.106), calls=%async_computation.3 | async-start | bytes 3145728 | tf_op jit(solution)/shard_map/all_to_all | solution.py:61
  188.2 23.7 %copy-start.19 = (f32[16,256]{1,0:T(8,128)S(1)}, f32[16,256]{1,0:T(8,128)}, u32[]{:S(2)}) copy-start(f32[16,256]{1,0:T(8,128)} %copy-done.18) | copy-start | bytes 49156
  188.2 23.7 %copy-start.21 = (bf16[16,256]{1,0:T(8,128)(2,1)S(1)}, bf16[16,256]{1,0:T(8,128)(2,1)}, u32[]{:S(2)}) copy-start(bf16[16,256]{1,0:T(8,128)(2,1)} %get-tuple-element.38) | copy-start | bytes 24580
  188.2 23.7 %copy-start.31 = (f32[24]{0:T(128)S(1)}, f32[24]{0:T(128)}, u32[]{:S(2)}) copy-start(f32[24]{0:T(128)} %copy-done.30) | copy-start | bytes 292
  191.4 7.2 %collective-permute-start.9 = (bf16[64,2048]{1,0:T(8,128)(2,1)S(1)}, bf16[64,2048]{1,0:T(8,128)(2,1)S(1)}, u32[]{:S(2)}, u32[]{:S(2)}) collective-permute-start(bf16[64,2048]{1,0:T(8,128)(2,1)S(1)} %pad_maximum_fusion.13), channel_id=1, source_target_pairs={{0,2},{2,4},{4,6},{6,8},{8,10},{10,12},{12,14},{14,0},{1,3},{3,5},... | collective-permute-start | bytes 786440 | tf_op jit(solution)/shard_map/ppermute | solution.py:23
  193.5 20.7 %collective-permute-start.13 = (bf16[64,2048]{1,0:T(8,128)(2,1)}, bf16[64,2048]{1,0:T(8,128)(2,1)}, u32[]{:S(2)}, u32[]{:S(2)}) collective-permute-start(bf16[64,2048]{1,0:T(8,128)(2,1)} %pad_maximum_fusion.14), channel_id=1, source_target_pairs={{0,14},{2,0},{4,2},{6,4},{8,6},{10,8},{12,10},{14,12},{1,15},{3,1}... | collective-permute-start | bytes 786440 | tf_op jit(solution)/shard_map/ppermute | solution.py:23
  199.7 14.5 %collective-permute-start.10 = (bf16[64,2048]{1,0:T(8,128)(2,1)S(1)}, bf16[64,2048]{1,0:T(8,128)(2,1)}, u32[]{:S(2)}, u32[]{:S(2)}) collective-permute-start(bf16[64,2048]{1,0:T(8,128)(2,1)S(1)} %add_convert_fusion.7), channel_id=1, source_target_pairs={{0,2},{2,4},{4,6},{6,8},{8,10},{10,12},{12,14},{14,0},{1,3},{3,5},... | collective-permute-start | bytes 786440 | tf_op jit(solution)/shard_map/ppermute | solution.py:23
  214.1 19.2 %copy-start.2 = (bf16[64,2048]{1,0:T(8,128)(2,1)S(1)}, bf16[64,2048]{1,0:T(8,128)(2,1)}, u32[]{:S(2)}) copy-start(bf16[64,2048]{1,0:T(8,128)(2,1)} %copy-done.1) | copy-start | bytes 786436
  214.1 19.2 %copy-start.10 = (f32[1,2048]{1,0:T(1,128)S(1)}, f32[1,2048]{1,0:T(1,128)}, u32[]{:S(2)}) copy-start(f32[1,2048]{1,0:T(1,128)} %param.10) | copy-start | bytes 24580
  214.1 19.5 %copy-start.7 = (bf16[1,64,2048]{2,1,0:T(8,128)(2,1)S(1)}, bf16[1,64,2048]{2,1,0:T(8,128)(2,1)}, u32[]{:S(2)}) copy-start(bf16[1,64,2048]{2,1,0:T(8,128)(2,1)} %param.8) | copy-start | bytes 786436
  214.2 19.5 %copy-start.26 = (f32[64]{0:T(128)S(1)}, f32[64]{0:T(128)}, u32[]{:S(2)}) copy-start(f32[64]{0:T(128)} %get-tuple-element.85) | copy-start | bytes 772
  215.4 27.1 %copy-start = (bf16[1,64,2048]{2,1,0:T(8,128)(2,1)S(1)}, bf16[1,64,2048]{2,1,0:T(8,128)(2,1)}, u32[]{:S(2)}) copy-start(bf16[1,64,2048]{2,1,0:T(8,128)(2,1)} %param.9) | copy-start | bytes 786436
  215.4 9.4 %collective-permute-start.14 = (bf16[64,2048]{1,0:T(8,128)(2,1)S(1)}, bf16[64,2048]{1,0:T(8,128)(2,1)S(1)}, u32[]{:S(2)}, u32[]{:S(2)}) collective-permute-start(bf16[64,2048]{1,0:T(8,128)(2,1)S(1)} %get-tuple-element.52), channel_id=1, source_target_pairs={{0,14},{2,0},{4,2},{6,4},{8,6},{10,8},{12,10},{14,12},{1,15},{3,1}... | collective-permute-start | bytes 786440 | tf_op jit(solution)/shard_map/ppermute | solution.py:23
  215.5 10.1 %collective-permute-start.11 = (bf16[64,2048]{1,0:T(8,128)(2,1)S(1)}, bf16[64,2048]{1,0:T(8,128)(2,1)S(1)}, u32[]{:S(2)}, u32[]{:S(2)}) collective-permute-start(bf16[64,2048]{1,0:T(8,128)(2,1)S(1)} %get-tuple-element.51), channel_id=1, source_target_pairs={{0,2},{2,4},{4,6},{6,8},{8,10},{10,12},{12,14},{14,0},{1,3},{3,5},... | collective-permute-start | bytes 786440 | tf_op jit(solution)/shard_map/ppermute | solution.py:23
  224.8 32.4 %copy-start.16 = (pred[384,256]{1,0:T(32,128)(4,1)S(1)}, pred[384,256]{1,0:T(32,128)(4,1)}, u32[]{:S(2)}) copy-start(pred[384,256]{1,0:T(32,128)(4,1)} %copy-done.15) | copy-start | bytes 294916
  224.9 8.5 %collective-permute-start.15 = (bf16[64,2048]{1,0:T(8,128)(2,1)S(1)}, bf16[64,2048]{1,0:T(8,128)(2,1)S(1)}, u32[]{:S(2)}, u32[]{:S(2)}) collective-permute-start(bf16[64,2048]{1,0:T(8,128)(2,1)S(1)} %add_convert_fusion.4), channel_id=1, source_target_pairs={{0,14},{2,0},{4,2},{6,4},{8,6},{10,8},{12,10},{14,12},{1,15},{3,1}... | collective-permute-start | bytes 786440 | tf_op jit(solution)/shard_map/ppermute | solution.py:23
  234.1 8.4 %collective-permute-start.16 = (bf16[64,2048]{1,0:T(8,128)(2,1)S(1)}, bf16[64,2048]{1,0:T(8,128)(2,1)S(1)}, u32[]{:S(2)}, u32[]{:S(2)}) collective-permute-start(bf16[64,2048]{1,0:T(8,128)(2,1)S(1)} %fusion.34), channel_id=1, source_target_pairs={{0,128},{128,0},{1,129},{129,1},{2,130},{130,2},{3,131},{131,3},{4... | collective-permute-start | bytes 786440 | tf_op jit(solution)/shard_map/ppermute | solution.py:279
  243.4 7.5 %collective-permute-start.17 = (bf16[64,2048]{1,0:T(8,128)(2,1)S(1)}, bf16[64,2048]{1,0:T(8,128)(2,1)S(1)}, u32[]{:S(2)}, u32[]{:S(2)}) collective-permute-start(bf16[64,2048]{1,0:T(8,128)(2,1)S(1)} %fusion.49), channel_id=1, source_target_pairs={{0,2},{2,4},{4,6},{6,8},{8,10},{10,12},{12,14},{14,0},{1,3},{3,5},... | collective-permute-start | bytes 786440 | tf_op jit(solution)/shard_map/ppermute | solution.py:23
  243.5 7.8 %collective-permute-start.18 = (bf16[64,2048]{1,0:T(8,128)(2,1)S(1)}, bf16[64,2048]{1,0:T(8,128)(2,1)}, u32[]{:S(2)}, u32[]{:S(2)}) collective-permute-start(bf16[64,2048]{1,0:T(8,128)(2,1)S(1)} %fusion.49), channel_id=1, source_target_pairs={{0,14},{2,0},{4,2},{6,4},{8,6},{10,8},{12,10},{14,12},{1,15},{3,1}... | collective-permute-start | bytes 786440 | tf_op jit(solution)/shard_map/ppermute | solution.py:23
  250.9 6.4 %collective-permute-start.19 = (bf16[64,2048]{1,0:T(8,128)(2,1)S(1)}, bf16[64,2048]{1,0:T(8,128)(2,1)S(1)}, u32[]{:S(2)}, u32[]{:S(2)}) collective-permute-start(bf16[64,2048]{1,0:T(8,128)(2,1)S(1)} %collective-permute-done.17), channel_id=1, source_target_pairs={{0,2},{2,4},{4,6},{6,8},{8,10},{10,12},{12,14},{14,0},{1,3},{3,5},... | collective-permute-start | bytes 786440 | tf_op jit(solution)/shard_map/ppermute | solution.py:23
  251.2 17.0 %collective-permute-start.20 = (bf16[64,2048]{1,0:T(8,128)(2,1)}, bf16[64,2048]{1,0:T(8,128)(2,1)}, u32[]{:S(2)}, u32[]{:S(2)}) collective-permute-start(bf16[64,2048]{1,0:T(8,128)(2,1)} %collective-permute-done.18), channel_id=1, source_target_pairs={{0,14},{2,0},{4,2},{6,4},{8,6},{10,8},{12,10},{14,12},{1,15},{3,1}... | collective-permute-start | bytes 786440 | tf_op jit(solution)/shard_map/ppermute | solution.py:23
  260.1 29.1 %all-to-all-start.4 = ((bf16[16,24,2048]{2,1,0:T(8,128)(2,1)}), bf16[16,24,2048]{2,1,0:T(8,128)(2,1)}, u32[]{:S(2)}, u32[]{:S(2)}) async-start(bf16[16,24,2048]{2,1,0:T(8,128)(2,1)} %bitcast.107), calls=%async_computation.4 | async-start | bytes 3145728 | tf_op jit(solution)/shard_map/all_to_all | solution.py:61
  265.5 9.1 %collective-permute-start.21 = (bf16[64,2048]{1,0:T(8,128)(2,1)}, bf16[64,2048]{1,0:T(8,128)(2,1)S(1)}, u32[]{:S(2)}, u32[]{:S(2)}) collective-permute-start(bf16[64,2048]{1,0:T(8,128)(2,1)} %copy-done.32), channel_id=1, source_target_pairs={{0,2},{2,4},{4,6},{6,8},{8,10},{10,12},{12,14},{14,0},{1,3},{3,5},... | collective-permute-start | bytes 786440 | tf_op jit(solution)/shard_map/ppermute | solution.py:23
  268.3 10.0 %collective-permute-start.22 = (bf16[64,2048]{1,0:T(8,128)(2,1)}, bf16[64,2048]{1,0:T(8,128)(2,1)S(1)}, u32[]{:S(2)}, u32[]{:S(2)}) collective-permute-start(bf16[64,2048]{1,0:T(8,128)(2,1)} %collective-permute-done.20), channel_id=1, source_target_pairs={{0,14},{2,0},{4,2},{6,4},{8,6},{10,8},{12,10},{14,12},{1,15},{3,1}... | collective-permute-start | bytes 786440 | tf_op jit(solution)/shard_map/ppermute | solution.py:23
  274.6 6.2 %collective-permute-start.23 = (bf16[32,2048]{1,0:T(8,128)(2,1)S(1)}, bf16[32,2048]{1,0:T(8,128)(2,1)S(1)}, u32[]{:S(2)}, u32[]{:S(2)}) collective-permute-start(bf16[32,2048]{1,0:T(8,128)(2,1)S(1)} %slice.243), channel_id=1, source_target_pairs={{0,2},{2,4},{4,6},{6,8},{8,10},{10,12},{12,14},{14,0},{1,3},{3,5},... | collective-permute-start | bytes 393224 | tf_op jit(solution)/shard_map/ppermute | solution.py:23
  278.3 6.4 %collective-permute-start.24 = (bf16[32,2048]{1,0:T(8,128)(2,1)S(1)}, bf16[32,2048]{1,0:T(8,128)(2,1)S(1)}, u32[]{:S(2)}, u32[]{:S(2)}) collective-permute-start(bf16[32,2048]{1,0:T(8,128)(2,1)S(1)} %slice.244), channel_id=1, source_target_pairs={{0,14},{2,0},{4,2},{6,4},{8,6},{10,8},{12,10},{14,12},{1,15},{3,1}... | collective-permute-start | bytes 393224 | tf_op jit(solution)/shard_map/ppermute | solution.py:23
  289.2 28.1 %all-to-all-start.5 = ((bf16[16,24,2048]{2,1,0:T(8,128)(2,1)}), bf16[16,24,2048]{2,1,0:T(8,128)(2,1)}, u32[]{:S(2)}, u32[]{:S(2)}) async-start(bf16[16,24,2048]{2,1,0:T(8,128)(2,1)} %bitcast.105), calls=%async_computation.5 | async-start | bytes 3145728 | tf_op jit(solution)/shard_map/all_to_all | solution.py:61
  329.1 28.1 %all-to-all-start.6 = ((bf16[16,24,2048]{2,1,0:T(8,128)(2,1)}), bf16[16,24,2048]{2,1,0:T(8,128)(2,1)}, u32[]{:S(2)}, u32[]{:S(2)}) async-start(bf16[16,24,2048]{2,1,0:T(8,128)(2,1)} %bitcast.108), calls=%async_computation.6 | async-start | bytes 3145728 | tf_op jit(solution)/shard_map/all_to_all | solution.py:61
  359.6 6.5 %collective-permute-start.25 = (bf16[32,2048]{1,0:T(8,128)(2,1)S(1)}, bf16[32,2048]{1,0:T(8,128)(2,1)S(1)}, u32[]{:S(2)}, u32[]{:S(2)}) collective-permute-start(bf16[32,2048]{1,0:T(8,128)(2,1)S(1)} %get-tuple-element.47), channel_id=1, source_target_pairs={{0,2},{2,4},{4,6},{6,8},{8,10},{10,12},{12,14},{14,0},{1,3},{3,5},... | collective-permute-start | bytes 393224 | tf_op jit(solution)/shard_map/ppermute | solution.py:23
  362.3 6.3 %collective-permute-start.29 = (bf16[32,2048]{1,0:T(8,128)(2,1)S(1)}, bf16[32,2048]{1,0:T(8,128)(2,1)}, u32[]{:S(2)}, u32[]{:S(2)}) collective-permute-start(bf16[32,2048]{1,0:T(8,128)(2,1)S(1)} %get-tuple-element.48), channel_id=1, source_target_pairs={{0,14},{2,0},{4,2},{6,4},{8,6},{10,8},{12,10},{14,12},{1,15},{3,1}... | collective-permute-start | bytes 393224 | tf_op jit(solution)/shard_map/ppermute | solution.py:23
  362.3 27.4 %all-to-all-start.7 = ((bf16[16,24,2048]{2,1,0:T(8,128)(2,1)}), bf16[16,24,2048]{2,1,0:T(8,128)(2,1)S(1)}, u32[]{:S(2)}, u32[]{:S(2)}) async-start(bf16[16,24,2048]{2,1,0:T(8,128)(2,1)} %bitcast.32), calls=%async_computation.7 | async-start | bytes 3145728 | tf_op jit(solution)/shard_map/all_to_all | solution.py:61
  366.0 23.7 %copy-start.20 = (bf16[16,256]{1,0:T(8,128)(2,1)S(1)}, bf16[16,256]{1,0:T(8,128)(2,1)}, u32[]{:S(2)}) copy-start(bf16[16,256]{1,0:T(8,128)(2,1)} %get-tuple-element.29) | copy-start | bytes 24580
  369.6 6.8 %collective-permute-start.26 = (bf16[64,2048]{1,0:T(8,128)(2,1)S(1)}, bf16[64,2048]{1,0:T(8,128)(2,1)S(1)}, u32[]{:S(2)}, u32[]{:S(2)}) collective-permute-start(bf16[64,2048]{1,0:T(8,128)(2,1)S(1)} %pad_maximum_fusion.15), channel_id=1, source_target_pairs={{0,2},{2,4},{4,6},{6,8},{8,10},{10,12},{12,14},{14,0},{1,3},{3,5},... | collective-permute-start | bytes 786440 | tf_op jit(solution)/shard_map/ppermute | solution.py:23
  371.1 20.2 %collective-permute-start.30 = (bf16[64,2048]{1,0:T(8,128)(2,1)}, bf16[64,2048]{1,0:T(8,128)(2,1)}, u32[]{:S(2)}, u32[]{:S(2)}) collective-permute-start(bf16[64,2048]{1,0:T(8,128)(2,1)} %pad_maximum_fusion.16), channel_id=1, source_target_pairs={{0,14},{2,0},{4,2},{6,4},{8,6},{10,8},{12,10},{14,12},{1,15},{3,1}... | collective-permute-start | bytes 786440 | tf_op jit(solution)/shard_map/ppermute | solution.py:23
  376.5 14.8 %collective-permute-start.27 = (bf16[64,2048]{1,0:T(8,128)(2,1)S(1)}, bf16[64,2048]{1,0:T(8,128)(2,1)}, u32[]{:S(2)}, u32[]{:S(2)}) collective-permute-start(bf16[64,2048]{1,0:T(8,128)(2,1)S(1)} %add_convert_fusion.3), channel_id=1, source_target_pairs={{0,2},{2,4},{4,6},{6,8},{8,10},{10,12},{12,14},{14,0},{1,3},{3,5},... | collective-permute-start | bytes 786440 | tf_op jit(solution)/shard_map/ppermute | solution.py:23
  391.2 19.2 %copy-start.5 = (bf16[64,2048]{1,0:T(8,128)(2,1)S(1)}, bf16[64,2048]{1,0:T(8,128)(2,1)}, u32[]{:S(2)}) copy-start(bf16[64,2048]{1,0:T(8,128)(2,1)} %copy-done.4) | copy-start | bytes 786436
  391.2 19.2 %copy-start.22 = (f32[64]{0:T(128)S(1)}, f32[64]{0:T(128)}, u32[]{:S(2)}) copy-start(f32[64]{0:T(128)} %get-tuple-element.27) | copy-start | bytes 772
  391.2 19.5 %copy-start.24 = (f32[64]{0:T(128)S(1)}, f32[64]{0:T(128)}, u32[]{:S(2)}) copy-start(f32[64]{0:T(128)} %copy-done.23) | copy-start | bytes 772
  391.2 19.5 %copy-start.29 = (f32[64]{0:T(128)S(1)}, f32[64]{0:T(128)}, u32[]{:S(2)}) copy-start(f32[64]{0:T(128)} %get-tuple-element.83) | copy-start | bytes 772
  392.5 9.4 %collective-permute-start.31 = (bf16[64,2048]{1,0:T(8,128)(2,1)S(1)}, bf16[64,2048]{1,0:T(8,128)(2,1)S(1)}, u32[]{:S(2)}, u32[]{:S(2)}) collective-permute-start(bf16[64,2048]{1,0:T(8,128)(2,1)S(1)} %get-tuple-element.44), channel_id=1, source_target_pairs={{0,14},{2,0},{4,2},{6,4},{8,6},{10,8},{12,10},{14,12},{1,15},{3,1}... | collective-permute-start | bytes 786440 | tf_op jit(solution)/shard_map/ppermute | solution.py:23
  392.6 9.4 %collective-permute-start.28 = (bf16[64,2048]{1,0:T(8,128)(2,1)S(1)}, bf16[64,2048]{1,0:T(8,128)(2,1)S(1)}, u32[]{:S(2)}, u32[]{:S(2)}) collective-permute-start(bf16[64,2048]{1,0:T(8,128)(2,1)S(1)} %get-tuple-element.43), channel_id=1, source_target_pairs={{0,2},{2,4},{4,6},{6,8},{8,10},{10,12},{12,14},{14,0},{1,3},{3,5},... | collective-permute-start | bytes 786440 | tf_op jit(solution)/shard_map/ppermute | solution.py:23
  401.9 8.5 %collective-permute-start.32 = (bf16[64,2048]{1,0:T(8,128)(2,1)S(1)}, bf16[64,2048]{1,0:T(8,128)(2,1)S(1)}, u32[]{:S(2)}, u32[]{:S(2)}) collective-permute-start(bf16[64,2048]{1,0:T(8,128)(2,1)S(1)} %add_convert_fusion), channel_id=1, source_target_pairs={{0,14},{2,0},{4,2},{6,4},{8,6},{10,8},{12,10},{14,12},{1,15},{3,1}... | collective-permute-start | bytes 786440 | tf_op jit(solution)/shard_map/ppermute | solution.py:23
  (12 other events, 44.0 us)
where the time goes:
time: 420 us; the launch traced here: 412 us
  waiting for transfers between devices  218 us (52%)
  starting transfers between devices  92.9 us (22%)
  Pallas kernels  40.4 us (10%)
  other arithmetic  22.7 us (5%)
  matrix products  22.3 us (5%)
  local copies, waits for them, and re-layouts  14.7 us (4%)
    all_to_all x8, waiting for transfers between devices, exchange(): lax.all_to_all(parts, PLANE, split_axis=0, concat_axis=0, tiled=True)  123 us
    ppermute x32, waiting for transfers between devices, step_ring(): lax.ppermute(block, RING, [(i, (i + step) % count) for i in range(count)])  90.8 us
    ppermute x32, starting transfers between devices, step_ring(): lax.ppermute(block, RING, [(i, (i + step) % count) for i in range(count)])  50.8 us
    pallas_call x4, Pallas kernels, apply_expert(): pl.pallas_call(functools.partial(expert_kernel, first_at, second_at, forw...  40.4 us
    all_to_all x8, starting transfers between devices, exchange(): lax.all_to_all(parts, PLANE, split_axis=0, concat_axis=0, tiled=True)  38.3 us
    dot_general x6, matrix products, pick(): jnp.dot(picking, tokens, preferred_element_type=jnp.float32)  11.5 us
  transfers between devices with their start and end apart: 41, of which 28 were waited for; matrix products, arithmetic and copies ran while one was open for 10% of the time, Pallas kernels for 5%

commit v1 on v0

--- a/solution.py
+++ b/solution.py
@@ -14,6 +14,7 @@
 
 CHUNKS = ((0, -1, 1, -2), (2, -3, 3, 4))
 CAPACITY = 6
+TOKENS = 64
 
 epsilon = 1e-06
 
@@ -62,27 +63,78 @@
     return moved.reshape(rows.shape)
 
 
-def slots(ids, codes):
+def one_hots(ids, codes, first_chip, ring, peers):
     width = ids.shape[1]
-    tokens = 64
-    blocks = width // tokens
-    peers = lax.axis_size(PLANE)
-    plane = lax.broadcasted_iota(jnp.int32, (peers, 1, 1), 0)
-    named = ((plane // 2) * lax.axis_size(RING) + lax.axis_index(RING)) * 2 + plane % 2
-    hit = ids[None] == named.astype(jnp.float32)
-    member = jnp.sum(hit.astype(jnp.float32), axis=1)
-    code = jnp.sum(jnp.where(hit, codes[None], 0.0), axis=1)
+    blocks = width // TOKENS
+    plane = lax.broadcasted_iota(jnp.int32, (peers, 1), 0)
+    named = ((((plane >> 1) * ring + first_chip) << 1) + (plane & 1)).astype(jnp.float32)
+    member = jnp.zeros((peers, width), jnp.float32)
+    code = jnp.zeros((peers, width), jnp.float32)
+    for k in range(ids.shape[0]):
+        hit = ids[k : k + 1, :] == named
+        member = jnp.where(hit, 1.0, member)
+        code = jnp.where(hit, codes[k : k + 1, :], code)
     row = lax.broadcasted_iota(jnp.int32, (width, width), 0)
     column = lax.broadcasted_iota(jnp.int32, (width, width), 1)
-    earlier = ((row // tokens == column // tokens) & (row < column)).astype(jnp.bfloat16)
-    rank = jnp.dot(member.astype(jnp.bfloat16), earlier, preferred_element_type=jnp.float32)
-    block = lax.broadcasted_iota(jnp.int32, (1, width), 1) // tokens
+    earlier = jnp.where((row // TOKENS == column // TOKENS) & (row < column), 1.0, 0.0)
+    rank = jnp.dot(
+        member.astype(jnp.bfloat16),
+        earlier.astype(jnp.bfloat16),
+        preferred_element_type=jnp.float32,
+    )
+    block = lax.broadcasted_iota(jnp.int32, (1, width), 1) // TOKENS
     key = jnp.where(member > 0.0, (block * CAPACITY).astype(jnp.float32) + rank, -1.0)
-    place = lax.broadcasted_iota(jnp.int32, (1, blocks * CAPACITY, 1), 1).astype(jnp.float32)
-    found = key[:, None, :] == place
-    picking = found.astype(jnp.bfloat16)
-    weighing = jnp.where(found, code[:, None, :], 0.0).astype(jnp.bfloat16)
+    rows = blocks * CAPACITY
+    place = lax.broadcasted_iota(jnp.int32, (peers, rows, width), 1).astype(jnp.float32)
+    found = jnp.broadcast_to(key[:, None, :], (peers, rows, width)) == place
+    picking = jnp.where(found, 1.0, 0.0)
+    weighing = jnp.where(found, jnp.broadcast_to(code[:, None, :], (peers, rows, width)), 0.0)
     return (picking.reshape(-1, width), weighing.reshape(-1, width))
+
+
+def pick_kernel(top, ring, peers, told, *refs):
+    count = len(refs) - 5
+    blocks, (picked, next_out, by_now_out, by_next_out, held) = refs[:count], refs[count:]
+    width = picked.shape[1] // 2
+    for i, block in enumerate(blocks):
+        held[i * TOKENS : (i + 1) * TOKENS, :] = block[...]
+    info = jnp.transpose(held[:, 2 * width :].astype(jnp.float32))
+    ids_now, codes_now, ids_next, codes_next = (info[i * top : (i + 1) * top, :] for i in range(4))
+    pick_now, by_now = one_hots(ids_now, codes_now, told[0], ring, peers)
+    pick_next, by_next = one_hots(ids_next, codes_next, told[0], ring, peers)
+    early = jnp.where(told[1] == 1, pick_next, pick_now).astype(jnp.bfloat16)
+    pick_now = pick_now.astype(jnp.bfloat16)
+    picked[:, :width] = jnp.dot(
+        pick_now, held[:, :width], preferred_element_type=jnp.float32
+    ).astype(jnp.bfloat16)
+    picked[:, width:] = jnp.dot(
+        early, held[:, width : 2 * width], preferred_element_type=jnp.float32
+    ).astype(jnp.bfloat16)
+    next_out[...] = pick_next.astype(jnp.bfloat16)
+    by_now_out[...] = by_now.astype(jnp.bfloat16)
+    by_next_out[...] = by_next.astype(jnp.bfloat16)
+
+
+def pick_both(told, blocks, top, width):
+    ring, peers = lax.axis_size(RING), lax.axis_size(PLANE)
+    tokens = len(blocks) * TOKENS
+    rows = peers * len(blocks) * CAPACITY
+    whole = pl.BlockSpec(memory_space=pltpu.VMEM)
+    kept = pltpu.HBM((rows, tokens), jnp.bfloat16)
+    blocks = [pltpu.with_memory_space_constraint(block, pltpu.HBM) for block in blocks]
+    return pl.pallas_call(
+        functools.partial(pick_kernel, top, ring, peers),
+        in_specs=[pl.BlockSpec(memory_space=pltpu.SMEM)] + [whole] * len(blocks),
+        out_specs=[whole] * 4,
+        out_shape=[pltpu.HBM((rows, 2 * width), jnp.bfloat16), kept, kept, kept],
+        scratch_shapes=[pltpu.VMEM((tokens, blocks[0].shape[1]), jnp.bfloat16)],
+        cost_estimate=pl.CostEstimate(
+            flops=4 * rows * tokens * width,
+            bytes_accessed=4 * width * (tokens + rows) + 6 * rows * tokens,
+            transcendentals=0,
+        ),
+        compiler_params=pltpu.CompilerParams(vmem_limit_bytes=32 * 1024 * 1024),
+    )(told, *blocks)
 
 
 def pick(picking, tokens):
@@ -246,23 +298,15 @@
     early_rows = jnp.where(first_segment, stored_normed, edge_rows)
 
     forward_first = first_segment.astype(jnp.int32).reshape(1)
+    told = jnp.stack((lax.axis_index(RING), first_segment.astype(jnp.int32)))
 
     blocks = gather_near(jnp.concatenate((normed, early_rows, info), axis=1))
     pairs, place_next, weigh_now, weigh_next = [], [], [], []
     for chunk in CHUNKS:
         if pairs:
             blocks = gather_far(blocks)
-        tokens = stack(blocks, chunk)
-        told = jnp.transpose(tokens[:, 2 * width : 2 * width + 4 * top]).astype(jnp.float32)
-        pick_now, by_now = slots(told[:top], told[top : 2 * top])
-        pick_next, by_next = slots(told[2 * top : 3 * top], told[3 * top :])
-        pick_early = jnp.where(first_segment, pick_next, pick_now)
-        picked = jnp.concatenate(
-            (
-                pick(pick_now, tokens[:, :width]),
-                pick(pick_early, tokens[:, width : 2 * width]),
-            ),
-            axis=1,
+        picked, pick_next, by_now, by_next = pick_both(
+            told, [blocks[k] for k in chunk], top, width
         )
         if pairs:
             pairs[-1], picked = after(pairs[-1], picked)

time: 420 us -> 413 us (0.983)
  blocking collectives: 0 us -> 44.1 us
  waiting for transfers between devices: 218 us -> 188 us
  matrix products: 22.3 us -> 12.9 us
  Pallas kernels: 40.4 us -> 49.3 us
  starting transfers between devices: 92.9 us -> 84.5 us
  other arithmetic: 22.7 us -> 15.5 us
  local copies, waits for them, and re-layouts: 14.7 us -> 8.92 us
    all_to_all x0 -> x1, blocking collectives: none -> 44.1 us  [exchange(): lax.all_to_all(parts, PLANE, split_axis=0, concat_axis=0, tiled=True)]
    all_to_all x8 -> x7, waiting for transfers between devices: 123 us -> 80.8 us  [exchange(): lax.all_to_all(parts, PLANE, split_axis=0, concat_axis=0, tiled=True)]
    ppermute x32, waiting for transfers between devices: 90.8 us -> 103 us  [step_ring(): lax.ppermute(block, RING, [(i, (i + step) % count) for i in range(count)])]
    pallas_call x0 -> x2, Pallas kernels: none -> 9 us  [pick_both(): pl.pallas_call(functools.partial(pick_kernel, top, ring, peers), in_specs...]
    dot_general x6 -> x2, matrix products: 11.5 us -> 4.64 us  [pick(): jnp.dot(picking, tokens, preferred_element_type=jnp.float32)]
    all_to_all x8 -> x7, starting transfers between devices: 38.3 us -> 32.8 us  [exchange(): lax.all_to_all(parts, PLANE, split_axis=0, concat_axis=0, tiled=True)]
  transfers between devices with their start and end apart: 41 -> 40, of which waited for: 28 -> 26; matrix products, arithmetic and copies ran while one was open for 10% -> 4% of each run, Pallas kernels for 5% -> 7%
where the time goes in v1:
time: 413 us; the launch traced here: 405 us
  waiting for transfers between devices  188 us (46%)
  starting transfers between devices  84.5 us (20%)
  Pallas kernels  49.3 us (12%)
  blocking collectives  44.1 us (11%)
  other arithmetic  15.5 us (4%)
  matrix products  12.9 us (3%)
  local copies, waits for them, and re-layouts  8.92 us (2%)
    ppermute x32, waiting for transfers between devices, step_ring(): lax.ppermute(block, RING, [(i, (i + step) % count) for i in range(count)])  103 us
    all_to_all x7, waiting for transfers between devices, exchange(): lax.all_to_all(parts, PLANE, split_axis=0, concat_axis=0, tiled=True)  80.8 us
    ppermute x32, starting transfers between devices, step_ring(): lax.ppermute(block, RING, [(i, (i + step) % count) for i in range(count)])  47.9 us
    all_to_all x1, blocking collectives, exchange(): lax.all_to_all(parts, PLANE, split_axis=0, concat_axis=0, tiled=True)  44.1 us
    pallas_call x4, Pallas kernels, apply_expert(): pl.pallas_call(functools.partial(expert_kernel, first_at, second_at, forw...  40.3 us
    all_to_all x7, starting transfers between devices, exchange(): lax.all_to_all(parts, PLANE, split_axis=0, concat_axis=0, tiled=True)  32.8 us
    pallas_call x2, Pallas kernels, pick_both(): pl.pallas_call(functools.partial(pick_kernel, top, ring, peers), in_specs...  9 us
    dot_general x4, matrix products, combine(): lax.dot_general(weighing, rows, (((0,), (0,)), ((), ())), preferred_eleme...  8.28 us
  transfers between devices with their start and end apart: 40, of which 26 were waited for; matrix products, arithmetic and copies ran while one was open for 4% of the time, Pallas kernels for 7%

profile of v1, /device:TPU:96, one launch (start us, length us, event | category | flops | bytes accessed | tf_op | source)
XLA Modules:
  0.0 404.9 jit_solution(15703930509748760778)
XLA Ops:
  1.8 1.3 fusion.10
  5.2 3.2 collective-permute-start
  8.4 11.5 %collective-permute-done.refs_1_ = bf16[64,4224]{1,0:T(8,128)(2,1)S(1)} collective-permute-done((bf16[64,4224]{1,0:T(8,128)(2,1)S(1)}, bf16[64,4224]{1,0:T(8,128)(2,1)S(1)}, u32[]{:S(2)}, u32[]{:S(2)}) %collective-permute-start) | collective-permute-done | bytes 540704 | tf_op jit(solution)/shard_map/ppermute | solution.py:24
  20.0 3.7 collective-permute-start.2
  23.7 10.6 %collective-permute-done.2.refs_3_ = bf16[64,4224]{1,0:T(8,128)(2,1)S(1)} collective-permute-done((bf16[64,4224]{1,0:T(8,128)(2,1)S(1)}, bf16[64,4224]{1,0:T(8,128)(2,1)S(1)}, u32[]{:S(2)}, u32[]{:S(2)}) %collective-permute-start.2) | collective-permute-done | bytes 540704 | tf_op jit(solution)/shard_map/ppermute | solution.py:24
  35.1 4.5 %shard_map.82 = (bf16[384,4096]{1,0:T(8,128)(2,1)}, bf16[384,256]{1,0:T(8,128)(2,1)}, bf16[384,256]{1,0:T(8,128)(2,1)}, bf16[384,256]{1,0:T(8,128)(2,1)}) custom-call(s32[2]{0:T(128)S(1)} %pad_add_fusion.told, bf16[64,4224]{1,0:T(8,128)(2,1)} %copy-done.9, bf16[64,4224]{1,0:T(8,128)(2,1)} %copy-done.24, bf16[64,4224]{1,0:T(8,128)(2,1)} %collective-permute-done.1.refs_2_, ...), custom_call_target="tpu_custom_call" | custom-call | flops 805306368 | bytes 5832704 | tf_op jit(solution)/shard_map/pallas_call | solution.py:125
  40.4 7.0 %all-to-all-start = ((bf16[16,24,4096]{2,1,0:T(8,128)(2,1)}), bf16[16,24,4096]{2,1,0:T(8,128)(2,1)S(1)}, u32[]{:S(2)}, u32[]{:S(2)}) async-start(bf16[16,24,4096]{2,1,0:T(8,128)(2,1)} %bitcast.70), calls=%async_computation | async-start | bytes 6291456 | tf_op jit(solution)/shard_map/all_to_all | solution.py:62
  47.5 3.8 collective-permute-start.4
  51.3 12.9 %collective-permute-done.5.refs_2_ = bf16[64,4224]{1,0:T(8,128)(2,1)S(1)} collective-permute-done((bf16[64,4224]{1,0:T(8,128)(2,1)}, bf16[64,4224]{1,0:T(8,128)(2,1)S(1)}, u32[]{:S(2)}, u32[]{:S(2)}) %collective-permute-start.5) | collective-permute-done | bytes 540704 | tf_op jit(solution)/shard_map/ppermute | solution.py:24
  64.4 3.3 collective-permute-start.6
  67.6 6.1 %collective-permute-done.7 = bf16[32,4224]{1,0:T(8,128)(2,1)S(1)} collective-permute-done((bf16[32,4224]{1,0:T(8,128)(2,1)S(1)}, bf16[32,4224]{1,0:T(8,128)(2,1)S(1)}, u32[]{:S(2)}, u32[]{:S(2)}) %collective-permute-start.7) | collective-permute-done | bytes 270368 | tf_op jit(solution)/shard_map/ppermute | solution.py:24
  74.6 4.5 %shard_map.83 = (bf16[384,4096]{1,0:T(8,128)(2,1)}, bf16[384,256]{1,0:T(8,128)(2,1)}, bf16[384,256]{1,0:T(8,128)(2,1)}, bf16[384,256]{1,0:T(8,128)(2,1)}) custom-call(s32[2]{0:T(128)S(1)} %pad_add_fusion.told, bf16[64,4224]{1,0:T(8,128)(2,1)} %copy-done.22, bf16[64,4224]{1,0:T(8,128)(2,1)} %copy-done.18, bf16[64,4224]{1,0:T(8,128)(2,1)} %copy-done.17, ...), custom_call_target="tpu_custom_call" | custom-call | flops 805306368 | bytes 5832704 | tf_op jit(solution)/shard_map/pallas_call | solution.py:125
  79.2 8.9 %all-to-all-done = bf16[16,24,4096]{2,1,0:T(8,128)(2,1)S(1)} async-done(((bf16[16,24,4096]{2,1,0:T(8,128)(2,1)}), bf16[16,24,4096]{2,1,0:T(8,128)(2,1)S(1)}, u32[]{:S(2)}, u32[]{:S(2)}) %all-to-all-start) | async-done | bytes 3145760 | tf_op jit(solution)/shard_map/all_to_all | solution.py:62
  88.0 44.1 %all_to_all.40 = bf16[16,24,4096]{2,1,0:T(8,128)(2,1)S(1)} all-to-all(bf16[16,24,4096]{2,1,0:T(8,128)(2,1)} %bitcast.71), channel_id=1, replica_groups=mesh['segment'=2,'expert_0'=4,'expert_1'=2,'expert_2'=8,'expert_3'=2] {'..., dimensions={0} | all-to-all | bytes 6291456 | tf_op jit(solution)/shard_map/all_to_all | solution.py:62
  132.2 9.1 %shard_map.84 = bf16[384,2048]{1,0:T(8,128)(2,1)} custom-call(s32[1]{0:T(128)} %bitcast.3.flag, bf16[384,4096]{1,0:T(8,128)(2,1)S(1)} %bitcast.65, bf16[384,4096]{1,0:T(8,128)(2,1)S(1)} %bitcast.66, bf16[2048,768]{1,0:T(8,128)(2,1)} %bitcast.84, bf16[2048,768]{1,0:T(8,128)(2,1)} %bitcast.88, bf16[768,2048]{1,0:T(8,128)(2,1)} %bitcast.92), custom_call_target="tpu_custom_call" | custom-call | flops 6039797760 | bytes 14155776 | tf_op jit(solution)/shard_map/pallas_call | solution.py:230
  141.3 4.4 %all-to-all-start.2 = ((bf16[16,24,2048]{2,1,0:T(8,128)(2,1)}), bf16[16,24,2048]{2,1,0:T(8,128)(2,1)}, u32[]{:S(2)}, u32[]{:S(2)}) async-start(bf16[16,24,2048]{2,1,0:T(8,128)(2,1)} %bitcast.76), calls=%async_computation.2 | async-start | bytes 3145728 | tf_op jit(solution)/shard_map/all_to_all | solution.py:62
  145.7 8.2 %shard_map.85 = bf16[384,2048]{1,0:T(8,128)(2,1)} custom-call(s32[1]{0:T(128)} %bitcast.3.flag, bf16[384,4096]{1,0:T(8,128)(2,1)S(1)} %bitcast.62, bf16[384,4096]{1,0:T(8,128)(2,1)S(1)} %bitcast.63, bf16[2048,768]{1,0:T(8,128)(2,1)} %bitcast.85, bf16[2048,768]{1,0:T(8,128)(2,1)} %bitcast.89, bf16[768,2048]{1,0:T(8,128)(2,1)} %bitcast.93), custom_call_target="tpu_custom_call" | custom-call | flops 6039797760 | bytes 14155776 | tf_op jit(solution)/shard_map/pallas_call | solution.py:230
  153.9 15.5 %all-to-all-done.2 = bf16[16,24,2048]{2,1,0:T(8,128)(2,1)} async-done(((bf16[16,24,2048]{2,1,0:T(8,128)(2,1)}), bf16[16,24,2048]{2,1,0:T(8,128)(2,1)}, u32[]{:S(2)}, u32[]{:S(2)}) %all-to-all-start.2) | async-done | bytes 1572896 | tf_op jit(solution)/shard_map/all_to_all | solution.py:62
  169.4 2.1 convolution_convert_fusion.4
  173.3 3.7 collective-permute-start.8
  177.0 4.4 %all-to-all-start.3 = ((bf16[16,24,2048]{2,1,0:T(8,128)(2,1)}), bf16[16,24,2048]{2,1,0:T(8,128)(2,1)}, u32[]{:S(2)}, u32[]{:S(2)}) async-start(bf16[16,24,2048]{2,1,0:T(8,128)(2,1)} %bitcast.73), calls=%async_computation.3 | async-start | bytes 3145728 | tf_op jit(solution)/shard_map/all_to_all | solution.py:62
  185.4 2.1 collective-permute-start.9
  188.3 5.2 %collective-permute-done.9 = bf16[64,2048]{1,0:T(8,128)(2,1)S(1)} collective-permute-done((bf16[64,2048]{1,0:T(8,128)(2,1)S(1)}, bf16[64,2048]{1,0:T(8,128)(2,1)S(1)}, u32[]{:S(2)}, u32[]{:S(2)}) %collective-permute-start.9) | collective-permute-done | bytes 262176 | tf_op jit(solution)/shard_map/ppermute | solution.py:24
  194.5 3.8 collective-permute-start.10
  198.3 6.9 %all-to-all-done.3 = bf16[16,24,2048]{2,1,0:T(8,128)(2,1)} async-done(((bf16[16,24,2048]{2,1,0:T(8,128)(2,1)}), bf16[16,24,2048]{2,1,0:T(8,128)(2,1)}, u32[]{:S(2)}, u32[]{:S(2)}) %all-to-all-start.3) | async-done | bytes 1572896 | tf_op jit(solution)/shard_map/all_to_all | solution.py:62
  205.2 2.2 convolution_convert_fusion.5
  207.5 1.2 add_convert_fusion.6
  208.8 3.5 collective-permute-start.11
  212.3 5.8 %collective-permute-done.14 = bf16[64,2048]{1,0:T(8,128)(2,1)S(1)} collective-permute-done((bf16[64,2048]{1,0:T(8,128)(2,1)S(1)}, bf16[64,2048]{1,0:T(8,128)(2,1)S(1)}, u32[]{:S(2)}, u32[]{:S(2)}) %collective-permute-start.14) | collective-permute-done | bytes 262176 | tf_op jit(solution)/shard_map/ppermute | solution.py:24
  218.4 8.3 %collective-permute-done.15 = bf16[64,2048]{1,0:T(8,128)(2,1)S(1)} collective-permute-done((bf16[64,2048]{1,0:T(8,128)(2,1)S(1)}, bf16[64,2048]{1,0:T(8,128)(2,1)S(1)}, u32[]{:S(2)}, u32[]{:S(2)}) %collective-permute-start.15) | collective-permute-done | bytes 262176 | tf_op jit(solution)/shard_map/ppermute | solution.py:24
  227.4 3.8 collective-permute-start.16
  231.1 4.5 %collective-permute-done.16 = bf16[64,2048]{1,0:T(8,128)(2,1)S(1)} collective-permute-done((bf16[64,2048]{1,0:T(8,128)(2,1)S(1)}, bf16[64,2048]{1,0:T(8,128)(2,1)S(1)}, u32[]{:S(2)}, u32[]{:S(2)}) %collective-permute-start.16) | collective-permute-done | bytes 262176 | tf_op jit(solution)/shard_map/ppermute | solution.py:323
  236.7 2.0 collective-permute-start.18
  238.7 5.4 %collective-permute-done.17 = bf16[64,2048]{1,0:T(8,128)(2,1)S(1)} collective-permute-done((bf16[64,2048]{1,0:T(8,128)(2,1)S(1)}, bf16[64,2048]{1,0:T(8,128)(2,1)S(1)}, u32[]{:S(2)}, u32[]{:S(2)}) %collective-permute-start.17) | collective-permute-done | bytes 262176 | tf_op jit(solution)/shard_map/ppermute | solution.py:24
  244.4 1.7 collective-permute-start.20
  246.1 4.3 %collective-permute-done.19 = bf16[64,2048]{1,0:T(8,128)(2,1)S(1)} collective-permute-done((bf16[64,2048]{1,0:T(8,128)(2,1)S(1)}, bf16[64,2048]{1,0:T(8,128)(2,1)S(1)}, u32[]{:S(2)}, u32[]{:S(2)}) %collective-permute-start.19) | collective-permute-done | bytes 262176 | tf_op jit(solution)/shard_map/ppermute | solution.py:24
  250.5 2.8 convolution_convert_fusion.1
  253.3 4.4 %all-to-all-start.4 = ((bf16[16,24,2048]{2,1,0:T(8,128)(2,1)}), bf16[16,24,2048]{2,1,0:T(8,128)(2,1)}, u32[]{:S(2)}, u32[]{:S(2)}) async-start(bf16[16,24,2048]{2,1,0:T(8,128)(2,1)} %bitcast.74), calls=%async_computation.4 | async-start | bytes 3145728 | tf_op jit(solution)/shard_map/all_to_all | solution.py:62
  257.7 1.7 collective-permute-start.21
  260.8 5.6 %collective-permute-done.21 = bf16[64,2048]{1,0:T(8,128)(2,1)S(1)} collective-permute-done((bf16[64,2048]{1,0:T(8,128)(2,1)}, bf16[64,2048]{1,0:T(8,128)(2,1)S(1)}, u32[]{:S(2)}, u32[]{:S(2)}) %collective-permute-start.21) | collective-permute-done | bytes 262176 | tf_op jit(solution)/shard_map/ppermute | solution.py:24
  266.4 3.0 collective-permute-start.23
  269.6 2.4 collective-permute-done.23
  272.0 3.7 collective-permute-done.24
  275.7 1.8 convolution_convert_fusion
  277.6 3.8 all-to-all-done.4
  281.4 4.4 %all-to-all-start.5 = ((bf16[16,24,2048]{2,1,0:T(8,128)(2,1)}), bf16[16,24,2048]{2,1,0:T(8,128)(2,1)}, u32[]{:S(2)}, u32[]{:S(2)}) async-start(bf16[16,24,2048]{2,1,0:T(8,128)(2,1)} %bitcast.69), calls=%async_computation.5 | async-start | bytes 3145728 | tf_op jit(solution)/shard_map/all_to_all | solution.py:62
  285.8 23.7 %all-to-all-done.5 = bf16[16,24,2048]{2,1,0:T(8,128)(2,1)} async-done(((bf16[16,24,2048]{2,1,0:T(8,128)(2,1)}), bf16[16,24,2048]{2,1,0:T(8,128)(2,1)}, u32[]{:S(2)}, u32[]{:S(2)}) %all-to-all-start.5) | async-done | bytes 1572896 | tf_op jit(solution)/shard_map/all_to_all | solution.py:62
  309.5 1.9 copy-done.1
  311.4 11.6 %shard_map.86 = bf16[384,2048]{1,0:T(8,128)(2,1)} custom-call(s32[1]{0:T(128)S(6)} %sub.11.flag, bf16[384,4096]{1,0:T(8,128)(2,1)S(1)} %bitcast.67, bf16[384,2048]{1,0:T(8,128)(2,1)} %bitcast.23.second, bf16[2048,768]{1,0:T(8,128)(2,1)} %bitcast.86, bf16[2048,768]{1,0:T(8,128)(2,1)} %bitcast.90, bf16[768,2048]{1,0:T(8,128)(2,1)} %bitcast.94), custom_call_target="tpu_custom_call" | custom-call | flops 6039797760 | bytes 14155776 | tf_op jit(solution)/shard_map/pallas_call | solution.py:230
  323.0 4.4 %all-to-all-start.6 = ((bf16[16,24,2048]{2,1,0:T(8,128)(2,1)}), bf16[16,24,2048]{2,1,0:T(8,128)(2,1)}, u32[]{:S(2)}, u32[]{:S(2)}) async-start(bf16[16,24,2048]{2,1,0:T(8,128)(2,1)} %bitcast.75), calls=%async_computation.6 | async-start | bytes 3145728 | tf_op jit(solution)/shard_map/all_to_all | solution.py:62
  327.4 11.5 %shard_map.87 = bf16[384,2048]{1,0:T(8,128)(2,1)} custom-call(s32[1]{0:T(128)S(6)} %sub.11.flag, bf16[384,4096]{1,0:T(8,128)(2,1)S(1)} %bitcast.64, bf16[384,2048]{1,0:T(8,128)(2,1)} %bitcast.21.second, bf16[2048,768]{1,0:T(8,128)(2,1)} %bitcast.87, bf16[2048,768]{1,0:T(8,128)(2,1)} %bitcast.91, bf16[768,2048]{1,0:T(8,128)(2,1)} %bitcast.95), custom_call_target="tpu_custom_call" | custom-call | flops 6039797760 | bytes 14155776 | tf_op jit(solution)/shard_map/pallas_call | solution.py:230
  338.9 12.2 %all-to-all-done.6 = bf16[16,24,2048]{2,1,0:T(8,128)(2,1)} async-done(((bf16[16,24,2048]{2,1,0:T(8,128)(2,1)}), bf16[16,24,2048]{2,1,0:T(8,128)(2,1)}, u32[]{:S(2)}, u32[]{:S(2)}) %all-to-all-start.6) | async-done | bytes 1572896 | tf_op jit(solution)/shard_map/all_to_all | solution.py:62
  351.1 2.2 convolution_convert_fusion.2
  353.4 1.7 collective-permute-start.25
  355.5 3.7 all-to-all-start.7
  359.2 2.2 collective-permute-done.29
  363.9 1.3 collective-permute-start.30
  365.2 3.9 collective-permute-done.26
  369.2 3.8 collective-permute-start.27
  373.0 9.9 %all-to-all-done.7 = bf16[16,24,2048]{2,1,0:T(8,128)(2,1)S(1)} async-done(((bf16[16,24,2048]{2,1,0:T(8,128)(2,1)}), bf16[16,24,2048]{2,1,0:T(8,128)(2,1)S(1)}, u32[]{:S(2)}, u32[]{:S(2)}) %all-to-all-start.7) | async-done | bytes 1572896 | tf_op jit(solution)/shard_map/all_to_all | solution.py:62
  382.9 1.7 convolution_convert_fusion.3
  385.8 3.2 collective-permute-start.28
  389.0 5.8 %collective-permute-done.31 = bf16[64,2048]{1,0:T(8,128)(2,1)S(1)} collective-permute-done((bf16[64,2048]{1,0:T(8,128)(2,1)S(1)}, bf16[64,2048]{1,0:T(8,128)(2,1)S(1)}, u32[]{:S(2)}, u32[]{:S(2)}) %collective-permute-start.31) | collective-permute-done | bytes 262176 | tf_op jit(solution)/shard_map/ppermute | solution.py:24
  394.9 8.1 %collective-permute-done.32 = bf16[64,2048]{1,0:T(8,128)(2,1)S(1)} collective-permute-done((bf16[64,2048]{1,0:T(8,128)(2,1)S(1)}, bf16[64,2048]{1,0:T(8,128)(2,1)S(1)}, u32[]{:S(2)}, u32[]{:S(2)}) %collective-permute-start.32) | collective-permute-done | bytes 262176 | tf_op jit(solution)/shard_map/ppermute | solution.py:24
  (131 shorter events, 23.9 us)
Async XLA Ops:
  0.0 4.9 %copy-start.10 = (f32[1,2048]{1,0:T(1,128)S(1)}, f32[1,2048]{1,0:T(1,128)}, u32[]{:S(2)}) copy-start(f32[1,2048]{1,0:T(1,128)} %param.10) | copy-start | bytes 24580
  0.8 4.4 %copy-start.11 = (s32[1,1,64,8]{3,2,1,0:T(8,128)}, s32[1,1,64,8]{3,2,1,0:T(8,128)S(1)}, u32[]{:S(2)}) copy-start(s32[1,1,64,8]{3,2,1,0:T(8,128)S(1)} %copy.16) | copy-start | bytes 6148
  0.9 4.3 %copy-start.13 = (s32[1,1,64,8]{3,2,1,0:T(8,128)}, s32[1,1,64,8]{3,2,1,0:T(8,128)S(1)}, u32[]{:S(2)}) copy-start(s32[1,1,64,8]{3,2,1,0:T(8,128)S(1)} %copy.15) | copy-start | bytes 6148
  3.0 36.6 %copy-start.3 = (bf16[64,2048]{1,0:T(8,128)(2,1)}, bf16[64,2048]{1,0:T(8,128)(2,1)S(1)}, u32[]{:S(2)}) copy-start(bf16[64,2048]{1,0:T(8,128)(2,1)S(1)} %get-tuple-element.46) | copy-start | bytes 786436
  5.2 29.1 %copy-start.9 = (bf16[64,4224]{1,0:T(8,128)(2,1)}, bf16[64,4224]{1,0:T(8,128)(2,1)S(1)}, u32[]{:S(2)}) copy-start(bf16[64,4224]{1,0:T(8,128)(2,1)S(1)} %pad_maximum_fusion.refs_0_) | copy-start | bytes 1622020
  5.2 14.7 %collective-permute-start = (bf16[64,4224]{1,0:T(8,128)(2,1)S(1)}, bf16[64,4224]{1,0:T(8,128)(2,1)S(1)}, u32[]{:S(2)}, u32[]{:S(2)}) collective-permute-start(bf16[64,4224]{1,0:T(8,128)(2,1)S(1)} %pad_maximum_fusion.refs_0_), channel_id=1, source_target_pairs={{0,2},{2,4},{4,6},{6,8},{8,10},{10,12},{12,14},{14,0},{1,3},{3,5},... | collective-permute-start | bytes 1622024 | tf_op jit(solution)/shard_map/ppermute | solution.py:24
  8.4 15.2 %collective-permute-start.1 = (bf16[64,4224]{1,0:T(8,128)(2,1)S(1)}, bf16[64,4224]{1,0:T(8,128)(2,1)}, u32[]{:S(2)}, u32[]{:S(2)}) collective-permute-start(bf16[64,4224]{1,0:T(8,128)(2,1)S(1)} %pad_maximum_fusion.refs_0_), channel_id=1, source_target_pairs={{0,14},{2,0},{4,2},{6,4},{8,6},{10,8},{12,10},{14,12},{1,15},{3,1}... | collective-permute-start | bytes 1622024 | tf_op jit(solution)/shard_map/ppermute | solution.py:24
  20.0 14.4 %copy-start.24 = (bf16[64,4224]{1,0:T(8,128)(2,1)}, bf16[64,4224]{1,0:T(8,128)(2,1)S(1)}, u32[]{:S(2)}) copy-start(bf16[64,4224]{1,0:T(8,128)(2,1)S(1)} %collective-permute-done.refs_1_) | copy-start | bytes 1622020
  20.0 14.4 %collective-permute-start.2 = (bf16[64,4224]{1,0:T(8,128)(2,1)S(1)}, bf16[64,4224]{1,0:T(8,128)(2,1)S(1)}, u32[]{:S(2)}, u32[]{:S(2)}) collective-permute-start(bf16[64,4224]{1,0:T(8,128)(2,1)S(1)} %collective-permute-done.refs_1_), channel_id=1, source_target_pairs={{0,2},{2,4},{4,6},{6,8},{8,10},{10,12},{12,14},{14,0},{1,3},{3,5},... | collective-permute-start | bytes 1622024 | tf_op jit(solution)/shard_map/ppermute | solution.py:24
  23.7 16.0 %collective-permute-start.3 = (bf16[64,4224]{1,0:T(8,128)(2,1)}, bf16[64,4224]{1,0:T(8,128)(2,1)S(1)}, u32[]{:S(2)}, u32[]{:S(2)}) collective-permute-start(bf16[64,4224]{1,0:T(8,128)(2,1)} %collective-permute-done.1.refs_2_), channel_id=1, source_target_pairs={{0,14},{2,0},{4,2},{6,4},{8,6},{10,8},{12,10},{14,12},{1,15},{3,1}... | collective-permute-start | bytes 1622024 | tf_op jit(solution)/shard_map/ppermute | solution.py:24
  34.3 0.8 copy-start.23
  40.4 47.6 %all-to-all-start = ((bf16[16,24,4096]{2,1,0:T(8,128)(2,1)}), bf16[16,24,4096]{2,1,0:T(8,128)(2,1)S(1)}, u32[]{:S(2)}, u32[]{:S(2)}) async-start(bf16[16,24,4096]{2,1,0:T(8,128)(2,1)} %bitcast.70), calls=%async_computation | async-start | bytes 6291456 | tf_op jit(solution)/shard_map/all_to_all | solution.py:62
  47.4 16.8 %collective-permute-start.5 = (bf16[64,4224]{1,0:T(8,128)(2,1)}, bf16[64,4224]{1,0:T(8,128)(2,1)S(1)}, u32[]{:S(2)}, u32[]{:S(2)}) collective-permute-start(bf16[64,4224]{1,0:T(8,128)(2,1)} %copy-done.22), channel_id=1, source_target_pairs={{0,14},{2,0},{4,2},{6,4},{8,6},{10,8},{12,10},{14,12},{1,15},{3,1}... | collective-permute-start | bytes 1622024 | tf_op jit(solution)/shard_map/ppermute | solution.py:24
  47.5 16.8 %collective-permute-start.4 = (bf16[64,4224]{1,0:T(8,128)(2,1)}, bf16[64,4224]{1,0:T(8,128)(2,1)S(1)}, u32[]{:S(2)}, u32[]{:S(2)}) collective-permute-start(bf16[64,4224]{1,0:T(8,128)(2,1)} %copy-done.23), channel_id=1, source_target_pairs={{0,2},{2,4},{4,6},{6,8},{8,10},{10,12},{12,14},{14,0},{1,3},{3,5},... | collective-permute-start | bytes 1622024 | tf_op jit(solution)/shard_map/ppermute | solution.py:24
  64.2 10.4 %copy-start.17 = (bf16[64,4224]{1,0:T(8,128)(2,1)}, bf16[64,4224]{1,0:T(8,128)(2,1)S(1)}, u32[]{:S(2)}) copy-start(bf16[64,4224]{1,0:T(8,128)(2,1)S(1)} %collective-permute-done.5.refs_2_) | copy-start | bytes 1622020
  64.2 9.5 %collective-permute-start.7 = (bf16[32,4224]{1,0:T(8,128)(2,1)S(1)}, bf16[32,4224]{1,0:T(8,128)(2,1)S(1)}, u32[]{:S(2)}, u32[]{:S(2)}) collective-permute-start(bf16[32,4224]{1,0:T(8,128)(2,1)S(1)} %slice.165), channel_id=1, source_target_pairs={{0,14},{2,0},{4,2},{6,4},{8,6},{10,8},{12,10},{14,12},{1,15},{3,1}... | collective-permute-start | bytes 811016 | tf_op jit(solution)/shard_map/ppermute | solution.py:24
  64.3 10.3 %copy-start.18 = (bf16[64,4224]{1,0:T(8,128)(2,1)}, bf16[64,4224]{1,0:T(8,128)(2,1)S(1)}, u32[]{:S(2)}) copy-start(bf16[64,4224]{1,0:T(8,128)(2,1)S(1)} %collective-permute-done.4.refs_1_) | copy-start | bytes 1622020
  64.4 9.4 %collective-permute-start.6 = (bf16[32,4224]{1,0:T(8,128)(2,1)S(1)}, bf16[32,4224]{1,0:T(8,128)(2,1)S(1)}, u32[]{:S(2)}, u32[]{:S(2)}) collective-permute-start(bf16[32,4224]{1,0:T(8,128)(2,1)S(1)} %slice.164), channel_id=1, source_target_pairs={{0,2},{2,4},{4,6},{6,8},{8,10},{10,12},{12,14},{14,0},{1,3},{3,5},... | collective-permute-start | bytes 811016 | tf_op jit(solution)/shard_map/ppermute | solution.py:24
  132.2 9.1 %copy-start = (bf16[16,24,4096]{2,1,0:T(8,128)(2,1)}, bf16[16,24,4096]{2,1,0:T(8,128)(2,1)S(1)}, u32[]{:S(2)}) copy-start(bf16[16,24,4096]{2,1,0:T(8,128)(2,1)S(1)} %all_to_all.40) | copy-start | bytes 9437188
  141.3 28.1 %all-to-all-start.2 = ((bf16[16,24,2048]{2,1,0:T(8,128)(2,1)}), bf16[16,24,2048]{2,1,0:T(8,128)(2,1)}, u32[]{:S(2)}, u32[]{:S(2)}) async-start(bf16[16,24,2048]{2,1,0:T(8,128)(2,1)} %bitcast.76), calls=%async_computation.2 | async-start | bytes 3145728 | tf_op jit(solution)/shard_map/all_to_all | solution.py:62
  145.7 23.7 %copy-start.16 = (bf16[384,256]{1,0:T(8,128)(2,1)S(1)}, bf16[384,256]{1,0:T(8,128)(2,1)}, u32[]{:S(2)}) copy-start(bf16[384,256]{1,0:T(8,128)(2,1)} %get-tuple-element.33) | copy-start | bytes 589828
  171.6 1.0 copy-start.5
  173.3 8.1 %collective-permute-start.8 = (bf16[32,2048]{1,0:T(8,128)(2,1)}, bf16[32,2048]{1,0:T(8,128)(2,1)S(1)}, u32[]{:S(2)}, u32[]{:S(2)}) collective-permute-start(bf16[32,2048]{1,0:T(8,128)(2,1)} %get-tuple-element.59), channel_id=1, source_target_pairs={{0,2},{2,4},{4,6},{6,8},{8,10},{10,12},{12,14},{14,0},{1,3},{3,5},... | collective-permute-start | bytes 393224 | tf_op jit(solution)/shard_map/ppermute | solution.py:24
  177.0 6.3 %collective-permute-start.12 = (bf16[32,2048]{1,0:T(8,128)(2,1)S(1)}, bf16[32,2048]{1,0:T(8,128)(2,1)}, u32[]{:S(2)}, u32[]{:S(2)}) collective-permute-start(bf16[32,2048]{1,0:T(8,128)(2,1)S(1)} %get-tuple-element.60), channel_id=1, source_target_pairs={{0,14},{2,0},{4,2},{6,4},{8,6},{10,8},{12,10},{14,12},{1,15},{3,1}... | collective-permute-start | bytes 393224 | tf_op jit(solution)/shard_map/ppermute | solution.py:24
  177.0 28.1 %all-to-all-start.3 = ((bf16[16,24,2048]{2,1,0:T(8,128)(2,1)}), bf16[16,24,2048]{2,1,0:T(8,128)(2,1)}, u32[]{:S(2)}, u32[]{:S(2)}) async-start(bf16[16,24,2048]{2,1,0:T(8,128)(2,1)} %bitcast.73), calls=%async_computation.3 | async-start | bytes 3145728 | tf_op jit(solution)/shard_map/all_to_all | solution.py:62
  185.4 8.1 %collective-permute-start.9 = (bf16[64,2048]{1,0:T(8,128)(2,1)S(1)}, bf16[64,2048]{1,0:T(8,128)(2,1)S(1)}, u32[]{:S(2)}, u32[]{:S(2)}) collective-permute-start(bf16[64,2048]{1,0:T(8,128)(2,1)S(1)} %pad_maximum_fusion.2), channel_id=1, source_target_pairs={{0,2},{2,4},{4,6},{6,8},{8,10},{10,12},{12,14},{14,0},{1,3},{3,5},... | collective-permute-start | bytes 786440 | tf_op jit(solution)/shard_map/ppermute | solution.py:24
  188.3 19.2 %collective-permute-start.13 = (bf16[64,2048]{1,0:T(8,128)(2,1)}, bf16[64,2048]{1,0:T(8,128)(2,1)}, u32[]{:S(2)}, u32[]{:S(2)}) collective-permute-start(bf16[64,2048]{1,0:T(8,128)(2,1)} %pad_maximum_fusion.3), channel_id=1, source_target_pairs={{0,14},{2,0},{4,2},{6,4},{8,6},{10,8},{12,10},{14,12},{1,15},{3,1}... | collective-permute-start | bytes 786440 | tf_op jit(solution)/shard_map/ppermute | solution.py:24
  194.5 13.0 %collective-permute-start.10 = (bf16[64,2048]{1,0:T(8,128)(2,1)S(1)}, bf16[64,2048]{1,0:T(8,128)(2,1)}, u32[]{:S(2)}, u32[]{:S(2)}) collective-permute-start(bf16[64,2048]{1,0:T(8,128)(2,1)S(1)} %add_convert_fusion.7), channel_id=1, source_target_pairs={{0,2},{2,4},{4,6},{6,8},{8,10},{10,12},{12,14},{14,0},{1,3},{3,5},... | collective-permute-start | bytes 786440 | tf_op jit(solution)/shard_map/ppermute | solution.py:24
  207.4 10.8 %copy-start.12 = (s32[1,1,64,8]{3,2,1,0:T(8,128)S(1)}, s32[1,1,64,8]{3,2,1,0:T(8,128)}, u32[]{:S(2)}) copy-start(s32[1,1,64,8]{3,2,1,0:T(8,128)} %copy-done.11) | copy-start | bytes 6148
  207.4 10.8 %copy-start.14 = (s32[1,1,64,8]{3,2,1,0:T(8,128)S(1)}, s32[1,1,64,8]{3,2,1,0:T(8,128)}, u32[]{:S(2)}) copy-start(s32[1,1,64,8]{3,2,1,0:T(8,128)} %copy-done.13) | copy-start | bytes 6148
  207.4 19.2 %copy-start.4 = (bf16[64,2048]{1,0:T(8,128)(2,1)S(1)}, bf16[64,2048]{1,0:T(8,128)(2,1)}, u32[]{:S(2)}) copy-start(bf16[64,2048]{1,0:T(8,128)(2,1)} %copy-done.3) | copy-start | bytes 786436
  207.5 19.5 %copy-start.8 = (bf16[1,64,2048]{2,1,0:T(8,128)(2,1)S(1)}, bf16[1,64,2048]{2,1,0:T(8,128)(2,1)}, u32[]{:S(2)}) copy-start(bf16[1,64,2048]{2,1,0:T(8,128)(2,1)} %param.8) | copy-start | bytes 786436
  207.5 19.5 %copy-start.20 = (f32[64]{0:T(128)S(1)}, f32[64]{0:T(128)}, u32[]{:S(2)}) copy-start(f32[64]{0:T(128)} %get-tuple-element.74) | copy-start | bytes 772
  208.7 9.4 %collective-permute-start.14 = (bf16[64,2048]{1,0:T(8,128)(2,1)S(1)}, bf16[64,2048]{1,0:T(8,128)(2,1)S(1)}, u32[]{:S(2)}, u32[]{:S(2)}) collective-permute-start(bf16[64,2048]{1,0:T(8,128)(2,1)S(1)} %get-tuple-element.56), channel_id=1, source_target_pairs={{0,14},{2,0},{4,2},{6,4},{8,6},{10,8},{12,10},{14,12},{1,15},{3,1}... | collective-permute-start | bytes 786440 | tf_op jit(solution)/shard_map/ppermute | solution.py:24
  208.8 26.9 %copy-start.2 = (bf16[1,64,2048]{2,1,0:T(8,128)(2,1)S(1)}, bf16[1,64,2048]{2,1,0:T(8,128)(2,1)}, u32[]{:S(2)}) copy-start(bf16[1,64,2048]{2,1,0:T(8,128)(2,1)} %param.9) | copy-start | bytes 786436
  208.8 9.6 %collective-permute-start.11 = (bf16[64,2048]{1,0:T(8,128)(2,1)S(1)}, bf16[64,2048]{1,0:T(8,128)(2,1)S(1)}, u32[]{:S(2)}, u32[]{:S(2)}) collective-permute-start(bf16[64,2048]{1,0:T(8,128)(2,1)S(1)} %get-tuple-element.55), channel_id=1, source_target_pairs={{0,2},{2,4},{4,6},{6,8},{8,10},{10,12},{12,14},{14,0},{1,3},{3,5},... | collective-permute-start | bytes 786440 | tf_op jit(solution)/shard_map/ppermute | solution.py:24
  218.1 8.5 %collective-permute-start.15 = (bf16[64,2048]{1,0:T(8,128)(2,1)S(1)}, bf16[64,2048]{1,0:T(8,128)(2,1)S(1)}, u32[]{:S(2)}, u32[]{:S(2)}) collective-permute-start(bf16[64,2048]{1,0:T(8,128)(2,1)S(1)} %add_convert_fusion.4), channel_id=1, source_target_pairs={{0,14},{2,0},{4,2},{6,4},{8,6},{10,8},{12,10},{14,12},{1,15},{3,1}... | collective-permute-start | bytes 786440 | tf_op jit(solution)/shard_map/ppermute | solution.py:24
  226.9 23.5 %copy-start.26 = (bf16[384,256]{1,0:T(8,128)(2,1)S(1)}, bf16[384,256]{1,0:T(8,128)(2,1)}, u32[]{:S(2)}) copy-start(bf16[384,256]{1,0:T(8,128)(2,1)} %get-tuple-element.36) | copy-start | bytes 589828
  227.4 8.3 %collective-permute-start.16 = (bf16[64,2048]{1,0:T(8,128)(2,1)S(1)}, bf16[64,2048]{1,0:T(8,128)(2,1)S(1)}, u32[]{:S(2)}, u32[]{:S(2)}) collective-permute-start(bf16[64,2048]{1,0:T(8,128)(2,1)S(1)} %fusion.14), channel_id=1, source_target_pairs={{0,128},{128,0},{1,129},{129,1},{2,130},{130,2},{3,131},{131,3},{4... | collective-permute-start | bytes 786440 | tf_op jit(solution)/shard_map/ppermute | solution.py:323
  236.6 7.5 %collective-permute-start.17 = (bf16[64,2048]{1,0:T(8,128)(2,1)S(1)}, bf16[64,2048]{1,0:T(8,128)(2,1)S(1)}, u32[]{:S(2)}, u32[]{:S(2)}) collective-permute-start(bf16[64,2048]{1,0:T(8,128)(2,1)S(1)} %fusion.27), channel_id=1, source_target_pairs={{0,2},{2,4},{4,6},{6,8},{8,10},{10,12},{12,14},{14,0},{1,3},{3,5},... | collective-permute-start | bytes 786440 | tf_op jit(solution)/shard_map/ppermute | solution.py:24
  236.7 7.8 %collective-permute-start.18 = (bf16[64,2048]{1,0:T(8,128)(2,1)S(1)}, bf16[64,2048]{1,0:T(8,128)(2,1)}, u32[]{:S(2)}, u32[]{:S(2)}) collective-permute-start(bf16[64,2048]{1,0:T(8,128)(2,1)S(1)} %fusion.27), channel_id=1, source_target_pairs={{0,14},{2,0},{4,2},{6,4},{8,6},{10,8},{12,10},{14,12},{1,15},{3,1}... | collective-permute-start | bytes 786440 | tf_op jit(solution)/shard_map/ppermute | solution.py:24
  244.1 6.4 %collective-permute-start.19 = (bf16[64,2048]{1,0:T(8,128)(2,1)S(1)}, bf16[64,2048]{1,0:T(8,128)(2,1)S(1)}, u32[]{:S(2)}, u32[]{:S(2)}) collective-permute-start(bf16[64,2048]{1,0:T(8,128)(2,1)S(1)} %collective-permute-done.17), channel_id=1, source_target_pairs={{0,2},{2,4},{4,6},{6,8},{8,10},{10,12},{12,14},{14,0},{1,3},{3,5},... | collective-permute-start | bytes 786440 | tf_op jit(solution)/shard_map/ppermute | solution.py:24
  244.4 14.9 %collective-permute-start.20 = (bf16[64,2048]{1,0:T(8,128)(2,1)}, bf16[64,2048]{1,0:T(8,128)(2,1)}, u32[]{:S(2)}, u32[]{:S(2)}) collective-permute-start(bf16[64,2048]{1,0:T(8,128)(2,1)} %collective-permute-done.18), channel_id=1, source_target_pairs={{0,14},{2,0},{4,2},{6,4},{8,6},{10,8},{12,10},{14,12},{1,15},{3,1}... | collective-permute-start | bytes 786440 | tf_op jit(solution)/shard_map/ppermute | solution.py:24
  250.5 2.8 copy-start.25
  253.3 28.1 %all-to-all-start.4 = ((bf16[16,24,2048]{2,1,0:T(8,128)(2,1)}), bf16[16,24,2048]{2,1,0:T(8,128)(2,1)}, u32[]{:S(2)}, u32[]{:S(2)}) async-start(bf16[16,24,2048]{2,1,0:T(8,128)(2,1)} %bitcast.74), calls=%async_computation.4 | async-start | bytes 3145728 | tf_op jit(solution)/shard_map/all_to_all | solution.py:62
  257.7 18.0 %copy-start.15 = (bf16[384,256]{1,0:T(8,128)(2,1)S(1)}, bf16[384,256]{1,0:T(8,128)(2,1)}, u32[]{:S(2)}) copy-start(bf16[384,256]{1,0:T(8,128)(2,1)} %get-tuple-element.37) | copy-start | bytes 589828
  257.7 8.7 %collective-permute-start.21 = (bf16[64,2048]{1,0:T(8,128)(2,1)}, bf16[64,2048]{1,0:T(8,128)(2,1)S(1)}, u32[]{:S(2)}, u32[]{:S(2)}) collective-permute-start(bf16[64,2048]{1,0:T(8,128)(2,1)} %copy-done.25), channel_id=1, source_target_pairs={{0,2},{2,4},{4,6},{6,8},{8,10},{10,12},{12,14},{14,0},{1,3},{3,5},... | collective-permute-start | bytes 786440 | tf_op jit(solution)/shard_map/ppermute | solution.py:24
  259.4 10.1 %collective-permute-start.22 = (bf16[64,2048]{1,0:T(8,128)(2,1)}, bf16[64,2048]{1,0:T(8,128)(2,1)S(1)}, u32[]{:S(2)}, u32[]{:S(2)}) collective-permute-start(bf16[64,2048]{1,0:T(8,128)(2,1)} %collective-permute-done.20), channel_id=1, source_target_pairs={{0,14},{2,0},{4,2},{6,4},{8,6},{10,8},{12,10},{14,12},{1,15},{3,1}... | collective-permute-start | bytes 786440 | tf_op jit(solution)/shard_map/ppermute | solution.py:24
  266.4 5.6 %collective-permute-start.23 = (bf16[32,2048]{1,0:T(8,128)(2,1)S(1)}, bf16[32,2048]{1,0:T(8,128)(2,1)S(1)}, u32[]{:S(2)}, u32[]{:S(2)}) collective-permute-start(bf16[32,2048]{1,0:T(8,128)(2,1)S(1)} %slice.177), channel_id=1, source_target_pairs={{0,2},{2,4},{4,6},{6,8},{8,10},{10,12},{12,14},{14,0},{1,3},{3,5},... | collective-permute-start | bytes 393224 | tf_op jit(solution)/shard_map/ppermute | solution.py:24
  269.5 6.3 %collective-permute-start.24 = (bf16[32,2048]{1,0:T(8,128)(2,1)S(1)}, bf16[32,2048]{1,0:T(8,128)(2,1)S(1)}, u32[]{:S(2)}, u32[]{:S(2)}) collective-permute-start(bf16[32,2048]{1,0:T(8,128)(2,1)S(1)} %slice.178), channel_id=1, source_target_pairs={{0,14},{2,0},{4,2},{6,4},{8,6},{10,8},{12,10},{14,12},{1,15},{3,1}... | collective-permute-start | bytes 393224 | tf_op jit(solution)/shard_map/ppermute | solution.py:24
  281.4 28.1 %all-to-all-start.5 = ((bf16[16,24,2048]{2,1,0:T(8,128)(2,1)}), bf16[16,24,2048]{2,1,0:T(8,128)(2,1)}, u32[]{:S(2)}, u32[]{:S(2)}) async-start(bf16[16,24,2048]{2,1,0:T(8,128)(2,1)} %bitcast.69), calls=%async_computation.5 | async-start | bytes 3145728 | tf_op jit(solution)/shard_map/all_to_all | solution.py:62
  309.5 1.9 copy-start.1
  323.0 28.1 %all-to-all-start.6 = ((bf16[16,24,2048]{2,1,0:T(8,128)(2,1)}), bf16[16,24,2048]{2,1,0:T(8,128)(2,1)}, u32[]{:S(2)}, u32[]{:S(2)}) async-start(bf16[16,24,2048]{2,1,0:T(8,128)(2,1)} %bitcast.75), calls=%async_computation.6 | async-start | bytes 3145728 | tf_op jit(solution)/shard_map/all_to_all | solution.py:62
  353.4 5.8 %collective-permute-start.25 = (bf16[32,2048]{1,0:T(8,128)(2,1)S(1)}, bf16[32,2048]{1,0:T(8,128)(2,1)S(1)}, u32[]{:S(2)}, u32[]{:S(2)}) collective-permute-start(bf16[32,2048]{1,0:T(8,128)(2,1)S(1)} %get-tuple-element.51), channel_id=1, source_target_pairs={{0,2},{2,4},{4,6},{6,8},{8,10},{10,12},{12,14},{14,0},{1,3},{3,5},... | collective-permute-start | bytes 393224 | tf_op jit(solution)/shard_map/ppermute | solution.py:24
  355.1 6.3 %collective-permute-start.29 = (bf16[32,2048]{1,0:T(8,128)(2,1)S(1)}, bf16[32,2048]{1,0:T(8,128)(2,1)}, u32[]{:S(2)}, u32[]{:S(2)}) collective-permute-start(bf16[32,2048]{1,0:T(8,128)(2,1)S(1)} %get-tuple-element.52), channel_id=1, source_target_pairs={{0,14},{2,0},{4,2},{6,4},{8,6},{10,8},{12,10},{14,12},{1,15},{3,1}... | collective-permute-start | bytes 393224 | tf_op jit(solution)/shard_map/ppermute | solution.py:24
  355.5 27.4 %all-to-all-start.7 = ((bf16[16,24,2048]{2,1,0:T(8,128)(2,1)}), bf16[16,24,2048]{2,1,0:T(8,128)(2,1)S(1)}, u32[]{:S(2)}, u32[]{:S(2)}) async-start(bf16[16,24,2048]{2,1,0:T(8,128)(2,1)} %bitcast.72), calls=%async_computation.7 | async-start | bytes 3145728 | tf_op jit(solution)/shard_map/all_to_all | solution.py:62
  362.4 6.8 %collective-permute-start.26 = (bf16[64,2048]{1,0:T(8,128)(2,1)S(1)}, bf16[64,2048]{1,0:T(8,128)(2,1)S(1)}, u32[]{:S(2)}, u32[]{:S(2)}) collective-permute-start(bf16[64,2048]{1,0:T(8,128)(2,1)S(1)} %pad_maximum_fusion.4), channel_id=1, source_target_pairs={{0,2},{2,4},{4,6},{6,8},{8,10},{10,12},{12,14},{14,0},{1,3},{3,5},... | collective-permute-start | bytes 786440 | tf_op jit(solution)/shard_map/ppermute | solution.py:24
  363.9 20.7 %collective-permute-start.30 = (bf16[64,2048]{1,0:T(8,128)(2,1)}, bf16[64,2048]{1,0:T(8,128)(2,1)S(1)}, u32[]{:S(2)}, u32[]{:S(2)}) collective-permute-start(bf16[64,2048]{1,0:T(8,128)(2,1)} %pad_maximum_fusion.5), channel_id=1, source_target_pairs={{0,14},{2,0},{4,2},{6,4},{8,6},{10,8},{12,10},{14,12},{1,15},{3,1}... | collective-permute-start | bytes 786440 | tf_op jit(solution)/shard_map/ppermute | solution.py:24
  369.2 15.3 %collective-permute-start.27 = (bf16[64,2048]{1,0:T(8,128)(2,1)S(1)}, bf16[64,2048]{1,0:T(8,128)(2,1)}, u32[]{:S(2)}, u32[]{:S(2)}) collective-permute-start(bf16[64,2048]{1,0:T(8,128)(2,1)S(1)} %add_convert_fusion.3), channel_id=1, source_target_pairs={{0,2},{2,4},{4,6},{6,8},{8,10},{10,12},{12,14},{14,0},{1,3},{3,5},... | collective-permute-start | bytes 786440 | tf_op jit(solution)/shard_map/ppermute | solution.py:24
  384.5 18.5 %copy-start.7 = (bf16[64,2048]{1,0:T(8,128)(2,1)S(1)}, bf16[64,2048]{1,0:T(8,128)(2,1)}, u32[]{:S(2)}) copy-start(bf16[64,2048]{1,0:T(8,128)(2,1)} %copy-done.6) | copy-start | bytes 786436
  384.5 18.8 %copy-start.21 = (f32[64]{0:T(128)S(1)}, f32[64]{0:T(128)}, u32[]{:S(2)}) copy-start(f32[64]{0:T(128)} %get-tuple-element.72) | copy-start | bytes 772
  385.7 9.1 %collective-permute-start.31 = (bf16[64,2048]{1,0:T(8,128)(2,1)S(1)}, bf16[64,2048]{1,0:T(8,128)(2,1)S(1)}, u32[]{:S(2)}, u32[]{:S(2)}) collective-permute-start(bf16[64,2048]{1,0:T(8,128)(2,1)S(1)} %get-tuple-element.48), channel_id=1, source_target_pairs={{0,14},{2,0},{4,2},{6,4},{8,6},{10,8},{12,10},{14,12},{1,15},{3,1}... | collective-permute-start | bytes 786440 | tf_op jit(solution)/shard_map/ppermute | solution.py:24
  385.8 9.2 %collective-permute-start.28 = (bf16[64,2048]{1,0:T(8,128)(2,1)S(1)}, bf16[64,2048]{1,0:T(8,128)(2,1)S(1)}, u32[]{:S(2)}, u32[]{:S(2)}) collective-permute-start(bf16[64,2048]{1,0:T(8,128)(2,1)S(1)} %get-tuple-element.47), channel_id=1, source_target_pairs={{0,2},{2,4},{4,6},{6,8},{8,10},{10,12},{12,14},{14,0},{1,3},{3,5},... | collective-permute-start | bytes 786440 | tf_op jit(solution)/shard_map/ppermute | solution.py:24
  394.8 8.2 %collective-permute-start.32 = (bf16[64,2048]{1,0:T(8,128)(2,1)S(1)}, bf16[64,2048]{1,0:T(8,128)(2,1)S(1)}, u32[]{:S(2)}, u32[]{:S(2)}) collective-permute-start(bf16[64,2048]{1,0:T(8,128)(2,1)S(1)} %add_convert_fusion), channel_id=1, source_target_pairs={{0,14},{2,0},{4,2},{6,4},{8,6},{10,8},{12,10},{14,12},{1,15},{3,1}... | collective-permute-start | bytes 786440 | tf_op jit(solution)/shard_map/ppermute | solution.py:24
  (3 other events, 2.2 us)

commit v2 on v1

--- a/solution.py
+++ b/solution.py
@@ -44,9 +44,9 @@
 
 
 def sum_ring(parts):
-    half = parts[4].shape[0] // 2
-    up = step_ring(parts[4][:half], 1)
-    down = step_ring(parts[4][half:], -1)
+    first, last = parts[4]
+    half = first.shape[0]
+    up, down = step_ring(first, 1), step_ring(last, -1)
     up = jnp.concatenate((add(parts[3][:half], up), parts[3][half:]), axis=0)
     down = jnp.concatenate((parts[-3][:half], add(parts[-3][half:], down)), axis=0)
     for distance in (2, 1):
@@ -141,10 +141,62 @@
     return jnp.dot(picking, tokens, preferred_element_type=jnp.float32).astype(jnp.bfloat16)
 
 
-def combine(weighing, rows):
-    return lax.dot_general(
-        weighing, rows, (((0,), (0,)), ((), ())), preferred_element_type=jnp.float32
+def combine_kernel(weighing, rows, *outs):
+    total = jnp.dot(
+        jnp.transpose(weighing[...]), rows[...], preferred_element_type=jnp.float32
     ).astype(jnp.bfloat16)
+    at = 0
+    for out in outs:
+        out[...] = total[at : at + out.shape[0], :]
+        at += out.shape[0]
+
+
+def combine(weighing, rows, heights):
+    whole = pl.BlockSpec(memory_space=pltpu.VMEM)
+    return pl.pallas_call(
+        combine_kernel,
+        in_specs=[whole] * 2,
+        out_specs=[whole] * len(heights),
+        out_shape=[pltpu.HBM((height, rows.shape[1]), jnp.bfloat16) for height in heights],
+        cost_estimate=pl.CostEstimate(
+            flops=2 * weighing.size * rows.shape[1],
+            bytes_accessed=2 * (weighing.size + rows.size + sum(heights) * rows.shape[1]),
+            transcendentals=0,
+        ),
+        compiler_params=pltpu.CompilerParams(vmem_limit_bytes=24 * 1024 * 1024),
+    )(weighing, rows)
+
+
+def start_kernel(forward, edge, stored, gain, info, out):
+    width = edge.shape[1]
+    kept = stored[...].astype(jnp.float32)
+    kept_scale = lax.rsqrt(jnp.mean(kept * kept, axis=-1, keepdims=True) + epsilon)
+    kept = (kept * kept_scale * gain[...]).astype(jnp.bfloat16)
+    out[:, 2 * width :] = info[...]
+
+    @pl.when(forward[0] == 1)
+    def _():
+        fresh = edge[...].astype(jnp.float32)
+        scale = lax.rsqrt(jnp.mean(fresh * fresh, axis=-1, keepdims=True) + epsilon)
+        out[:, :width] = (fresh * scale * gain[...]).astype(jnp.bfloat16)
+        out[:, width : 2 * width] = kept
+
+    @pl.when(forward[0] != 1)
+    def _():
+        out[:, :width] = kept
+        out[:, width : 2 * width] = edge[...]
+
+
+def starting_block(forward, edge, stored, gain, info):
+    whole = pl.BlockSpec(memory_space=pltpu.VMEM)
+    tokens, width = edge.shape
+    return pl.pallas_call(
+        start_kernel,
+        in_specs=[pl.BlockSpec(memory_space=pltpu.SMEM)] + [whole] * 4,
+        out_specs=whole,
+        out_shape=pltpu.HBM((tokens, 2 * width + info.shape[1]), jnp.bfloat16),
+        compiler_params=pltpu.CompilerParams(vmem_limit_bytes=16 * 1024 * 1024),
+    )(forward, edge, stored, gain.reshape(1, -1), info)
 
 
 def normalize(inputs, gain_row):
@@ -240,7 +292,7 @@
             bytes_accessed=6 * width * (rows + inner),
             transcendentals=rows * inner,
         ),
-        compiler_params=pltpu.CompilerParams(vmem_limit_bytes=48 * 1024 * 1024),
+        compiler_params=pltpu.CompilerParams(vmem_limit_bytes=56 * 1024 * 1024),
     )(flag, first, second, *weights)
 
 
@@ -266,11 +318,11 @@
     far_back = exchange(far)
     far_back, near = after(far_back, near)
     near_back = exchange(near)
-    parts = {}
-    for chunk, back, weighing in zip(CHUNKS, (near_back, far_back), weighings):
-        share = combine(weighing, back).reshape(len(chunk), -1, back.shape[-1])
-        for i, k in enumerate(chunk):
-            parts[k] = share[i]
+    parts = dict(zip(CHUNKS[0], combine(weighings[0], near_back, [TOKENS] * len(CHUNKS[0]))))
+    *rest, first, last = combine(
+        weighings[1], far_back, [TOKENS] * (len(CHUNKS[1]) - 1) + [TOKENS // 2] * 2
+    )
+    parts.update(zip(CHUNKS[1], (*rest, (first, last))))
     return sum_ring(parts) / code_sum
 
 
@@ -293,14 +345,12 @@
     info = jnp.pad(info.astype(jnp.bfloat16), ((0, 0), (0, 128 - 4 * top)))
 
     inputs_now = jnp.where(first_segment, edge_rows, stored)
-    widened, scaling, normed = normalize(inputs_now, gain_row)
-    stored_normed = normalize(stored, gain_row)[2]
-    early_rows = jnp.where(first_segment, stored_normed, edge_rows)
+    widened, scaling, _ = normalize(inputs_now, gain_row)
 
     forward_first = first_segment.astype(jnp.int32).reshape(1)
     told = jnp.stack((lax.axis_index(RING), first_segment.astype(jnp.int32)))
 
-    blocks = gather_near(jnp.concatenate((normed, early_rows, info), axis=1))
+    blocks = gather_near(starting_block(forward_first, edge_rows, stored, gain_row, info))
     pairs, place_next, weigh_now, weigh_next = [], [], [], []
     for chunk in CHUNKS:
         if pairs:

time: 413 us -> 409 us (level)
  matrix products: 12.9 us -> 3.58 us
  Pallas kernels: 49.3 us -> 58.1 us
  other arithmetic: 15.5 us -> 8.44 us
    dot_general x4 -> x0, matrix products: 8.28 us -> none  [combine(): lax.dot_general(weighing, rows, (((0,), (0,)), ((), ())), preferred_eleme...]
    pallas_call x0 -> x5, Pallas kernels: none -> 7.67 us  [the longest x4 6.54 us: combine(): pl.pallas_call(combine_kernel, in_specs=[whole] * 2, out_specs=[whole] *...]
    ppermute x32, starting transfers between devices: 47.9 us -> 52.5 us  [step_ring(): lax.ppermute(block, RING, [(i, (i + step) % count) for i in range(count)])]
  transfers between devices with their start and end apart: 40 -> 40, of which waited for: 26 -> 26; matrix products, arithmetic and copies ran while one was open for 4% -> 3% of each run, Pallas kernels for 7% -> 8%
where the time goes in v2:
time: 409 us; the launch traced here: 401 us
  waiting for transfers between devices  189 us (46%)
  starting transfers between devices  87.1 us (21%)
  Pallas kernels  58.1 us (14%)
  blocking collectives  44.9 us (11%)
  local copies, waits for them, and re-layouts  9.27 us (2%)
  other arithmetic  8.44 us (2%)
    ppermute x32, waiting for transfers between devices, step_ring(): lax.ppermute(block, RING, [(i, (i + step) % count) for i in range(count)])  102 us
    all_to_all x7, waiting for transfers between devices, exchange(): lax.all_to_all(parts, PLANE, split_axis=0, concat_axis=0, tiled=True)  82.7 us
    ppermute x32, starting transfers between devices, step_ring(): lax.ppermute(block, RING, [(i, (i + step) % count) for i in range(count)])  52.5 us
    all_to_all x1, blocking collectives, exchange(): lax.all_to_all(parts, PLANE, split_axis=0, concat_axis=0, tiled=True)  44.9 us
    pallas_call x4, Pallas kernels, apply_expert(): pl.pallas_call(functools.partial(expert_kernel, first_at, second_at, forw...  41.4 us
    all_to_all x7, starting transfers between devices, exchange(): lax.all_to_all(parts, PLANE, split_axis=0, concat_axis=0, tiled=True)  30.9 us
    pallas_call x2, Pallas kernels, pick_both(): pl.pallas_call(functools.partial(pick_kernel, top, ring, peers), in_specs...  9.04 us
  transfers between devices with their start and end apart: 40, of which 26 were waited for; matrix products, arithmetic and copies ran while one was open for 3% of the time, Pallas kernels for 8%

profile of v2, /device:TPU:96, one launch (start us, length us, event | category | flops | bytes accessed | tf_op | source)
XLA Modules:
  0.0 401.2 jit_solution(945544109011771381)
XLA Ops:
  4.5 1.1 shard_map.82.refs_0_
  5.6 3.1 collective-permute-start
  8.7 11.8 %collective-permute-done.refs_1_ = bf16[64,4224]{1,0:T(8,128)(2,1)S(1)} collective-permute-done((bf16[64,4224]{1,0:T(8,128)(2,1)}, bf16[64,4224]{1,0:T(8,128)(2,1)S(1)}, u32[]{:S(2)}, u32[]{:S(2)}) %collective-permute-start) | collective-permute-done | bytes 540704 | tf_op jit(solution)/shard_map/ppermute | solution.py:24
  20.6 3.6 collective-permute-start.2
  24.3 10.6 %collective-permute-done.2.refs_3_ = bf16[64,4224]{1,0:T(8,128)(2,1)S(1)} collective-permute-done((bf16[64,4224]{1,0:T(8,128)(2,1)S(1)}, bf16[64,4224]{1,0:T(8,128)(2,1)S(1)}, u32[]{:S(2)}, u32[]{:S(2)}) %collective-permute-start.2) | collective-permute-done | bytes 540704 | tf_op jit(solution)/shard_map/ppermute | solution.py:24
  35.6 4.5 %shard_map.83 = (bf16[384,4096]{1,0:T(8,128)(2,1)}, bf16[384,256]{1,0:T(8,128)(2,1)}, bf16[384,256]{1,0:T(8,128)(2,1)}, bf16[384,256]{1,0:T(8,128)(2,1)}) custom-call(s32[2]{0:T(128)S(1)} %pad_add_fusion.told, bf16[64,4224]{1,0:T(8,128)(2,1)} %shard_map.82.refs_0_, bf16[64,4224]{1,0:T(8,128)(2,1)} %copy-done.27, bf16[64,4224]{1,0:T(8,128)(2,1)} %copy-done.28, ...), custom_call_target="tpu_custom_call" | custom-call | flops 805306368 | bytes 5832704 | tf_op jit(solution)/shard_map/pallas_call | solution.py:125
  40.9 7.0 %all-to-all-start = ((bf16[16,24,4096]{2,1,0:T(8,128)(2,1)}), bf16[16,24,4096]{2,1,0:T(8,128)(2,1)S(1)}, u32[]{:S(2)}, u32[]{:S(2)}) async-start(bf16[16,24,4096]{2,1,0:T(8,128)(2,1)} %bitcast.64), calls=%async_computation | async-start | bytes 6291456 | tf_op jit(solution)/shard_map/all_to_all | solution.py:62
  48.1 3.8 collective-permute-start.4
  51.8 12.9 %collective-permute-done.5.refs_2_ = bf16[64,4224]{1,0:T(8,128)(2,1)S(1)} collective-permute-done((bf16[64,4224]{1,0:T(8,128)(2,1)}, bf16[64,4224]{1,0:T(8,128)(2,1)S(1)}, u32[]{:S(2)}, u32[]{:S(2)}) %collective-permute-start.5) | collective-permute-done | bytes 540704 | tf_op jit(solution)/shard_map/ppermute | solution.py:24
  64.9 3.3 collective-permute-start.6
  68.2 6.1 %collective-permute-done.7 = bf16[32,4224]{1,0:T(8,128)(2,1)S(1)} collective-permute-done((bf16[32,4224]{1,0:T(8,128)(2,1)S(1)}, bf16[32,4224]{1,0:T(8,128)(2,1)S(1)}, u32[]{:S(2)}, u32[]{:S(2)}) %collective-permute-start.7) | collective-permute-done | bytes 270368 | tf_op jit(solution)/shard_map/ppermute | solution.py:24
  75.1 4.6 %shard_map.84 = (bf16[384,4096]{1,0:T(8,128)(2,1)}, bf16[384,256]{1,0:T(8,128)(2,1)}, bf16[384,256]{1,0:T(8,128)(2,1)}, bf16[384,256]{1,0:T(8,128)(2,1)}) custom-call(s32[2]{0:T(128)S(1)} %pad_add_fusion.told, bf16[64,4224]{1,0:T(8,128)(2,1)} %copy-done.25, bf16[64,4224]{1,0:T(8,128)(2,1)} %copy-done.24, bf16[64,4224]{1,0:T(8,128)(2,1)} %copy-done.23, ...), custom_call_target="tpu_custom_call" | custom-call | flops 805306368 | bytes 5832704 | tf_op jit(solution)/shard_map/pallas_call | solution.py:125
  79.7 8.9 %all-to-all-done = bf16[16,24,4096]{2,1,0:T(8,128)(2,1)S(1)} async-done(((bf16[16,24,4096]{2,1,0:T(8,128)(2,1)}), bf16[16,24,4096]{2,1,0:T(8,128)(2,1)S(1)}, u32[]{:S(2)}, u32[]{:S(2)}) %all-to-all-start) | async-done | bytes 3145760 | tf_op jit(solution)/shard_map/all_to_all | solution.py:62
  88.5 44.9 %all_to_all.40 = bf16[16,24,4096]{2,1,0:T(8,128)(2,1)} all-to-all(bf16[16,24,4096]{2,1,0:T(8,128)(2,1)} %bitcast.65), channel_id=1, replica_groups=mesh['segment'=2,'expert_0'=4,'expert_1'=2,'expert_2'=8,'expert_3'=2] {'..., dimensions={0} | all-to-all | bytes 6291456 | tf_op jit(solution)/shard_map/all_to_all | solution.py:62
  133.5 8.9 %shard_map.85 = bf16[384,2048]{1,0:T(8,128)(2,1)} custom-call(s32[1]{0:T(128)} %bitcast.3.forward.flag, bf16[384,4096]{1,0:T(8,128)(2,1)} %bitcast.61, bf16[384,4096]{1,0:T(8,128)(2,1)} %bitcast.62, bf16[2048,768]{1,0:T(8,128)(2,1)} %bitcast.71, bf16[2048,768]{1,0:T(8,128)(2,1)} %bitcast.75, bf16[768,2048]{1,0:T(8,128)(2,1)} %bitcast.79), custom_call_target="tpu_custom_call" | custom-call | flops 6039797760 | bytes 14155776 | tf_op jit(solution)/shard_map/pallas_call | solution.py:282
  142.4 3.7 all-to-all-start.2
  146.1 8.9 %shard_map.86 = bf16[384,2048]{1,0:T(8,128)(2,1)} custom-call(s32[1]{0:T(128)} %bitcast.3.forward.flag, bf16[384,4096]{1,0:T(8,128)(2,1)} %bitcast.58, bf16[384,4096]{1,0:T(8,128)(2,1)} %bitcast.59, bf16[2048,768]{1,0:T(8,128)(2,1)} %bitcast.72, bf16[2048,768]{1,0:T(8,128)(2,1)} %bitcast.76, bf16[768,2048]{1,0:T(8,128)(2,1)} %bitcast.80), custom_call_target="tpu_custom_call" | custom-call | flops 6039797760 | bytes 14155776 | tf_op jit(solution)/shard_map/pallas_call | solution.py:282
  155.0 14.8 %all-to-all-done.2 = bf16[16,24,2048]{2,1,0:T(8,128)(2,1)S(1)} async-done(((bf16[16,24,2048]{2,1,0:T(8,128)(2,1)}), bf16[16,24,2048]{2,1,0:T(8,128)(2,1)S(1)}, u32[]{:S(2)}, u32[]{:S(2)}) %all-to-all-start.2) | async-done | bytes 1572896 | tf_op jit(solution)/shard_map/all_to_all | solution.py:62
  169.7 1.6 shard_map.88
  171.4 3.7 collective-permute-start.8
  176.0 3.9 all-to-all-start.3
  180.0 3.3 collective-permute-start.9
  183.5 5.9 %collective-permute-done.9 = bf16[64,2048]{1,0:T(8,128)(2,1)S(1)} collective-permute-done((bf16[64,2048]{1,0:T(8,128)(2,1)S(1)}, bf16[64,2048]{1,0:T(8,128)(2,1)S(1)}, u32[]{:S(2)}, u32[]{:S(2)}) %collective-permute-start.9) | collective-permute-done | bytes 262176 | tf_op jit(solution)/shard_map/ppermute | solution.py:24
  189.4 3.8 collective-permute-start.10
  193.2 10.3 %all-to-all-done.3 = bf16[16,24,2048]{2,1,0:T(8,128)(2,1)S(1)} async-done(((bf16[16,24,2048]{2,1,0:T(8,128)(2,1)}), bf16[16,24,2048]{2,1,0:T(8,128)(2,1)S(1)}, u32[]{:S(2)}, u32[]{:S(2)}) %all-to-all-start.3) | async-done | bytes 1572896 | tf_op jit(solution)/shard_map/all_to_all | solution.py:62
  203.5 1.6 shard_map.87
  205.2 1.1 add_convert_fusion.5
  207.5 3.5 collective-permute-start.11
  210.9 4.7 %collective-permute-done.14 = bf16[64,2048]{1,0:T(8,128)(2,1)S(1)} collective-permute-done((bf16[64,2048]{1,0:T(8,128)(2,1)S(1)}, bf16[64,2048]{1,0:T(8,128)(2,1)S(1)}, u32[]{:S(2)}, u32[]{:S(2)}) %collective-permute-start.14) | collective-permute-done | bytes 262176 | tf_op jit(solution)/shard_map/ppermute | solution.py:24
  216.3 8.0 %collective-permute-done.15 = bf16[64,2048]{1,0:T(8,128)(2,1)S(1)} collective-permute-done((bf16[64,2048]{1,0:T(8,128)(2,1)S(1)}, bf16[64,2048]{1,0:T(8,128)(2,1)S(1)}, u32[]{:S(2)}, u32[]{:S(2)}) %collective-permute-start.15) | collective-permute-done | bytes 262176 | tf_op jit(solution)/shard_map/ppermute | solution.py:24
  225.1 3.6 collective-permute-start.16
  228.7 4.5 %collective-permute-done.16 = bf16[64,2048]{1,0:T(8,128)(2,1)S(1)} collective-permute-done((bf16[64,2048]{1,0:T(8,128)(2,1)S(1)}, bf16[64,2048]{1,0:T(8,128)(2,1)S(1)}, u32[]{:S(2)}, u32[]{:S(2)}) %collective-permute-start.16) | collective-permute-done | bytes 262176 | tf_op jit(solution)/shard_map/ppermute | solution.py:373
  233.7 2.0 collective-permute-start.18
  235.8 5.4 %collective-permute-done.17 = bf16[64,2048]{1,0:T(8,128)(2,1)S(1)} collective-permute-done((bf16[64,2048]{1,0:T(8,128)(2,1)S(1)}, bf16[64,2048]{1,0:T(8,128)(2,1)S(1)}, u32[]{:S(2)}, u32[]{:S(2)}) %collective-permute-start.17) | collective-permute-done | bytes 262176 | tf_op jit(solution)/shard_map/ppermute | solution.py:24
  241.4 1.8 collective-permute-start.20
  243.2 4.3 %collective-permute-done.19 = bf16[64,2048]{1,0:T(8,128)(2,1)S(1)} collective-permute-done((bf16[64,2048]{1,0:T(8,128)(2,1)S(1)}, bf16[64,2048]{1,0:T(8,128)(2,1)S(1)}, u32[]{:S(2)}, u32[]{:S(2)}) %collective-permute-start.19) | collective-permute-done | bytes 262176 | tf_op jit(solution)/shard_map/ppermute | solution.py:24
  247.5 1.8 convolution_convert_fusion.1
  249.4 4.4 %all-to-all-start.4 = ((bf16[16,24,2048]{2,1,0:T(8,128)(2,1)}), bf16[16,24,2048]{2,1,0:T(8,128)(2,1)S(1)}, u32[]{:S(2)}, u32[]{:S(2)}) async-start(bf16[16,24,2048]{2,1,0:T(8,128)(2,1)} %bitcast.68), calls=%async_computation.4 | async-start | bytes 3145728 | tf_op jit(solution)/shard_map/all_to_all | solution.py:62
  253.7 2.8 collective-permute-start.21
  256.5 6.1 %collective-permute-done.21 = bf16[64,2048]{1,0:T(8,128)(2,1)S(1)} collective-permute-done((bf16[64,2048]{1,0:T(8,128)(2,1)S(1)}, bf16[64,2048]{1,0:T(8,128)(2,1)S(1)}, u32[]{:S(2)}, u32[]{:S(2)}) %collective-permute-start.21) | collective-permute-done | bytes 262176 | tf_op jit(solution)/shard_map/ppermute | solution.py:24
  262.7 3.8 collective-permute-start.23
  266.6 2.4 collective-permute-done.23
  269.0 3.7 collective-permute-done.24
  272.8 1.8 convolution_convert_fusion
  274.5 2.9 all-to-all-done.4
  277.4 1.2 copy-done.11
  278.7 4.4 %all-to-all-start.5 = ((bf16[16,24,2048]{2,1,0:T(8,128)(2,1)}), bf16[16,24,2048]{2,1,0:T(8,128)(2,1)}, u32[]{:S(2)}, u32[]{:S(2)}) async-start(bf16[16,24,2048]{2,1,0:T(8,128)(2,1)} %bitcast.22), calls=%async_computation.5 | async-start | bytes 3145728 | tf_op jit(solution)/shard_map/all_to_all | solution.py:62
  283.1 23.7 %all-to-all-done.5 = bf16[16,24,2048]{2,1,0:T(8,128)(2,1)} async-done(((bf16[16,24,2048]{2,1,0:T(8,128)(2,1)}), bf16[16,24,2048]{2,1,0:T(8,128)(2,1)}, u32[]{:S(2)}, u32[]{:S(2)}) %all-to-all-start.5) | async-done | bytes 1572896 | tf_op jit(solution)/shard_map/all_to_all | solution.py:62
  306.8 11.8 %shard_map.89 = bf16[384,2048]{1,0:T(8,128)(2,1)} custom-call(s32[1]{0:T(128)S(6)} %sub.11.flag, bf16[384,4096]{1,0:T(8,128)(2,1)} %bitcast.63, bf16[384,2048]{1,0:T(8,128)(2,1)} %bitcast.23.second, bf16[2048,768]{1,0:T(8,128)(2,1)} %bitcast.73, bf16[2048,768]{1,0:T(8,128)(2,1)} %bitcast.77, bf16[768,2048]{1,0:T(8,128)(2,1)} %bitcast.81), custom_call_target="tpu_custom_call" | custom-call | flops 6039797760 | bytes 14155776 | tf_op jit(solution)/shard_map/pallas_call | solution.py:282
  318.6 3.7 all-to-all-start.6
  322.3 11.8 %shard_map.90 = bf16[384,2048]{1,0:T(8,128)(2,1)} custom-call(s32[1]{0:T(128)S(6)} %sub.11.flag, bf16[384,4096]{1,0:T(8,128)(2,1)} %bitcast.60, bf16[384,2048]{1,0:T(8,128)(2,1)} %bitcast.66, bf16[2048,768]{1,0:T(8,128)(2,1)} %bitcast.74, bf16[2048,768]{1,0:T(8,128)(2,1)} %bitcast.78, bf16[768,2048]{1,0:T(8,128)(2,1)} %bitcast.82), custom_call_target="tpu_custom_call" | custom-call | flops 6039797760 | bytes 14155776 | tf_op jit(solution)/shard_map/pallas_call | solution.py:282
  334.1 11.8 %all-to-all-done.6 = bf16[16,24,2048]{2,1,0:T(8,128)(2,1)S(1)} async-done(((bf16[16,24,2048]{2,1,0:T(8,128)(2,1)}), bf16[16,24,2048]{2,1,0:T(8,128)(2,1)S(1)}, u32[]{:S(2)}, u32[]{:S(2)}) %all-to-all-start.6) | async-done | bytes 1572896 | tf_op jit(solution)/shard_map/all_to_all | solution.py:62
  345.9 1.6 shard_map.92
  347.6 2.7 collective-permute-start.25
  351.2 3.9 all-to-all-start.7
  355.2 3.3 collective-permute-start.26
  358.7 5.9 %collective-permute-done.26 = bf16[64,2048]{1,0:T(8,128)(2,1)S(1)} collective-permute-done((bf16[64,2048]{1,0:T(8,128)(2,1)S(1)}, bf16[64,2048]{1,0:T(8,128)(2,1)S(1)}, u32[]{:S(2)}, u32[]{:S(2)}) %collective-permute-start.26) | collective-permute-done | bytes 262176 | tf_op jit(solution)/shard_map/ppermute | solution.py:24
  364.6 3.8 collective-permute-start.27
  368.4 10.3 %all-to-all-done.7 = bf16[16,24,2048]{2,1,0:T(8,128)(2,1)S(1)} async-done(((bf16[16,24,2048]{2,1,0:T(8,128)(2,1)}), bf16[16,24,2048]{2,1,0:T(8,128)(2,1)S(1)}, u32[]{:S(2)}, u32[]{:S(2)}) %all-to-all-start.7) | async-done | bytes 1572896 | tf_op jit(solution)/shard_map/all_to_all | solution.py:62
  378.7 1.6 shard_map.91
  382.6 3.3 collective-permute-start.28
  385.9 4.9 %collective-permute-done.31 = bf16[64,2048]{1,0:T(8,128)(2,1)S(1)} collective-permute-done((bf16[64,2048]{1,0:T(8,128)(2,1)S(1)}, bf16[64,2048]{1,0:T(8,128)(2,1)S(1)}, u32[]{:S(2)}, u32[]{:S(2)}) %collective-permute-start.31) | collective-permute-done | bytes 262176 | tf_op jit(solution)/shard_map/ppermute | solution.py:24
  391.2 8.2 %collective-permute-done.32 = bf16[64,2048]{1,0:T(8,128)(2,1)S(1)} collective-permute-done((bf16[64,2048]{1,0:T(8,128)(2,1)S(1)}, bf16[64,2048]{1,0:T(8,128)(2,1)S(1)}, u32[]{:S(2)}, u32[]{:S(2)}) %collective-permute-start.32) | collective-permute-done | bytes 262176 | tf_op jit(solution)/shard_map/ppermute | solution.py:24
  399.7 1.1 fusion.21
  (140 shorter events, 15.9 us)
Async XLA Ops:
  5.6 15.0 %collective-permute-start = (bf16[64,4224]{1,0:T(8,128)(2,1)}, bf16[64,4224]{1,0:T(8,128)(2,1)S(1)}, u32[]{:S(2)}, u32[]{:S(2)}) collective-permute-start(bf16[64,4224]{1,0:T(8,128)(2,1)} %shard_map.82.refs_0_), channel_id=1, source_target_pairs={{0,2},{2,4},{4,6},{6,8},{8,10},{10,12},{12,14},{14,0},{1,3},{3,5},... | collective-permute-start | bytes 1622024 | tf_op jit(solution)/shard_map/ppermute | solution.py:24
  8.7 15.4 %collective-permute-start.1 = (bf16[64,4224]{1,0:T(8,128)(2,1)}, bf16[64,4224]{1,0:T(8,128)(2,1)S(1)}, u32[]{:S(2)}, u32[]{:S(2)}) collective-permute-start(bf16[64,4224]{1,0:T(8,128)(2,1)} %shard_map.82.refs_0_), channel_id=1, source_target_pairs={{0,14},{2,0},{4,2},{6,4},{8,6},{10,8},{12,10},{14,12},{1,15},{3,1}... | collective-permute-start | bytes 1622024 | tf_op jit(solution)/shard_map/ppermute | solution.py:24
  20.6 14.3 %copy-start.27 = (bf16[64,4224]{1,0:T(8,128)(2,1)}, bf16[64,4224]{1,0:T(8,128)(2,1)S(1)}, u32[]{:S(2)}) copy-start(bf16[64,4224]{1,0:T(8,128)(2,1)S(1)} %collective-permute-done.refs_1_) | copy-start | bytes 1622020
  20.6 14.2 %collective-permute-start.2 = (bf16[64,4224]{1,0:T(8,128)(2,1)S(1)}, bf16[64,4224]{1,0:T(8,128)(2,1)S(1)}, u32[]{:S(2)}, u32[]{:S(2)}) collective-permute-start(bf16[64,4224]{1,0:T(8,128)(2,1)S(1)} %collective-permute-done.refs_1_), channel_id=1, source_target_pairs={{0,2},{2,4},{4,6},{6,8},{8,10},{10,12},{12,14},{14,0},{1,3},{3,5},... | collective-permute-start | bytes 1622024 | tf_op jit(solution)/shard_map/ppermute | solution.py:24
  24.2 10.7 %copy-start.28 = (bf16[64,4224]{1,0:T(8,128)(2,1)}, bf16[64,4224]{1,0:T(8,128)(2,1)S(1)}, u32[]{:S(2)}) copy-start(bf16[64,4224]{1,0:T(8,128)(2,1)S(1)} %collective-permute-done.1.refs_2_) | copy-start | bytes 1622020
  24.2 16.0 %collective-permute-start.3 = (bf16[64,4224]{1,0:T(8,128)(2,1)S(1)}, bf16[64,4224]{1,0:T(8,128)(2,1)S(1)}, u32[]{:S(2)}, u32[]{:S(2)}) collective-permute-start(bf16[64,4224]{1,0:T(8,128)(2,1)S(1)} %collective-permute-done.1.refs_2_), channel_id=1, source_target_pairs={{0,14},{2,0},{4,2},{6,4},{8,6},{10,8},{12,10},{14,12},{1,15},{3,1}... | collective-permute-start | bytes 1622024 | tf_op jit(solution)/shard_map/ppermute | solution.py:24
  40.9 47.6 %all-to-all-start = ((bf16[16,24,4096]{2,1,0:T(8,128)(2,1)}), bf16[16,24,4096]{2,1,0:T(8,128)(2,1)S(1)}, u32[]{:S(2)}, u32[]{:S(2)}) async-start(bf16[16,24,4096]{2,1,0:T(8,128)(2,1)} %bitcast.64), calls=%async_computation | async-start | bytes 6291456 | tf_op jit(solution)/shard_map/all_to_all | solution.py:62
  48.0 16.8 %collective-permute-start.5 = (bf16[64,4224]{1,0:T(8,128)(2,1)}, bf16[64,4224]{1,0:T(8,128)(2,1)S(1)}, u32[]{:S(2)}, u32[]{:S(2)}) collective-permute-start(bf16[64,4224]{1,0:T(8,128)(2,1)} %copy-done.25), channel_id=1, source_target_pairs={{0,14},{2,0},{4,2},{6,4},{8,6},{10,8},{12,10},{14,12},{1,15},{3,1}... | collective-permute-start | bytes 1622024 | tf_op jit(solution)/shard_map/ppermute | solution.py:24
  48.1 16.8 %collective-permute-start.4 = (bf16[64,4224]{1,0:T(8,128)(2,1)}, bf16[64,4224]{1,0:T(8,128)(2,1)S(1)}, u32[]{:S(2)}, u32[]{:S(2)}) collective-permute-start(bf16[64,4224]{1,0:T(8,128)(2,1)} %copy-done.26), channel_id=1, source_target_pairs={{0,2},{2,4},{4,6},{6,8},{8,10},{10,12},{12,14},{14,0},{1,3},{3,5},... | collective-permute-start | bytes 1622024 | tf_op jit(solution)/shard_map/ppermute | solution.py:24
  64.7 10.4 %copy-start.23 = (bf16[64,4224]{1,0:T(8,128)(2,1)}, bf16[64,4224]{1,0:T(8,128)(2,1)S(1)}, u32[]{:S(2)}) copy-start(bf16[64,4224]{1,0:T(8,128)(2,1)S(1)} %collective-permute-done.5.refs_2_) | copy-start | bytes 1622020
  64.7 9.5 %collective-permute-start.7 = (bf16[32,4224]{1,0:T(8,128)(2,1)S(1)}, bf16[32,4224]{1,0:T(8,128)(2,1)S(1)}, u32[]{:S(2)}, u32[]{:S(2)}) collective-permute-start(bf16[32,4224]{1,0:T(8,128)(2,1)S(1)} %slice.69), channel_id=1, source_target_pairs={{0,14},{2,0},{4,2},{6,4},{8,6},{10,8},{12,10},{14,12},{1,15},{3,1}... | collective-permute-start | bytes 811016 | tf_op jit(solution)/shard_map/ppermute | solution.py:24
  64.8 10.3 %copy-start.24 = (bf16[64,4224]{1,0:T(8,128)(2,1)}, bf16[64,4224]{1,0:T(8,128)(2,1)S(1)}, u32[]{:S(2)}) copy-start(bf16[64,4224]{1,0:T(8,128)(2,1)S(1)} %collective-permute-done.4.refs_1_) | copy-start | bytes 1622020
  64.9 9.4 %collective-permute-start.6 = (bf16[32,4224]{1,0:T(8,128)(2,1)S(1)}, bf16[32,4224]{1,0:T(8,128)(2,1)S(1)}, u32[]{:S(2)}, u32[]{:S(2)}) collective-permute-start(bf16[32,4224]{1,0:T(8,128)(2,1)S(1)} %slice.68), channel_id=1, source_target_pairs={{0,2},{2,4},{4,6},{6,8},{8,10},{10,12},{12,14},{14,0},{1,3},{3,5},... | collective-permute-start | bytes 811016 | tf_op jit(solution)/shard_map/ppermute | solution.py:24
  88.5 44.9 %copy-start.10 = (bf16[16,24,4096]{2,1,0:T(8,128)(2,1)}, bf16[16,24,4096]{2,1,0:T(8,128)(2,1)S(1)}, u32[]{:S(2)}) copy-start(bf16[16,24,4096]{2,1,0:T(8,128)(2,1)S(1)} %all-to-all-done) | copy-start | bytes 9437188
  142.4 27.4 %all-to-all-start.2 = ((bf16[16,24,2048]{2,1,0:T(8,128)(2,1)}), bf16[16,24,2048]{2,1,0:T(8,128)(2,1)S(1)}, u32[]{:S(2)}, u32[]{:S(2)}) async-start(bf16[16,24,2048]{2,1,0:T(8,128)(2,1)} %bitcast.70), calls=%async_computation.2 | async-start | bytes 3145728 | tf_op jit(solution)/shard_map/all_to_all | solution.py:62
  146.1 23.7 %copy-start.9 = (bf16[384,256]{1,0:T(8,128)(2,1)S(1)}, bf16[384,256]{1,0:T(8,128)(2,1)}, u32[]{:S(2)}) copy-start(bf16[384,256]{1,0:T(8,128)(2,1)} %get-tuple-element.53.weighing) | copy-start | bytes 589828
  171.4 8.6 %collective-permute-start.8 = (bf16[32,2048]{1,0:T(8,128)(2,1)}, bf16[32,2048]{1,0:T(8,128)(2,1)S(1)}, u32[]{:S(2)}, u32[]{:S(2)}) collective-permute-start(bf16[32,2048]{1,0:T(8,128)(2,1)} %get-tuple-element.57), channel_id=1, source_target_pairs={{0,2},{2,4},{4,6},{6,8},{8,10},{10,12},{12,14},{14,0},{1,3},{3,5},... | collective-permute-start | bytes 393224 | tf_op jit(solution)/shard_map/ppermute | solution.py:24
  175.1 8.2 %collective-permute-start.12 = (bf16[32,2048]{1,0:T(8,128)(2,1)}, bf16[32,2048]{1,0:T(8,128)(2,1)S(1)}, u32[]{:S(2)}, u32[]{:S(2)}) collective-permute-start(bf16[32,2048]{1,0:T(8,128)(2,1)} %get-tuple-element.61), channel_id=1, source_target_pairs={{0,14},{2,0},{4,2},{6,4},{8,6},{10,8},{12,10},{14,12},{1,15},{3,1}... | collective-permute-start | bytes 393224 | tf_op jit(solution)/shard_map/ppermute | solution.py:24
  176.0 3.9 copy-start.20
  176.0 7.3 %copy-start.18 = (bf16[64,2048]{1,0:T(8,128)(2,1)S(1)}, bf16[64,2048]{1,0:T(8,128)(2,1)}, u32[]{:S(2)}) copy-start(bf16[64,2048]{1,0:T(8,128)(2,1)} %get-tuple-element.60) | copy-start | bytes 786436
  176.0 27.5 %all-to-all-start.3 = ((bf16[16,24,2048]{2,1,0:T(8,128)(2,1)}), bf16[16,24,2048]{2,1,0:T(8,128)(2,1)S(1)}, u32[]{:S(2)}, u32[]{:S(2)}) async-start(bf16[16,24,2048]{2,1,0:T(8,128)(2,1)} %bitcast.17), calls=%async_computation.3 | async-start | bytes 3145728 | tf_op jit(solution)/shard_map/all_to_all | solution.py:62
  179.9 9.5 %copy-start.14 = (bf16[64,2048]{1,0:T(8,128)(2,1)S(1)}, bf16[64,2048]{1,0:T(8,128)(2,1)}, u32[]{:S(2)}) copy-start(bf16[64,2048]{1,0:T(8,128)(2,1)} %get-tuple-element.55) | copy-start | bytes 786436
  179.9 23.6 %copy-start.8 = (bf16[384,256]{1,0:T(8,128)(2,1)S(1)}, bf16[384,256]{1,0:T(8,128)(2,1)}, u32[]{:S(2)}) copy-start(bf16[384,256]{1,0:T(8,128)(2,1)} %get-tuple-element.42.weighing) | copy-start | bytes 589828
  180.0 9.3 %collective-permute-start.9 = (bf16[64,2048]{1,0:T(8,128)(2,1)S(1)}, bf16[64,2048]{1,0:T(8,128)(2,1)S(1)}, u32[]{:S(2)}, u32[]{:S(2)}) collective-permute-start(bf16[64,2048]{1,0:T(8,128)(2,1)S(1)} %pad_maximum_fusion.1), channel_id=1, source_target_pairs={{0,2},{2,4},{4,6},{6,8},{8,10},{10,12},{12,14},{14,0},{1,3},{3,5},... | collective-permute-start | bytes 786440 | tf_op jit(solution)/shard_map/ppermute | solution.py:24
  183.4 21.8 %collective-permute-start.13 = (bf16[64,2048]{1,0:T(8,128)(2,1)S(1)}, bf16[64,2048]{1,0:T(8,128)(2,1)S(1)}, u32[]{:S(2)}, u32[]{:S(2)}) collective-permute-start(bf16[64,2048]{1,0:T(8,128)(2,1)S(1)} %pad_maximum_fusion.2), channel_id=1, source_target_pairs={{0,14},{2,0},{4,2},{6,4},{8,6},{10,8},{12,10},{14,12},{1,15},{3,1}... | collective-permute-start | bytes 786440 | tf_op jit(solution)/shard_map/ppermute | solution.py:24
  189.4 17.0 %collective-permute-start.10 = (bf16[64,2048]{1,0:T(8,128)(2,1)S(1)}, bf16[64,2048]{1,0:T(8,128)(2,1)S(1)}, u32[]{:S(2)}, u32[]{:S(2)}) collective-permute-start(bf16[64,2048]{1,0:T(8,128)(2,1)S(1)} %add_convert_fusion.7), channel_id=1, source_target_pairs={{0,2},{2,4},{4,6},{6,8},{8,10},{10,12},{12,14},{14,0},{1,3},{3,5},... | collective-permute-start | bytes 786440 | tf_op jit(solution)/shard_map/ppermute | solution.py:24
  205.2 10.5 %copy-start.16 = (bf16[64,2048]{1,0:T(8,128)(2,1)S(1)}, bf16[64,2048]{1,0:T(8,128)(2,1)}, u32[]{:S(2)}) copy-start(bf16[64,2048]{1,0:T(8,128)(2,1)} %get-tuple-element.58) | copy-start | bytes 786436
  205.2 19.1 %copy-start.1 = (bf16[1,64,2048]{2,1,0:T(8,128)(2,1)S(1)}, bf16[1,64,2048]{2,1,0:T(8,128)(2,1)}, u32[]{:S(2)}) copy-start(bf16[1,64,2048]{2,1,0:T(8,128)(2,1)} %param.9) | copy-start | bytes 786436
  205.2 19.1 %copy-start.3 = (bf16[1,64,2048]{2,1,0:T(8,128)(2,1)S(1)}, bf16[1,64,2048]{2,1,0:T(8,128)(2,1)}, u32[]{:S(2)}) copy-start(bf16[1,64,2048]{2,1,0:T(8,128)(2,1)} %param.8) | copy-start | bytes 786436
  205.2 19.1 %copy-start.5 = (f32[1,2048]{1,0:T(1,128)S(1)}, f32[1,2048]{1,0:T(1,128)}, u32[]{:S(2)}) copy-start(f32[1,2048]{1,0:T(1,128)} %gain.1) | copy-start | bytes 24580
  205.2 19.1 %copy-start.12 = (bf16[64,2048]{1,0:T(8,128)(2,1)S(1)}, bf16[64,2048]{1,0:T(8,128)(2,1)}, u32[]{:S(2)}) copy-start(bf16[64,2048]{1,0:T(8,128)(2,1)} %get-tuple-element.51) | copy-start | bytes 786436
  206.3 9.4 %collective-permute-start.14 = (bf16[64,2048]{1,0:T(8,128)(2,1)S(1)}, bf16[64,2048]{1,0:T(8,128)(2,1)S(1)}, u32[]{:S(2)}, u32[]{:S(2)}) collective-permute-start(bf16[64,2048]{1,0:T(8,128)(2,1)S(1)} %add_convert_fusion.5), channel_id=1, source_target_pairs={{0,14},{2,0},{4,2},{6,4},{8,6},{10,8},{12,10},{14,12},{1,15},{3,1}... | collective-permute-start | bytes 786440 | tf_op jit(solution)/shard_map/ppermute | solution.py:24
  207.5 8.8 %collective-permute-start.11 = (bf16[64,2048]{1,0:T(8,128)(2,1)S(1)}, bf16[64,2048]{1,0:T(8,128)(2,1)S(1)}, u32[]{:S(2)}, u32[]{:S(2)}) collective-permute-start(bf16[64,2048]{1,0:T(8,128)(2,1)S(1)} %add_convert_fusion.6), channel_id=1, source_target_pairs={{0,2},{2,4},{4,6},{6,8},{8,10},{10,12},{12,14},{14,0},{1,3},{3,5},... | collective-permute-start | bytes 786440 | tf_op jit(solution)/shard_map/ppermute | solution.py:24
  215.8 8.5 %collective-permute-start.15 = (bf16[64,2048]{1,0:T(8,128)(2,1)S(1)}, bf16[64,2048]{1,0:T(8,128)(2,1)S(1)}, u32[]{:S(2)}, u32[]{:S(2)}) collective-permute-start(bf16[64,2048]{1,0:T(8,128)(2,1)S(1)} %add_convert_fusion.4), channel_id=1, source_target_pairs={{0,14},{2,0},{4,2},{6,4},{8,6},{10,8},{12,10},{14,12},{1,15},{3,1}... | collective-permute-start | bytes 786440 | tf_op jit(solution)/shard_map/ppermute | solution.py:24
  224.6 22.9 %copy-start.29 = (bf16[384,256]{1,0:T(8,128)(2,1)S(1)}, bf16[384,256]{1,0:T(8,128)(2,1)}, u32[]{:S(2)}) copy-start(bf16[384,256]{1,0:T(8,128)(2,1)} %get-tuple-element.63) | copy-start | bytes 589828
  225.1 8.2 %collective-permute-start.16 = (bf16[64,2048]{1,0:T(8,128)(2,1)S(1)}, bf16[64,2048]{1,0:T(8,128)(2,1)S(1)}, u32[]{:S(2)}, u32[]{:S(2)}) collective-permute-start(bf16[64,2048]{1,0:T(8,128)(2,1)S(1)} %fusion.8), channel_id=1, source_target_pairs={{0,128},{128,0},{1,129},{129,1},{2,130},{130,2},{3,131},{131,3},{4... | collective-permute-start | bytes 786440 | tf_op jit(solution)/shard_map/ppermute | solution.py:373
  233.6 7.5 %collective-permute-start.17 = (bf16[64,2048]{1,0:T(8,128)(2,1)S(1)}, bf16[64,2048]{1,0:T(8,128)(2,1)S(1)}, u32[]{:S(2)}, u32[]{:S(2)}) collective-permute-start(bf16[64,2048]{1,0:T(8,128)(2,1)S(1)} %fusion.22), channel_id=1, source_target_pairs={{0,2},{2,4},{4,6},{6,8},{8,10},{10,12},{12,14},{14,0},{1,3},{3,5},... | collective-permute-start | bytes 786440 | tf_op jit(solution)/shard_map/ppermute | solution.py:24
  233.7 7.7 %collective-permute-start.18 = (bf16[64,2048]{1,0:T(8,128)(2,1)S(1)}, bf16[64,2048]{1,0:T(8,128)(2,1)S(1)}, u32[]{:S(2)}, u32[]{:S(2)}) collective-permute-start(bf16[64,2048]{1,0:T(8,128)(2,1)S(1)} %fusion.22), channel_id=1, source_target_pairs={{0,14},{2,0},{4,2},{6,4},{8,6},{10,8},{12,10},{14,12},{1,15},{3,1}... | collective-permute-start | bytes 786440 | tf_op jit(solution)/shard_map/ppermute | solution.py:24
  241.2 6.4 %collective-permute-start.19 = (bf16[64,2048]{1,0:T(8,128)(2,1)S(1)}, bf16[64,2048]{1,0:T(8,128)(2,1)S(1)}, u32[]{:S(2)}, u32[]{:S(2)}) collective-permute-start(bf16[64,2048]{1,0:T(8,128)(2,1)S(1)} %collective-permute-done.17), channel_id=1, source_target_pairs={{0,2},{2,4},{4,6},{6,8},{8,10},{10,12},{12,14},{14,0},{1,3},{3,5},... | collective-permute-start | bytes 786440 | tf_op jit(solution)/shard_map/ppermute | solution.py:24
  241.4 15.1 %collective-permute-start.20 = (bf16[64,2048]{1,0:T(8,128)(2,1)S(1)}, bf16[64,2048]{1,0:T(8,128)(2,1)S(1)}, u32[]{:S(2)}, u32[]{:S(2)}) collective-permute-start(bf16[64,2048]{1,0:T(8,128)(2,1)S(1)} %collective-permute-done.18), channel_id=1, source_target_pairs={{0,14},{2,0},{4,2},{6,4},{8,6},{10,8},{12,10},{14,12},{1,15},{3,1}... | collective-permute-start | bytes 786440 | tf_op jit(solution)/shard_map/ppermute | solution.py:24
  249.4 28.1 %all-to-all-start.4 = ((bf16[16,24,2048]{2,1,0:T(8,128)(2,1)}), bf16[16,24,2048]{2,1,0:T(8,128)(2,1)S(1)}, u32[]{:S(2)}, u32[]{:S(2)}) async-start(bf16[16,24,2048]{2,1,0:T(8,128)(2,1)} %bitcast.68), calls=%async_computation.4 | async-start | bytes 3145728 | tf_op jit(solution)/shard_map/all_to_all | solution.py:62
  253.7 19.0 %copy-start.22 = (bf16[384,256]{1,0:T(8,128)(2,1)S(1)}, bf16[384,256]{1,0:T(8,128)(2,1)}, u32[]{:S(2)}) copy-start(bf16[384,256]{1,0:T(8,128)(2,1)} %get-tuple-element.64) | copy-start | bytes 589828
  253.7 8.9 %collective-permute-start.21 = (bf16[64,2048]{1,0:T(8,128)(2,1)S(1)}, bf16[64,2048]{1,0:T(8,128)(2,1)S(1)}, u32[]{:S(2)}, u32[]{:S(2)}) collective-permute-start(bf16[64,2048]{1,0:T(8,128)(2,1)S(1)} %collective-permute-done.19), channel_id=1, source_target_pairs={{0,2},{2,4},{4,6},{6,8},{8,10},{10,12},{12,14},{14,0},{1,3},{3,5},... | collective-permute-start | bytes 786440 | tf_op jit(solution)/shard_map/ppermute | solution.py:24
  256.5 9.9 %collective-permute-start.22 = (bf16[64,2048]{1,0:T(8,128)(2,1)S(1)}, bf16[64,2048]{1,0:T(8,128)(2,1)S(1)}, u32[]{:S(2)}, u32[]{:S(2)}) collective-permute-start(bf16[64,2048]{1,0:T(8,128)(2,1)S(1)} %collective-permute-done.20), channel_id=1, source_target_pairs={{0,14},{2,0},{4,2},{6,4},{8,6},{10,8},{12,10},{14,12},{1,15},{3,1}... | collective-permute-start | bytes 786440 | tf_op jit(solution)/shard_map/ppermute | solution.py:24
  262.7 6.3 %collective-permute-start.23 = (bf16[32,2048]{1,0:T(8,128)(2,1)S(1)}, bf16[32,2048]{1,0:T(8,128)(2,1)S(1)}, u32[]{:S(2)}, u32[]{:S(2)}) collective-permute-start(bf16[32,2048]{1,0:T(8,128)(2,1)S(1)} %slice.70), channel_id=1, source_target_pairs={{0,2},{2,4},{4,6},{6,8},{8,10},{10,12},{12,14},{14,0},{1,3},{3,5},... | collective-permute-start | bytes 393224 | tf_op jit(solution)/shard_map/ppermute | solution.py:24
  266.5 6.3 %collective-permute-start.24 = (bf16[32,2048]{1,0:T(8,128)(2,1)S(1)}, bf16[32,2048]{1,0:T(8,128)(2,1)S(1)}, u32[]{:S(2)}, u32[]{:S(2)}) collective-permute-start(bf16[32,2048]{1,0:T(8,128)(2,1)S(1)} %slice.71), channel_id=1, source_target_pairs={{0,14},{2,0},{4,2},{6,4},{8,6},{10,8},{12,10},{14,12},{1,15},{3,1}... | collective-permute-start | bytes 393224 | tf_op jit(solution)/shard_map/ppermute | solution.py:24
  278.7 28.1 %all-to-all-start.5 = ((bf16[16,24,2048]{2,1,0:T(8,128)(2,1)}), bf16[16,24,2048]{2,1,0:T(8,128)(2,1)}, u32[]{:S(2)}, u32[]{:S(2)}) async-start(bf16[16,24,2048]{2,1,0:T(8,128)(2,1)} %bitcast.22), calls=%async_computation.5 | async-start | bytes 3145728 | tf_op jit(solution)/shard_map/all_to_all | solution.py:62
  318.6 27.4 %all-to-all-start.6 = ((bf16[16,24,2048]{2,1,0:T(8,128)(2,1)}), bf16[16,24,2048]{2,1,0:T(8,128)(2,1)S(1)}, u32[]{:S(2)}, u32[]{:S(2)}) async-start(bf16[16,24,2048]{2,1,0:T(8,128)(2,1)} %bitcast.69), calls=%async_computation.6 | async-start | bytes 3145728 | tf_op jit(solution)/shard_map/all_to_all | solution.py:62
  322.3 23.7 %copy-start.7 = (bf16[384,256]{1,0:T(8,128)(2,1)S(1)}, bf16[384,256]{1,0:T(8,128)(2,1)}, u32[]{:S(2)}) copy-start(bf16[384,256]{1,0:T(8,128)(2,1)} %get-tuple-element.70.weighing) | copy-start | bytes 589828
  347.6 7.6 %collective-permute-start.25 = (bf16[32,2048]{1,0:T(8,128)(2,1)}, bf16[32,2048]{1,0:T(8,128)(2,1)S(1)}, u32[]{:S(2)}, u32[]{:S(2)}) collective-permute-start(bf16[32,2048]{1,0:T(8,128)(2,1)} %get-tuple-element.74), channel_id=1, source_target_pairs={{0,2},{2,4},{4,6},{6,8},{8,10},{10,12},{12,14},{14,0},{1,3},{3,5},... | collective-permute-start | bytes 393224 | tf_op jit(solution)/shard_map/ppermute | solution.py:24
  350.3 8.2 %collective-permute-start.29 = (bf16[32,2048]{1,0:T(8,128)(2,1)}, bf16[32,2048]{1,0:T(8,128)(2,1)S(1)}, u32[]{:S(2)}, u32[]{:S(2)}) collective-permute-start(bf16[32,2048]{1,0:T(8,128)(2,1)} %get-tuple-element.78), channel_id=1, source_target_pairs={{0,14},{2,0},{4,2},{6,4},{8,6},{10,8},{12,10},{14,12},{1,15},{3,1}... | collective-permute-start | bytes 393224 | tf_op jit(solution)/shard_map/ppermute | solution.py:24
  351.2 3.9 copy-start.21
  351.2 7.3 %copy-start.19 = (bf16[64,2048]{1,0:T(8,128)(2,1)S(1)}, bf16[64,2048]{1,0:T(8,128)(2,1)}, u32[]{:S(2)}) copy-start(bf16[64,2048]{1,0:T(8,128)(2,1)} %get-tuple-element.77) | copy-start | bytes 786436
  351.2 27.5 %all-to-all-start.7 = ((bf16[16,24,2048]{2,1,0:T(8,128)(2,1)}), bf16[16,24,2048]{2,1,0:T(8,128)(2,1)S(1)}, u32[]{:S(2)}, u32[]{:S(2)}) async-start(bf16[16,24,2048]{2,1,0:T(8,128)(2,1)} %bitcast.67), calls=%async_computation.7 | async-start | bytes 3145728 | tf_op jit(solution)/shard_map/all_to_all | solution.py:62
  355.1 9.5 %copy-start.15 = (bf16[64,2048]{1,0:T(8,128)(2,1)S(1)}, bf16[64,2048]{1,0:T(8,128)(2,1)}, u32[]{:S(2)}) copy-start(bf16[64,2048]{1,0:T(8,128)(2,1)} %get-tuple-element.72) | copy-start | bytes 786436
  355.1 23.6 %copy-start.6 = (bf16[384,256]{1,0:T(8,128)(2,1)S(1)}, bf16[384,256]{1,0:T(8,128)(2,1)}, u32[]{:S(2)}) copy-start(bf16[384,256]{1,0:T(8,128)(2,1)} %get-tuple-element.62.weighing) | copy-start | bytes 589828
  355.2 9.3 %collective-permute-start.26 = (bf16[64,2048]{1,0:T(8,128)(2,1)S(1)}, bf16[64,2048]{1,0:T(8,128)(2,1)S(1)}, u32[]{:S(2)}, u32[]{:S(2)}) collective-permute-start(bf16[64,2048]{1,0:T(8,128)(2,1)S(1)} %pad_maximum_fusion.3), channel_id=1, source_target_pairs={{0,2},{2,4},{4,6},{6,8},{8,10},{10,12},{12,14},{14,0},{1,3},{3,5},... | collective-permute-start | bytes 786440 | tf_op jit(solution)/shard_map/ppermute | solution.py:24
  358.6 21.8 %collective-permute-start.30 = (bf16[64,2048]{1,0:T(8,128)(2,1)S(1)}, bf16[64,2048]{1,0:T(8,128)(2,1)S(1)}, u32[]{:S(2)}, u32[]{:S(2)}) collective-permute-start(bf16[64,2048]{1,0:T(8,128)(2,1)S(1)} %pad_maximum_fusion.4), channel_id=1, source_target_pairs={{0,14},{2,0},{4,2},{6,4},{8,6},{10,8},{12,10},{14,12},{1,15},{3,1}... | collective-permute-start | bytes 786440 | tf_op jit(solution)/shard_map/ppermute | solution.py:24
  364.6 16.9 %collective-permute-start.27 = (bf16[64,2048]{1,0:T(8,128)(2,1)S(1)}, bf16[64,2048]{1,0:T(8,128)(2,1)S(1)}, u32[]{:S(2)}, u32[]{:S(2)}) collective-permute-start(bf16[64,2048]{1,0:T(8,128)(2,1)S(1)} %add_convert_fusion.3), channel_id=1, source_target_pairs={{0,2},{2,4},{4,6},{6,8},{8,10},{10,12},{12,14},{14,0},{1,3},{3,5},... | collective-permute-start | bytes 786440 | tf_op jit(solution)/shard_map/ppermute | solution.py:24
  380.4 10.5 %copy-start.17 = (bf16[64,2048]{1,0:T(8,128)(2,1)S(1)}, bf16[64,2048]{1,0:T(8,128)(2,1)}, u32[]{:S(2)}) copy-start(bf16[64,2048]{1,0:T(8,128)(2,1)} %get-tuple-element.75) | copy-start | bytes 786436
  380.4 19.0 %copy-start.13 = (bf16[64,2048]{1,0:T(8,128)(2,1)S(1)}, bf16[64,2048]{1,0:T(8,128)(2,1)}, u32[]{:S(2)}) copy-start(bf16[64,2048]{1,0:T(8,128)(2,1)} %get-tuple-element.68) | copy-start | bytes 786436
  381.5 9.4 %collective-permute-start.31 = (bf16[64,2048]{1,0:T(8,128)(2,1)S(1)}, bf16[64,2048]{1,0:T(8,128)(2,1)S(1)}, u32[]{:S(2)}, u32[]{:S(2)}) collective-permute-start(bf16[64,2048]{1,0:T(8,128)(2,1)S(1)} %add_convert_fusion.1), channel_id=1, source_target_pairs={{0,14},{2,0},{4,2},{6,4},{8,6},{10,8},{12,10},{14,12},{1,15},{3,1}... | collective-permute-start | bytes 786440 | tf_op jit(solution)/shard_map/ppermute | solution.py:24
  382.6 8.6 %collective-permute-start.28 = (bf16[64,2048]{1,0:T(8,128)(2,1)S(1)}, bf16[64,2048]{1,0:T(8,128)(2,1)S(1)}, u32[]{:S(2)}, u32[]{:S(2)}) collective-permute-start(bf16[64,2048]{1,0:T(8,128)(2,1)S(1)} %add_convert_fusion.2), channel_id=1, source_target_pairs={{0,2},{2,4},{4,6},{6,8},{8,10},{10,12},{12,14},{14,0},{1,3},{3,5},... | collective-permute-start | bytes 786440 | tf_op jit(solution)/shard_map/ppermute | solution.py:24
  390.9 8.5 %collective-permute-start.32 = (bf16[64,2048]{1,0:T(8,128)(2,1)S(1)}, bf16[64,2048]{1,0:T(8,128)(2,1)S(1)}, u32[]{:S(2)}, u32[]{:S(2)}) collective-permute-start(bf16[64,2048]{1,0:T(8,128)(2,1)S(1)} %add_convert_fusion), channel_id=1, source_target_pairs={{0,14},{2,0},{4,2},{6,4},{8,6},{10,8},{12,10},{14,12},{1,15},{3,1}... | collective-permute-start | bytes 786440 | tf_op jit(solution)/shard_map/ppermute | solution.py:24
  (6 other events, 5.5 us)

commit v3 on v2

--- a/solution.py
+++ b/solution.py
@@ -41,19 +41,6 @@
 
 def add(part, arrived):
     return (part.astype(jnp.float32) + arrived.astype(jnp.float32)).astype(jnp.bfloat16)
-
-
-def sum_ring(parts):
-    first, last = parts[4]
-    half = first.shape[0]
-    up, down = step_ring(first, 1), step_ring(last, -1)
-    up = jnp.concatenate((add(parts[3][:half], up), parts[3][half:]), axis=0)
-    down = jnp.concatenate((parts[-3][:half], add(parts[-3][half:], down)), axis=0)
-    for distance in (2, 1):
-        up = add(parts[distance], step_ring(up, 1))
-        down = add(parts[-distance], step_ring(down, -1))
-    up, down = step_ring(up, 1), step_ring(down, -1)
-    return sum(part.astype(jnp.float32) for part in (parts[0], up, down))
 
 
 def exchange(rows):
@@ -141,21 +128,24 @@
     return jnp.dot(picking, tokens, preferred_element_type=jnp.float32).astype(jnp.bfloat16)
 
 
-def combine_kernel(weighing, rows, *outs):
-    total = jnp.dot(
-        jnp.transpose(weighing[...]), rows[...], preferred_element_type=jnp.float32
-    ).astype(jnp.bfloat16)
+def combine_kernel(added, weighing, rows, *refs):
+    arrived, outs = refs[: len(added)], refs[len(added) :]
+    total = jnp.dot(jnp.transpose(weighing[...]), rows[...], preferred_element_type=jnp.float32)
     at = 0
-    for out in outs:
-        out[...] = total[at : at + out.shape[0], :]
+    for i, out in enumerate(outs):
+        piece = total[at : at + out.shape[0], :]
+        if i in added:
+            piece = piece + arrived[added.index(i)][...].astype(jnp.float32)
+        out[...] = piece.astype(jnp.bfloat16)
         at += out.shape[0]
 
 
-def combine(weighing, rows, heights):
+def combine(weighing, rows, heights, arrived=None):
+    arrived = arrived or {}
     whole = pl.BlockSpec(memory_space=pltpu.VMEM)
     return pl.pallas_call(
-        combine_kernel,
-        in_specs=[whole] * 2,
+        functools.partial(combine_kernel, tuple(arrived)),
+        in_specs=[whole] * (2 + len(arrived)),
         out_specs=[whole] * len(heights),
         out_shape=[pltpu.HBM((height, rows.shape[1]), jnp.bfloat16) for height in heights],
         cost_estimate=pl.CostEstimate(
@@ -164,7 +154,7 @@
             transcendentals=0,
         ),
         compiler_params=pltpu.CompilerParams(vmem_limit_bytes=24 * 1024 * 1024),
-    )(weighing, rows)
+    )(weighing, rows, *arrived.values())
 
 
 def start_kernel(forward, edge, stored, gain, info, out):
@@ -318,12 +308,17 @@
     far_back = exchange(far)
     far_back, near = after(far_back, near)
     near_back = exchange(near)
-    parts = dict(zip(CHUNKS[0], combine(weighings[0], near_back, [TOKENS] * len(CHUNKS[0]))))
-    *rest, first, last = combine(
-        weighings[1], far_back, [TOKENS] * (len(CHUNKS[1]) - 1) + [TOKENS // 2] * 2
-    )
-    parts.update(zip(CHUNKS[1], (*rest, (first, last))))
-    return sum_ring(parts) / code_sum
+    half = TOKENS // 2
+    up_2, down_3, up_3, first, last = combine(weighings[1], far_back, [TOKENS] * 3 + [half] * 2)
+    up, down = step_ring(first, 1), step_ring(last, -1)
+    up = jnp.concatenate((add(up_3[:half], up), up_3[half:]), axis=0)
+    down = jnp.concatenate((down_3[:half], add(down_3[half:], down)), axis=0)
+    up = step_ring(add(up_2, step_ring(up, 1)), 1)
+    down = step_ring(down, -1)
+    own, down_1, up, down = combine(weighings[0], near_back, [TOKENS] * 4, {2: up, 3: down})
+    up = step_ring(up, 1)
+    down = step_ring(add(down_1, step_ring(down, -1)), -1)
+    return sum(part.astype(jnp.float32) for part in (own, up, down)) / code_sum
 
 
 def body(boundary, saved, norm_gain, gate_weight, up_weight, down_weight, routes, gate_codes):

time: 409 us -> 413 us (level)
    ppermute x32, waiting for transfers between devices: 102 us -> 117 us  [step_ring(): lax.ppermute(block, RING, [(i, (i + step) % count) for i in range(count)])]
    all_to_all x7, waiting for transfers between devices: 82.7 us -> 69.9 us  [exchange(): lax.all_to_all(parts, PLANE, split_axis=0, concat_axis=0, tiled=True)]
  transfers between devices with their start and end apart: 40 -> 40, of which waited for: 26 -> 27; matrix products, arithmetic and copies ran while one was open for 3% -> 3% of each run, Pallas kernels for 8% -> 7%
where the time goes in v3:
time: 413 us; the launch traced here: 405 us
  waiting for transfers between devices  191 us (46%)
  starting transfers between devices  87.1 us (21%)
  Pallas kernels  58 us (14%)
  blocking collectives  44.9 us (11%)
  local copies, waits for them, and re-layouts  11.1 us (3%)
  other arithmetic  7.98 us (2%)
    ppermute x32, waiting for transfers between devices, step_ring(): lax.ppermute(block, RING, [(i, (i + step) % count) for i in range(count)])  117 us
    all_to_all x7, waiting for transfers between devices, exchange(): lax.all_to_all(parts, PLANE, split_axis=0, concat_axis=0, tiled=True)  69.9 us
    ppermute x32, starting transfers between devices, step_ring(): lax.ppermute(block, RING, [(i, (i + step) % count) for i in range(count)])  52.5 us
    all_to_all x1, blocking collectives, exchange(): lax.all_to_all(parts, PLANE, split_axis=0, concat_axis=0, tiled=True)  44.9 us
    pallas_call x4, Pallas kernels, apply_expert(): pl.pallas_call(functools.partial(expert_kernel, first_at, second_at, forw...  41.3 us
    all_to_all x7, starting transfers between devices, exchange(): lax.all_to_all(parts, PLANE, split_axis=0, concat_axis=0, tiled=True)  30.9 us
    pallas_call x2, Pallas kernels, pick_both(): pl.pallas_call(functools.partial(pick_kernel, top, ring, peers), in_specs...  9.03 us
  transfers between devices with their start and end apart: 40, of which 27 were waited for; matrix products, arithmetic and copies ran while one was open for 3% of the time, Pallas kernels for 7%

profile of v3, /device:TPU:96, one launch (start us, length us, event | category | flops | bytes accessed | tf_op | source)
XLA Modules:
  0.0 404.9 jit_solution(6922892691510718786)
XLA Ops:
  5.6 3.1 collective-permute-start
  8.7 11.8 %collective-permute-done.refs_1_ = bf16[64,4224]{1,0:T(8,128)(2,1)S(1)} collective-permute-done((bf16[64,4224]{1,0:T(8,128)(2,1)}, bf16[64,4224]{1,0:T(8,128)(2,1)S(1)}, u32[]{:S(2)}, u32[]{:S(2)}) %collective-permute-start) | collective-permute-done | bytes 540704 | tf_op jit(solution)/shard_map/ppermute | solution.py:24
  20.6 3.6 collective-permute-start.2
  24.3 10.6 %collective-permute-done.2.refs_3_ = bf16[64,4224]{1,0:T(8,128)(2,1)S(1)} collective-permute-done((bf16[64,4224]{1,0:T(8,128)(2,1)S(1)}, bf16[64,4224]{1,0:T(8,128)(2,1)S(1)}, u32[]{:S(2)}, u32[]{:S(2)}) %collective-permute-start.2) | collective-permute-done | bytes 540704 | tf_op jit(solution)/shard_map/ppermute | solution.py:24
  35.6 4.5 %shard_map.83 = (bf16[384,4096]{1,0:T(8,128)(2,1)}, bf16[384,256]{1,0:T(8,128)(2,1)}, bf16[384,256]{1,0:T(8,128)(2,1)}, bf16[384,256]{1,0:T(8,128)(2,1)}) custom-call(s32[2]{0:T(128)S(1)} %pad_add_fusion.told, bf16[64,4224]{1,0:T(8,128)(2,1)} %shard_map.82.refs_0_, bf16[64,4224]{1,0:T(8,128)(2,1)} %copy-done.25, bf16[64,4224]{1,0:T(8,128)(2,1)} %copy-done.26, ...), custom_call_target="tpu_custom_call" | custom-call | flops 805306368 | bytes 5832704 | tf_op jit(solution)/shard_map/pallas_call | solution.py:112
  40.9 7.0 %all-to-all-start = ((bf16[16,24,4096]{2,1,0:T(8,128)(2,1)}), bf16[16,24,4096]{2,1,0:T(8,128)(2,1)S(1)}, u32[]{:S(2)}, u32[]{:S(2)}) async-start(bf16[16,24,4096]{2,1,0:T(8,128)(2,1)} %bitcast.64), calls=%async_computation | async-start | bytes 6291456 | tf_op jit(solution)/shard_map/all_to_all | solution.py:49
  48.0 3.8 collective-permute-start.4
  51.7 12.3 %collective-permute-done.4.refs_1_ = bf16[64,4224]{1,0:T(8,128)(2,1)S(1)} collective-permute-done((bf16[64,4224]{1,0:T(8,128)(2,1)}, bf16[64,4224]{1,0:T(8,128)(2,1)S(1)}, u32[]{:S(2)}, u32[]{:S(2)}) %collective-permute-start.4) | collective-permute-done | bytes 540704 | tf_op jit(solution)/shard_map/ppermute | solution.py:24
  64.1 3.7 collective-permute-start.6
  67.9 5.3 %collective-permute-done.6 = bf16[32,4224]{1,0:T(8,128)(2,1)S(1)} collective-permute-done((bf16[32,4224]{1,0:T(8,128)(2,1)S(1)}, bf16[32,4224]{1,0:T(8,128)(2,1)S(1)}, u32[]{:S(2)}, u32[]{:S(2)}) %collective-permute-start.6) | collective-permute-done | bytes 270368 | tf_op jit(solution)/shard_map/ppermute | solution.py:24
  73.2 3.5 collective-permute-done.7
  77.6 4.6 %shard_map.84 = (bf16[384,4096]{1,0:T(8,128)(2,1)}, bf16[384,256]{1,0:T(8,128)(2,1)}, bf16[384,256]{1,0:T(8,128)(2,1)}, bf16[384,256]{1,0:T(8,128)(2,1)}) custom-call(s32[2]{0:T(128)S(1)} %pad_add_fusion.told, bf16[64,4224]{1,0:T(8,128)(2,1)} %copy-done.23, bf16[64,4224]{1,0:T(8,128)(2,1)} %copy-done.21, bf16[64,4224]{1,0:T(8,128)(2,1)} %copy-done.22, ...), custom_call_target="tpu_custom_call" | custom-call | flops 805306368 | bytes 5832704 | tf_op jit(solution)/shard_map/pallas_call | solution.py:112
  82.1 6.4 %all-to-all-done = bf16[16,24,4096]{2,1,0:T(8,128)(2,1)S(1)} async-done(((bf16[16,24,4096]{2,1,0:T(8,128)(2,1)}), bf16[16,24,4096]{2,1,0:T(8,128)(2,1)S(1)}, u32[]{:S(2)}, u32[]{:S(2)}) %all-to-all-start) | async-done | bytes 3145760 | tf_op jit(solution)/shard_map/all_to_all | solution.py:49
  88.5 44.9 %all_to_all.40 = bf16[16,24,4096]{2,1,0:T(8,128)(2,1)} all-to-all(bf16[16,24,4096]{2,1,0:T(8,128)(2,1)} %bitcast.65), channel_id=1, replica_groups=mesh['segment'=2,'expert_0'=4,'expert_1'=2,'expert_2'=8,'expert_3'=2] {'..., dimensions={0} | all-to-all | bytes 6291456 | tf_op jit(solution)/shard_map/all_to_all | solution.py:49
  133.5 8.9 %shard_map.85 = bf16[384,2048]{1,0:T(8,128)(2,1)} custom-call(s32[1]{0:T(128)} %bitcast.3.forward.flag, bf16[384,4096]{1,0:T(8,128)(2,1)} %bitcast.61, bf16[384,4096]{1,0:T(8,128)(2,1)} %bitcast.62, bf16[2048,768]{1,0:T(8,128)(2,1)} %bitcast.71, bf16[2048,768]{1,0:T(8,128)(2,1)} %bitcast.75, bf16[768,2048]{1,0:T(8,128)(2,1)} %bitcast.79), custom_call_target="tpu_custom_call" | custom-call | flops 6039797760 | bytes 14155776 | tf_op jit(solution)/shard_map/pallas_call | solution.py:272
  142.3 3.7 all-to-all-start.2
  146.1 8.9 %shard_map.86 = bf16[384,2048]{1,0:T(8,128)(2,1)} custom-call(s32[1]{0:T(128)} %bitcast.3.forward.flag, bf16[384,4096]{1,0:T(8,128)(2,1)} %bitcast.58, bf16[384,4096]{1,0:T(8,128)(2,1)} %bitcast.59, bf16[2048,768]{1,0:T(8,128)(2,1)} %bitcast.72, bf16[2048,768]{1,0:T(8,128)(2,1)} %bitcast.76, bf16[768,2048]{1,0:T(8,128)(2,1)} %bitcast.80), custom_call_target="tpu_custom_call" | custom-call | flops 6039797760 | bytes 14155776 | tf_op jit(solution)/shard_map/pallas_call | solution.py:272
  155.0 14.8 %all-to-all-done.2 = bf16[16,24,2048]{2,1,0:T(8,128)(2,1)S(1)} async-done(((bf16[16,24,2048]{2,1,0:T(8,128)(2,1)}), bf16[16,24,2048]{2,1,0:T(8,128)(2,1)S(1)}, u32[]{:S(2)}, u32[]{:S(2)}) %all-to-all-start.2) | async-done | bytes 1572896 | tf_op jit(solution)/shard_map/all_to_all | solution.py:49
  169.7 1.6 shard_map.87
  171.4 3.7 collective-permute-start.8
  176.9 3.9 all-to-all-start.3
  180.9 3.3 collective-permute-start.9
  184.4 5.9 %collective-permute-done.9 = bf16[64,2048]{1,0:T(8,128)(2,1)S(1)} collective-permute-done((bf16[64,2048]{1,0:T(8,128)(2,1)S(1)}, bf16[64,2048]{1,0:T(8,128)(2,1)S(1)}, u32[]{:S(2)}, u32[]{:S(2)}) %collective-permute-start.9) | collective-permute-done | bytes 262176 | tf_op jit(solution)/shard_map/ppermute | solution.py:24
  190.3 3.8 collective-permute-start.10
  194.1 5.2 %collective-permute-done.10.refs_0_ = bf16[64,2048]{1,0:T(8,128)(2,1)S(1)} collective-permute-done((bf16[64,2048]{1,0:T(8,128)(2,1)S(1)}, bf16[64,2048]{1,0:T(8,128)(2,1)S(1)}, u32[]{:S(2)}, u32[]{:S(2)}) %collective-permute-start.10) | collective-permute-done | bytes 262176 | tf_op jit(solution)/shard_map/ppermute | solution.py:24
  199.3 5.2 %all-to-all-done.3 = bf16[16,24,2048]{2,1,0:T(8,128)(2,1)S(1)} async-done(((bf16[16,24,2048]{2,1,0:T(8,128)(2,1)}), bf16[16,24,2048]{2,1,0:T(8,128)(2,1)S(1)}, u32[]{:S(2)}, u32[]{:S(2)}) %all-to-all-start.3) | async-done | bytes 1572896 | tf_op jit(solution)/shard_map/all_to_all | solution.py:49
  204.4 1.6 shard_map.88
  206.1 3.4 collective-permute-start.13
  209.5 6.1 %collective-permute-done.14 = bf16[64,2048]{1,0:T(8,128)(2,1)S(1)} collective-permute-done((bf16[64,2048]{1,0:T(8,128)(2,1)}, bf16[64,2048]{1,0:T(8,128)(2,1)S(1)}, u32[]{:S(2)}, u32[]{:S(2)}) %collective-permute-start.14) | collective-permute-done | bytes 262176 | tf_op jit(solution)/shard_map/ppermute | solution.py:24
  216.8 8.3 %collective-permute-done.15 = bf16[64,2048]{1,0:T(8,128)(2,1)S(1)} collective-permute-done((bf16[64,2048]{1,0:T(8,128)(2,1)S(1)}, bf16[64,2048]{1,0:T(8,128)(2,1)S(1)}, u32[]{:S(2)}, u32[]{:S(2)}) %collective-permute-start.15) | collective-permute-done | bytes 262176 | tf_op jit(solution)/shard_map/ppermute | solution.py:24
  225.1 1.3 fusion.9
  226.9 3.6 collective-permute-start.16
  230.5 4.5 %collective-permute-done.16 = bf16[64,2048]{1,0:T(8,128)(2,1)S(1)} collective-permute-done((bf16[64,2048]{1,0:T(8,128)(2,1)S(1)}, bf16[64,2048]{1,0:T(8,128)(2,1)S(1)}, u32[]{:S(2)}, u32[]{:S(2)}) %collective-permute-start.16) | collective-permute-done | bytes 262176 | tf_op jit(solution)/shard_map/ppermute | solution.py:368
  235.6 2.0 collective-permute-start.18
  237.5 5.4 %collective-permute-done.17 = bf16[64,2048]{1,0:T(8,128)(2,1)S(1)} collective-permute-done((bf16[64,2048]{1,0:T(8,128)(2,1)S(1)}, bf16[64,2048]{1,0:T(8,128)(2,1)S(1)}, u32[]{:S(2)}, u32[]{:S(2)}) %collective-permute-start.17) | collective-permute-done | bytes 262176 | tf_op jit(solution)/shard_map/ppermute | solution.py:24
  243.2 1.8 collective-permute-start.20
  245.0 4.3 %collective-permute-done.19 = bf16[64,2048]{1,0:T(8,128)(2,1)S(1)} collective-permute-done((bf16[64,2048]{1,0:T(8,128)(2,1)S(1)}, bf16[64,2048]{1,0:T(8,128)(2,1)S(1)}, u32[]{:S(2)}, u32[]{:S(2)}) %collective-permute-start.19) | collective-permute-done | bytes 262176 | tf_op jit(solution)/shard_map/ppermute | solution.py:24
  249.3 1.8 convolution_convert_fusion.1
  251.1 4.4 %all-to-all-start.4 = ((bf16[16,24,2048]{2,1,0:T(8,128)(2,1)}), bf16[16,24,2048]{2,1,0:T(8,128)(2,1)S(1)}, u32[]{:S(2)}, u32[]{:S(2)}) async-start(bf16[16,24,2048]{2,1,0:T(8,128)(2,1)} %bitcast.68), calls=%async_computation.4 | async-start | bytes 3145728 | tf_op jit(solution)/shard_map/all_to_all | solution.py:49
  255.5 2.8 collective-permute-start.21
  258.3 6.1 %collective-permute-done.21 = bf16[64,2048]{1,0:T(8,128)(2,1)S(1)} collective-permute-done((bf16[64,2048]{1,0:T(8,128)(2,1)S(1)}, bf16[64,2048]{1,0:T(8,128)(2,1)S(1)}, u32[]{:S(2)}, u32[]{:S(2)}) %collective-permute-start.21) | collective-permute-done | bytes 262176 | tf_op jit(solution)/shard_map/ppermute | solution.py:24
  264.5 3.8 collective-permute-start.23
  268.4 2.4 collective-permute-done.23
  270.8 3.7 collective-permute-done.24
  274.5 1.8 convolution_convert_fusion
  276.3 2.9 all-to-all-done.4
  280.4 4.4 %all-to-all-start.5 = ((bf16[16,24,2048]{2,1,0:T(8,128)(2,1)}), bf16[16,24,2048]{2,1,0:T(8,128)(2,1)}, u32[]{:S(2)}, u32[]{:S(2)}) async-start(bf16[16,24,2048]{2,1,0:T(8,128)(2,1)} %bitcast.22), calls=%async_computation.5 | async-start | bytes 3145728 | tf_op jit(solution)/shard_map/all_to_all | solution.py:49
  284.8 23.7 %all-to-all-done.5 = bf16[16,24,2048]{2,1,0:T(8,128)(2,1)} async-done(((bf16[16,24,2048]{2,1,0:T(8,128)(2,1)}), bf16[16,24,2048]{2,1,0:T(8,128)(2,1)}, u32[]{:S(2)}, u32[]{:S(2)}) %all-to-all-start.5) | async-done | bytes 1572896 | tf_op jit(solution)/shard_map/all_to_all | solution.py:49
  308.5 11.8 %shard_map.89 = bf16[384,2048]{1,0:T(8,128)(2,1)} custom-call(s32[1]{0:T(128)S(6)} %sub.11.flag, bf16[384,4096]{1,0:T(8,128)(2,1)} %bitcast.63, bf16[384,2048]{1,0:T(8,128)(2,1)} %bitcast.23.second, bf16[2048,768]{1,0:T(8,128)(2,1)} %bitcast.73, bf16[2048,768]{1,0:T(8,128)(2,1)} %bitcast.77, bf16[768,2048]{1,0:T(8,128)(2,1)} %bitcast.81), custom_call_target="tpu_custom_call" | custom-call | flops 6039797760 | bytes 14155776 | tf_op jit(solution)/shard_map/pallas_call | solution.py:272
  320.3 3.7 all-to-all-start.6
  324.1 11.8 %shard_map.90 = bf16[384,2048]{1,0:T(8,128)(2,1)} custom-call(s32[1]{0:T(128)S(6)} %sub.11.flag, bf16[384,4096]{1,0:T(8,128)(2,1)} %bitcast.60, bf16[384,2048]{1,0:T(8,128)(2,1)} %bitcast.66, bf16[2048,768]{1,0:T(8,128)(2,1)} %bitcast.74, bf16[2048,768]{1,0:T(8,128)(2,1)} %bitcast.78, bf16[768,2048]{1,0:T(8,128)(2,1)} %bitcast.82), custom_call_target="tpu_custom_call" | custom-call | flops 6039797760 | bytes 14155776 | tf_op jit(solution)/shard_map/pallas_call | solution.py:272
  335.9 11.8 %all-to-all-done.6 = bf16[16,24,2048]{2,1,0:T(8,128)(2,1)S(1)} async-done(((bf16[16,24,2048]{2,1,0:T(8,128)(2,1)}), bf16[16,24,2048]{2,1,0:T(8,128)(2,1)S(1)}, u32[]{:S(2)}, u32[]{:S(2)}) %all-to-all-start.6) | async-done | bytes 1572896 | tf_op jit(solution)/shard_map/all_to_all | solution.py:49
  347.7 1.6 shard_map.91
  349.4 2.7 collective-permute-start.25
  353.9 3.9 all-to-all-start.7
  357.9 3.3 collective-permute-start.26
  361.4 5.9 %collective-permute-done.26 = bf16[64,2048]{1,0:T(8,128)(2,1)S(1)} collective-permute-done((bf16[64,2048]{1,0:T(8,128)(2,1)S(1)}, bf16[64,2048]{1,0:T(8,128)(2,1)S(1)}, u32[]{:S(2)}, u32[]{:S(2)}) %collective-permute-start.26) | collective-permute-done | bytes 262176 | tf_op jit(solution)/shard_map/ppermute | solution.py:24
  367.3 3.8 collective-permute-start.27
  371.1 5.2 %collective-permute-done.27.refs_0_ = bf16[64,2048]{1,0:T(8,128)(2,1)S(1)} collective-permute-done((bf16[64,2048]{1,0:T(8,128)(2,1)S(1)}, bf16[64,2048]{1,0:T(8,128)(2,1)S(1)}, u32[]{:S(2)}, u32[]{:S(2)}) %collective-permute-start.27) | collective-permute-done | bytes 262176 | tf_op jit(solution)/shard_map/ppermute | solution.py:24
  376.3 5.2 %all-to-all-done.7 = bf16[16,24,2048]{2,1,0:T(8,128)(2,1)S(1)} async-done(((bf16[16,24,2048]{2,1,0:T(8,128)(2,1)}), bf16[16,24,2048]{2,1,0:T(8,128)(2,1)S(1)}, u32[]{:S(2)}, u32[]{:S(2)}) %all-to-all-start.7) | async-done | bytes 1572896 | tf_op jit(solution)/shard_map/all_to_all | solution.py:49
  381.4 1.6 shard_map.92
  383.1 3.2 collective-permute-start.30
  386.3 6.3 %collective-permute-done.31 = bf16[64,2048]{1,0:T(8,128)(2,1)S(1)} collective-permute-done((bf16[64,2048]{1,0:T(8,128)(2,1)}, bf16[64,2048]{1,0:T(8,128)(2,1)S(1)}, u32[]{:S(2)}, u32[]{:S(2)}) %collective-permute-start.31) | collective-permute-done | bytes 262176 | tf_op jit(solution)/shard_map/ppermute | solution.py:24
  393.7 8.4 %collective-permute-done.32 = bf16[64,2048]{1,0:T(8,128)(2,1)S(1)} collective-permute-done((bf16[64,2048]{1,0:T(8,128)(2,1)S(1)}, bf16[64,2048]{1,0:T(8,128)(2,1)S(1)}, u32[]{:S(2)}, u32[]{:S(2)}) %collective-permute-start.32) | collective-permute-done | bytes 262176 | tf_op jit(solution)/shard_map/ppermute | solution.py:24
  (132 shorter events, 19.8 us)
Async XLA Ops:
  1.9 1.0 copy-start
  5.6 15.0 %collective-permute-start = (bf16[64,4224]{1,0:T(8,128)(2,1)}, bf16[64,4224]{1,0:T(8,128)(2,1)S(1)}, u32[]{:S(2)}, u32[]{:S(2)}) collective-permute-start(bf16[64,4224]{1,0:T(8,128)(2,1)} %shard_map.82.refs_0_), channel_id=1, source_target_pairs={{0,2},{2,4},{4,6},{6,8},{8,10},{10,12},{12,14},{14,0},{1,3},{3,5},... | collective-permute-start | bytes 1622024 | tf_op jit(solution)/shard_map/ppermute | solution.py:24
  8.7 15.4 %collective-permute-start.1 = (bf16[64,4224]{1,0:T(8,128)(2,1)}, bf16[64,4224]{1,0:T(8,128)(2,1)S(1)}, u32[]{:S(2)}, u32[]{:S(2)}) collective-permute-start(bf16[64,4224]{1,0:T(8,128)(2,1)} %shard_map.82.refs_0_), channel_id=1, source_target_pairs={{0,14},{2,0},{4,2},{6,4},{8,6},{10,8},{12,10},{14,12},{1,15},{3,1}... | collective-permute-start | bytes 1622024 | tf_op jit(solution)/shard_map/ppermute | solution.py:24
  20.6 14.3 %copy-start.25 = (bf16[64,4224]{1,0:T(8,128)(2,1)}, bf16[64,4224]{1,0:T(8,128)(2,1)S(1)}, u32[]{:S(2)}) copy-start(bf16[64,4224]{1,0:T(8,128)(2,1)S(1)} %collective-permute-done.refs_1_) | copy-start | bytes 1622020
  20.6 14.2 %collective-permute-start.2 = (bf16[64,4224]{1,0:T(8,128)(2,1)S(1)}, bf16[64,4224]{1,0:T(8,128)(2,1)S(1)}, u32[]{:S(2)}, u32[]{:S(2)}) collective-permute-start(bf16[64,4224]{1,0:T(8,128)(2,1)S(1)} %collective-permute-done.refs_1_), channel_id=1, source_target_pairs={{0,2},{2,4},{4,6},{6,8},{8,10},{10,12},{12,14},{14,0},{1,3},{3,5},... | collective-permute-start | bytes 1622024 | tf_op jit(solution)/shard_map/ppermute | solution.py:24
  24.2 10.7 %copy-start.26 = (bf16[64,4224]{1,0:T(8,128)(2,1)}, bf16[64,4224]{1,0:T(8,128)(2,1)S(1)}, u32[]{:S(2)}) copy-start(bf16[64,4224]{1,0:T(8,128)(2,1)S(1)} %collective-permute-done.1.refs_2_) | copy-start | bytes 1622020
  24.2 16.0 %collective-permute-start.3 = (bf16[64,4224]{1,0:T(8,128)(2,1)S(1)}, bf16[64,4224]{1,0:T(8,128)(2,1)S(1)}, u32[]{:S(2)}, u32[]{:S(2)}) collective-permute-start(bf16[64,4224]{1,0:T(8,128)(2,1)S(1)} %collective-permute-done.1.refs_2_), channel_id=1, source_target_pairs={{0,14},{2,0},{4,2},{6,4},{8,6},{10,8},{12,10},{14,12},{1,15},{3,1}... | collective-permute-start | bytes 1622024 | tf_op jit(solution)/shard_map/ppermute | solution.py:24
  40.9 47.6 %all-to-all-start = ((bf16[16,24,4096]{2,1,0:T(8,128)(2,1)}), bf16[16,24,4096]{2,1,0:T(8,128)(2,1)S(1)}, u32[]{:S(2)}, u32[]{:S(2)}) async-start(bf16[16,24,4096]{2,1,0:T(8,128)(2,1)} %bitcast.64), calls=%async_computation | async-start | bytes 6291456 | tf_op jit(solution)/shard_map/all_to_all | solution.py:49
  48.0 16.1 %collective-permute-start.4 = (bf16[64,4224]{1,0:T(8,128)(2,1)}, bf16[64,4224]{1,0:T(8,128)(2,1)S(1)}, u32[]{:S(2)}, u32[]{:S(2)}) collective-permute-start(bf16[64,4224]{1,0:T(8,128)(2,1)} %copy-done.24), channel_id=1, source_target_pairs={{0,2},{2,4},{4,6},{6,8},{8,10},{10,12},{12,14},{14,0},{1,3},{3,5},... | collective-permute-start | bytes 1622024 | tf_op jit(solution)/shard_map/ppermute | solution.py:24
  51.7 16.0 %collective-permute-start.5 = (bf16[64,4224]{1,0:T(8,128)(2,1)}, bf16[64,4224]{1,0:T(8,128)(2,1)S(1)}, u32[]{:S(2)}, u32[]{:S(2)}) collective-permute-start(bf16[64,4224]{1,0:T(8,128)(2,1)} %copy-done.23), channel_id=1, source_target_pairs={{0,14},{2,0},{4,2},{6,4},{8,6},{10,8},{12,10},{14,12},{1,15},{3,1}... | collective-permute-start | bytes 1622024 | tf_op jit(solution)/shard_map/ppermute | solution.py:24
  64.1 13.5 %copy-start.21 = (bf16[64,4224]{1,0:T(8,128)(2,1)}, bf16[64,4224]{1,0:T(8,128)(2,1)S(1)}, u32[]{:S(2)}) copy-start(bf16[64,4224]{1,0:T(8,128)(2,1)S(1)} %collective-permute-done.4.refs_1_) | copy-start | bytes 1622020
  64.1 9.1 %collective-permute-start.6 = (bf16[32,4224]{1,0:T(8,128)(2,1)S(1)}, bf16[32,4224]{1,0:T(8,128)(2,1)S(1)}, u32[]{:S(2)}, u32[]{:S(2)}) collective-permute-start(bf16[32,4224]{1,0:T(8,128)(2,1)S(1)} %slice.68), channel_id=1, source_target_pairs={{0,2},{2,4},{4,6},{6,8},{8,10},{10,12},{12,14},{14,0},{1,3},{3,5},... | collective-permute-start | bytes 811016 | tf_op jit(solution)/shard_map/ppermute | solution.py:24
  67.8 9.8 %copy-start.22 = (bf16[64,4224]{1,0:T(8,128)(2,1)}, bf16[64,4224]{1,0:T(8,128)(2,1)S(1)}, u32[]{:S(2)}) copy-start(bf16[64,4224]{1,0:T(8,128)(2,1)S(1)} %collective-permute-done.5.refs_2_) | copy-start | bytes 1622020
  67.8 8.9 %collective-permute-start.7 = (bf16[32,4224]{1,0:T(8,128)(2,1)S(1)}, bf16[32,4224]{1,0:T(8,128)(2,1)S(1)}, u32[]{:S(2)}, u32[]{:S(2)}) collective-permute-start(bf16[32,4224]{1,0:T(8,128)(2,1)S(1)} %slice.69), channel_id=1, source_target_pairs={{0,14},{2,0},{4,2},{6,4},{8,6},{10,8},{12,10},{14,12},{1,15},{3,1}... | collective-permute-start | bytes 811016 | tf_op jit(solution)/shard_map/ppermute | solution.py:24
  88.5 44.9 %copy-start.10 = (bf16[16,24,4096]{2,1,0:T(8,128)(2,1)}, bf16[16,24,4096]{2,1,0:T(8,128)(2,1)S(1)}, u32[]{:S(2)}) copy-start(bf16[16,24,4096]{2,1,0:T(8,128)(2,1)S(1)} %all-to-all-done) | copy-start | bytes 9437188
  142.3 27.4 %all-to-all-start.2 = ((bf16[16,24,2048]{2,1,0:T(8,128)(2,1)}), bf16[16,24,2048]{2,1,0:T(8,128)(2,1)S(1)}, u32[]{:S(2)}, u32[]{:S(2)}) async-start(bf16[16,24,2048]{2,1,0:T(8,128)(2,1)} %bitcast.70), calls=%async_computation.2 | async-start | bytes 3145728 | tf_op jit(solution)/shard_map/all_to_all | solution.py:49
  146.1 23.7 %copy-start.9 = (bf16[384,256]{1,0:T(8,128)(2,1)S(1)}, bf16[384,256]{1,0:T(8,128)(2,1)}, u32[]{:S(2)}) copy-start(bf16[384,256]{1,0:T(8,128)(2,1)} %get-tuple-element.51.weighing) | copy-start | bytes 589828
  171.4 9.4 %collective-permute-start.8 = (bf16[32,2048]{1,0:T(8,128)(2,1)}, bf16[32,2048]{1,0:T(8,128)(2,1)S(1)}, u32[]{:S(2)}, u32[]{:S(2)}) collective-permute-start(bf16[32,2048]{1,0:T(8,128)(2,1)} %get-tuple-element.55), channel_id=1, source_target_pairs={{0,2},{2,4},{4,6},{6,8},{8,10},{10,12},{12,14},{14,0},{1,3},{3,5},... | collective-permute-start | bytes 393224 | tf_op jit(solution)/shard_map/ppermute | solution.py:24
  175.1 9.1 %collective-permute-start.11 = (bf16[32,2048]{1,0:T(8,128)(2,1)}, bf16[32,2048]{1,0:T(8,128)(2,1)S(1)}, u32[]{:S(2)}, u32[]{:S(2)}) collective-permute-start(bf16[32,2048]{1,0:T(8,128)(2,1)} %get-tuple-element.57), channel_id=1, source_target_pairs={{0,14},{2,0},{4,2},{6,4},{8,6},{10,8},{12,10},{14,12},{1,15},{3,1}... | collective-permute-start | bytes 393224 | tf_op jit(solution)/shard_map/ppermute | solution.py:24
  176.9 3.9 copy-start.18
  176.9 7.3 %copy-start.16 = (bf16[64,2048]{1,0:T(8,128)(2,1)S(1)}, bf16[64,2048]{1,0:T(8,128)(2,1)}, u32[]{:S(2)}) copy-start(bf16[64,2048]{1,0:T(8,128)(2,1)} %get-tuple-element.56) | copy-start | bytes 786436
  176.9 27.5 %all-to-all-start.3 = ((bf16[16,24,2048]{2,1,0:T(8,128)(2,1)}), bf16[16,24,2048]{2,1,0:T(8,128)(2,1)S(1)}, u32[]{:S(2)}, u32[]{:S(2)}) async-start(bf16[16,24,2048]{2,1,0:T(8,128)(2,1)} %bitcast.17), calls=%async_computation.3 | async-start | bytes 3145728 | tf_op jit(solution)/shard_map/all_to_all | solution.py:49
  180.8 9.4 %copy-start.14 = (bf16[64,2048]{1,0:T(8,128)(2,1)S(1)}, bf16[64,2048]{1,0:T(8,128)(2,1)}, u32[]{:S(2)}) copy-start(bf16[64,2048]{1,0:T(8,128)(2,1)} %get-tuple-element.53) | copy-start | bytes 786436
  180.8 23.6 %copy-start.8 = (bf16[384,256]{1,0:T(8,128)(2,1)S(1)}, bf16[384,256]{1,0:T(8,128)(2,1)}, u32[]{:S(2)}) copy-start(bf16[384,256]{1,0:T(8,128)(2,1)} %get-tuple-element.42.weighing) | copy-start | bytes 589828
  180.9 9.3 %collective-permute-start.9 = (bf16[64,2048]{1,0:T(8,128)(2,1)S(1)}, bf16[64,2048]{1,0:T(8,128)(2,1)S(1)}, u32[]{:S(2)}, u32[]{:S(2)}) collective-permute-start(bf16[64,2048]{1,0:T(8,128)(2,1)S(1)} %pad_maximum_fusion.1), channel_id=1, source_target_pairs={{0,2},{2,4},{4,6},{6,8},{8,10},{10,12},{12,14},{14,0},{1,3},{3,5},... | collective-permute-start | bytes 786440 | tf_op jit(solution)/shard_map/ppermute | solution.py:24
  184.3 9.8 %collective-permute-start.12 = (bf16[64,2048]{1,0:T(8,128)(2,1)S(1)}, bf16[64,2048]{1,0:T(8,128)(2,1)S(1)}, u32[]{:S(2)}, u32[]{:S(2)}) collective-permute-start(bf16[64,2048]{1,0:T(8,128)(2,1)S(1)} %pad_maximum_fusion.2), channel_id=1, source_target_pairs={{0,14},{2,0},{4,2},{6,4},{8,6},{10,8},{12,10},{14,12},{1,15},{3,1}... | collective-permute-start | bytes 786440 | tf_op jit(solution)/shard_map/ppermute | solution.py:24
  190.3 9.0 %collective-permute-start.10 = (bf16[64,2048]{1,0:T(8,128)(2,1)S(1)}, bf16[64,2048]{1,0:T(8,128)(2,1)S(1)}, u32[]{:S(2)}, u32[]{:S(2)}) collective-permute-start(bf16[64,2048]{1,0:T(8,128)(2,1)S(1)} %add_convert_fusion.3), channel_id=1, source_target_pairs={{0,2},{2,4},{4,6},{6,8},{8,10},{10,12},{12,14},{14,0},{1,3},{3,5},... | collective-permute-start | bytes 786440 | tf_op jit(solution)/shard_map/ppermute | solution.py:24
  204.4 20.7 %copy-start.1 = (bf16[1,64,2048]{2,1,0:T(8,128)(2,1)S(1)}, bf16[1,64,2048]{2,1,0:T(8,128)(2,1)}, u32[]{:S(2)}) copy-start(bf16[1,64,2048]{2,1,0:T(8,128)(2,1)} %param.9) | copy-start | bytes 786436
  204.4 20.7 %copy-start.3 = (bf16[1,64,2048]{2,1,0:T(8,128)(2,1)S(1)}, bf16[1,64,2048]{2,1,0:T(8,128)(2,1)}, u32[]{:S(2)}) copy-start(bf16[1,64,2048]{2,1,0:T(8,128)(2,1)} %param.8) | copy-start | bytes 786436
  204.4 20.7 %copy-start.5 = (f32[1,2048]{1,0:T(1,128)S(1)}, f32[1,2048]{1,0:T(1,128)}, u32[]{:S(2)}) copy-start(f32[1,2048]{1,0:T(1,128)} %gain.1) | copy-start | bytes 24580
  206.1 20.4 %copy-start.12 = (bf16[64,2048]{1,0:T(8,128)(2,1)S(1)}, bf16[64,2048]{1,0:T(8,128)(2,1)}, u32[]{:S(2)}) copy-start(bf16[64,2048]{1,0:T(8,128)(2,1)} %get-tuple-element.58) | copy-start | bytes 786436
  206.1 9.5 %collective-permute-start.14 = (bf16[64,2048]{1,0:T(8,128)(2,1)}, bf16[64,2048]{1,0:T(8,128)(2,1)S(1)}, u32[]{:S(2)}, u32[]{:S(2)}) collective-permute-start(bf16[64,2048]{1,0:T(8,128)(2,1)} %get-tuple-element.61), channel_id=1, source_target_pairs={{0,14},{2,0},{4,2},{6,4},{8,6},{10,8},{12,10},{14,12},{1,15},{3,1}... | collective-permute-start | bytes 786440 | tf_op jit(solution)/shard_map/ppermute | solution.py:24
  206.1 10.7 %collective-permute-start.13 = (bf16[64,2048]{1,0:T(8,128)(2,1)}, bf16[64,2048]{1,0:T(8,128)(2,1)S(1)}, u32[]{:S(2)}, u32[]{:S(2)}) collective-permute-start(bf16[64,2048]{1,0:T(8,128)(2,1)} %get-tuple-element.59), channel_id=1, source_target_pairs={{0,2},{2,4},{4,6},{6,8},{8,10},{10,12},{12,14},{14,0},{1,3},{3,5},... | collective-permute-start | bytes 786440 | tf_op jit(solution)/shard_map/ppermute | solution.py:24
  216.6 8.5 %collective-permute-start.15 = (bf16[64,2048]{1,0:T(8,128)(2,1)S(1)}, bf16[64,2048]{1,0:T(8,128)(2,1)S(1)}, u32[]{:S(2)}, u32[]{:S(2)}) collective-permute-start(bf16[64,2048]{1,0:T(8,128)(2,1)S(1)} %add_convert_fusion.2), channel_id=1, source_target_pairs={{0,14},{2,0},{4,2},{6,4},{8,6},{10,8},{12,10},{14,12},{1,15},{3,1}... | collective-permute-start | bytes 786440 | tf_op jit(solution)/shard_map/ppermute | solution.py:24
  226.4 22.9 %copy-start.27 = (bf16[384,256]{1,0:T(8,128)(2,1)S(1)}, bf16[384,256]{1,0:T(8,128)(2,1)}, u32[]{:S(2)}) copy-start(bf16[384,256]{1,0:T(8,128)(2,1)} %get-tuple-element.63) | copy-start | bytes 589828
  226.9 8.2 %collective-permute-start.16 = (bf16[64,2048]{1,0:T(8,128)(2,1)S(1)}, bf16[64,2048]{1,0:T(8,128)(2,1)S(1)}, u32[]{:S(2)}, u32[]{:S(2)}) collective-permute-start(bf16[64,2048]{1,0:T(8,128)(2,1)S(1)} %fusion.8), channel_id=1, source_target_pairs={{0,128},{128,0},{1,129},{129,1},{2,130},{130,2},{3,131},{131,3},{4... | collective-permute-start | bytes 786440 | tf_op jit(solution)/shard_map/ppermute | solution.py:368
  235.4 7.5 %collective-permute-start.17 = (bf16[64,2048]{1,0:T(8,128)(2,1)S(1)}, bf16[64,2048]{1,0:T(8,128)(2,1)S(1)}, u32[]{:S(2)}, u32[]{:S(2)}) collective-permute-start(bf16[64,2048]{1,0:T(8,128)(2,1)S(1)} %fusion.22), channel_id=1, source_target_pairs={{0,2},{2,4},{4,6},{6,8},{8,10},{10,12},{12,14},{14,0},{1,3},{3,5},... | collective-permute-start | bytes 786440 | tf_op jit(solution)/shard_map/ppermute | solution.py:24
  235.6 7.6 %collective-permute-start.18 = (bf16[64,2048]{1,0:T(8,128)(2,1)S(1)}, bf16[64,2048]{1,0:T(8,128)(2,1)S(1)}, u32[]{:S(2)}, u32[]{:S(2)}) collective-permute-start(bf16[64,2048]{1,0:T(8,128)(2,1)S(1)} %fusion.22), channel_id=1, source_target_pairs={{0,14},{2,0},{4,2},{6,4},{8,6},{10,8},{12,10},{14,12},{1,15},{3,1}... | collective-permute-start | bytes 786440 | tf_op jit(solution)/shard_map/ppermute | solution.py:24
  242.9 6.4 %collective-permute-start.19 = (bf16[64,2048]{1,0:T(8,128)(2,1)S(1)}, bf16[64,2048]{1,0:T(8,128)(2,1)S(1)}, u32[]{:S(2)}, u32[]{:S(2)}) collective-permute-start(bf16[64,2048]{1,0:T(8,128)(2,1)S(1)} %collective-permute-done.17), channel_id=1, source_target_pairs={{0,2},{2,4},{4,6},{6,8},{8,10},{10,12},{12,14},{14,0},{1,3},{3,5},... | collective-permute-start | bytes 786440 | tf_op jit(solution)/shard_map/ppermute | solution.py:24
  243.2 15.1 %collective-permute-start.20 = (bf16[64,2048]{1,0:T(8,128)(2,1)S(1)}, bf16[64,2048]{1,0:T(8,128)(2,1)S(1)}, u32[]{:S(2)}, u32[]{:S(2)}) collective-permute-start(bf16[64,2048]{1,0:T(8,128)(2,1)S(1)} %collective-permute-done.18), channel_id=1, source_target_pairs={{0,14},{2,0},{4,2},{6,4},{8,6},{10,8},{12,10},{14,12},{1,15},{3,1}... | collective-permute-start | bytes 786440 | tf_op jit(solution)/shard_map/ppermute | solution.py:24
  251.1 28.1 %all-to-all-start.4 = ((bf16[16,24,2048]{2,1,0:T(8,128)(2,1)}), bf16[16,24,2048]{2,1,0:T(8,128)(2,1)S(1)}, u32[]{:S(2)}, u32[]{:S(2)}) async-start(bf16[16,24,2048]{2,1,0:T(8,128)(2,1)} %bitcast.68), calls=%async_computation.4 | async-start | bytes 3145728 | tf_op jit(solution)/shard_map/all_to_all | solution.py:49
  255.5 19.0 %copy-start.20 = (bf16[384,256]{1,0:T(8,128)(2,1)S(1)}, bf16[384,256]{1,0:T(8,128)(2,1)}, u32[]{:S(2)}) copy-start(bf16[384,256]{1,0:T(8,128)(2,1)} %get-tuple-element.64) | copy-start | bytes 589828
  255.5 8.9 %collective-permute-start.21 = (bf16[64,2048]{1,0:T(8,128)(2,1)S(1)}, bf16[64,2048]{1,0:T(8,128)(2,1)S(1)}, u32[]{:S(2)}, u32[]{:S(2)}) collective-permute-start(bf16[64,2048]{1,0:T(8,128)(2,1)S(1)} %collective-permute-done.19), channel_id=1, source_target_pairs={{0,2},{2,4},{4,6},{6,8},{8,10},{10,12},{12,14},{14,0},{1,3},{3,5},... | collective-permute-start | bytes 786440 | tf_op jit(solution)/shard_map/ppermute | solution.py:24
  258.3 9.9 %collective-permute-start.22 = (bf16[64,2048]{1,0:T(8,128)(2,1)S(1)}, bf16[64,2048]{1,0:T(8,128)(2,1)S(1)}, u32[]{:S(2)}, u32[]{:S(2)}) collective-permute-start(bf16[64,2048]{1,0:T(8,128)(2,1)S(1)} %collective-permute-done.20), channel_id=1, source_target_pairs={{0,14},{2,0},{4,2},{6,4},{8,6},{10,8},{12,10},{14,12},{1,15},{3,1}... | collective-permute-start | bytes 786440 | tf_op jit(solution)/shard_map/ppermute | solution.py:24
  264.5 6.3 %collective-permute-start.23 = (bf16[32,2048]{1,0:T(8,128)(2,1)S(1)}, bf16[32,2048]{1,0:T(8,128)(2,1)S(1)}, u32[]{:S(2)}, u32[]{:S(2)}) collective-permute-start(bf16[32,2048]{1,0:T(8,128)(2,1)S(1)} %slice.70), channel_id=1, source_target_pairs={{0,2},{2,4},{4,6},{6,8},{8,10},{10,12},{12,14},{14,0},{1,3},{3,5},... | collective-permute-start | bytes 393224 | tf_op jit(solution)/shard_map/ppermute | solution.py:24
  268.3 6.3 %collective-permute-start.24 = (bf16[32,2048]{1,0:T(8,128)(2,1)S(1)}, bf16[32,2048]{1,0:T(8,128)(2,1)S(1)}, u32[]{:S(2)}, u32[]{:S(2)}) collective-permute-start(bf16[32,2048]{1,0:T(8,128)(2,1)S(1)} %slice.71), channel_id=1, source_target_pairs={{0,14},{2,0},{4,2},{6,4},{8,6},{10,8},{12,10},{14,12},{1,15},{3,1}... | collective-permute-start | bytes 393224 | tf_op jit(solution)/shard_map/ppermute | solution.py:24
  279.2 1.2 copy-start.11
  280.4 28.1 %all-to-all-start.5 = ((bf16[16,24,2048]{2,1,0:T(8,128)(2,1)}), bf16[16,24,2048]{2,1,0:T(8,128)(2,1)}, u32[]{:S(2)}, u32[]{:S(2)}) async-start(bf16[16,24,2048]{2,1,0:T(8,128)(2,1)} %bitcast.22), calls=%async_computation.5 | async-start | bytes 3145728 | tf_op jit(solution)/shard_map/all_to_all | solution.py:49
  320.3 27.4 %all-to-all-start.6 = ((bf16[16,24,2048]{2,1,0:T(8,128)(2,1)}), bf16[16,24,2048]{2,1,0:T(8,128)(2,1)S(1)}, u32[]{:S(2)}, u32[]{:S(2)}) async-start(bf16[16,24,2048]{2,1,0:T(8,128)(2,1)} %bitcast.69), calls=%async_computation.6 | async-start | bytes 3145728 | tf_op jit(solution)/shard_map/all_to_all | solution.py:49
  324.1 23.7 %copy-start.7 = (bf16[384,256]{1,0:T(8,128)(2,1)S(1)}, bf16[384,256]{1,0:T(8,128)(2,1)}, u32[]{:S(2)}) copy-start(bf16[384,256]{1,0:T(8,128)(2,1)} %get-tuple-element.68.weighing) | copy-start | bytes 589828
  349.4 8.4 %collective-permute-start.25 = (bf16[32,2048]{1,0:T(8,128)(2,1)}, bf16[32,2048]{1,0:T(8,128)(2,1)S(1)}, u32[]{:S(2)}, u32[]{:S(2)}) collective-permute-start(bf16[32,2048]{1,0:T(8,128)(2,1)} %get-tuple-element.72), channel_id=1, source_target_pairs={{0,2},{2,4},{4,6},{6,8},{8,10},{10,12},{12,14},{14,0},{1,3},{3,5},... | collective-permute-start | bytes 393224 | tf_op jit(solution)/shard_map/ppermute | solution.py:24
  352.1 9.1 %collective-permute-start.28 = (bf16[32,2048]{1,0:T(8,128)(2,1)}, bf16[32,2048]{1,0:T(8,128)(2,1)S(1)}, u32[]{:S(2)}, u32[]{:S(2)}) collective-permute-start(bf16[32,2048]{1,0:T(8,128)(2,1)} %get-tuple-element.74), channel_id=1, source_target_pairs={{0,14},{2,0},{4,2},{6,4},{8,6},{10,8},{12,10},{14,12},{1,15},{3,1}... | collective-permute-start | bytes 393224 | tf_op jit(solution)/shard_map/ppermute | solution.py:24
  353.9 3.9 copy-start.19
  353.9 7.3 %copy-start.17 = (bf16[64,2048]{1,0:T(8,128)(2,1)S(1)}, bf16[64,2048]{1,0:T(8,128)(2,1)}, u32[]{:S(2)}) copy-start(bf16[64,2048]{1,0:T(8,128)(2,1)} %get-tuple-element.73) | copy-start | bytes 786436
  353.9 27.5 %all-to-all-start.7 = ((bf16[16,24,2048]{2,1,0:T(8,128)(2,1)}), bf16[16,24,2048]{2,1,0:T(8,128)(2,1)S(1)}, u32[]{:S(2)}, u32[]{:S(2)}) async-start(bf16[16,24,2048]{2,1,0:T(8,128)(2,1)} %bitcast.67), calls=%async_computation.7 | async-start | bytes 3145728 | tf_op jit(solution)/shard_map/all_to_all | solution.py:49
  357.8 9.4 %copy-start.15 = (bf16[64,2048]{1,0:T(8,128)(2,1)S(1)}, bf16[64,2048]{1,0:T(8,128)(2,1)}, u32[]{:S(2)}) copy-start(bf16[64,2048]{1,0:T(8,128)(2,1)} %get-tuple-element.70) | copy-start | bytes 786436
  357.8 23.6 %copy-start.6 = (bf16[384,256]{1,0:T(8,128)(2,1)S(1)}, bf16[384,256]{1,0:T(8,128)(2,1)}, u32[]{:S(2)}) copy-start(bf16[384,256]{1,0:T(8,128)(2,1)} %get-tuple-element.62.weighing) | copy-start | bytes 589828
  357.9 9.3 %collective-permute-start.26 = (bf16[64,2048]{1,0:T(8,128)(2,1)S(1)}, bf16[64,2048]{1,0:T(8,128)(2,1)S(1)}, u32[]{:S(2)}, u32[]{:S(2)}) collective-permute-start(bf16[64,2048]{1,0:T(8,128)(2,1)S(1)} %pad_maximum_fusion.3), channel_id=1, source_target_pairs={{0,2},{2,4},{4,6},{6,8},{8,10},{10,12},{12,14},{14,0},{1,3},{3,5},... | collective-permute-start | bytes 786440 | tf_op jit(solution)/shard_map/ppermute | solution.py:24
  361.3 9.8 %collective-permute-start.29 = (bf16[64,2048]{1,0:T(8,128)(2,1)S(1)}, bf16[64,2048]{1,0:T(8,128)(2,1)S(1)}, u32[]{:S(2)}, u32[]{:S(2)}) collective-permute-start(bf16[64,2048]{1,0:T(8,128)(2,1)S(1)} %pad_maximum_fusion.4), channel_id=1, source_target_pairs={{0,14},{2,0},{4,2},{6,4},{8,6},{10,8},{12,10},{14,12},{1,15},{3,1}... | collective-permute-start | bytes 786440 | tf_op jit(solution)/shard_map/ppermute | solution.py:24
  367.3 9.0 %collective-permute-start.27 = (bf16[64,2048]{1,0:T(8,128)(2,1)S(1)}, bf16[64,2048]{1,0:T(8,128)(2,1)S(1)}, u32[]{:S(2)}, u32[]{:S(2)}) collective-permute-start(bf16[64,2048]{1,0:T(8,128)(2,1)S(1)} %add_convert_fusion.1), channel_id=1, source_target_pairs={{0,2},{2,4},{4,6},{6,8},{8,10},{10,12},{12,14},{14,0},{1,3},{3,5},... | collective-permute-start | bytes 786440 | tf_op jit(solution)/shard_map/ppermute | solution.py:24
  383.1 20.3 %copy-start.13 = (bf16[64,2048]{1,0:T(8,128)(2,1)S(1)}, bf16[64,2048]{1,0:T(8,128)(2,1)}, u32[]{:S(2)}) copy-start(bf16[64,2048]{1,0:T(8,128)(2,1)} %get-tuple-element.75) | copy-start | bytes 786436
  383.1 9.5 %collective-permute-start.31 = (bf16[64,2048]{1,0:T(8,128)(2,1)}, bf16[64,2048]{1,0:T(8,128)(2,1)S(1)}, u32[]{:S(2)}, u32[]{:S(2)}) collective-permute-start(bf16[64,2048]{1,0:T(8,128)(2,1)} %get-tuple-element.78), channel_id=1, source_target_pairs={{0,14},{2,0},{4,2},{6,4},{8,6},{10,8},{12,10},{14,12},{1,15},{3,1}... | collective-permute-start | bytes 786440 | tf_op jit(solution)/shard_map/ppermute | solution.py:24
  383.1 10.6 %collective-permute-start.30 = (bf16[64,2048]{1,0:T(8,128)(2,1)}, bf16[64,2048]{1,0:T(8,128)(2,1)S(1)}, u32[]{:S(2)}, u32[]{:S(2)}) collective-permute-start(bf16[64,2048]{1,0:T(8,128)(2,1)} %get-tuple-element.76), channel_id=1, source_target_pairs={{0,2},{2,4},{4,6},{6,8},{8,10},{10,12},{12,14},{14,0},{1,3},{3,5},... | collective-permute-start | bytes 786440 | tf_op jit(solution)/shard_map/ppermute | solution.py:24
  393.6 8.5 %collective-permute-start.32 = (bf16[64,2048]{1,0:T(8,128)(2,1)S(1)}, bf16[64,2048]{1,0:T(8,128)(2,1)S(1)}, u32[]{:S(2)}, u32[]{:S(2)}) collective-permute-start(bf16[64,2048]{1,0:T(8,128)(2,1)S(1)} %add_convert_fusion), channel_id=1, source_target_pairs={{0,14},{2,0},{4,2},{6,4},{8,6},{10,8},{12,10},{14,12},{1,15},{3,1}... | collective-permute-start | bytes 786440 | tf_op jit(solution)/shard_map/ppermute | solution.py:24
  (4 other events, 3.2 us)

commit v4 on v2

--- a/solution.py
+++ b/solution.py
@@ -190,6 +190,7 @@
 def starting_block(forward, edge, stored, gain, info):
     whole = pl.BlockSpec(memory_space=pltpu.VMEM)
     tokens, width = edge.shape
+    edge, stored = (pltpu.with_memory_space_constraint(rows, pltpu.HBM) for rows in (edge, stored))
     return pl.pallas_call(
         start_kernel,
         in_specs=[pl.BlockSpec(memory_space=pltpu.SMEM)] + [whole] * 4,
@@ -226,11 +227,11 @@
     copies = [
         pltpu.make_async_copy(source, target, done.at[i]) for i, (source, target) in enumerate(into)
     ]
-    for copy in copies[:3]:
+    for copy in (copies[0], copies[2]):
         copy.start()
-    for copy in copies[:3]:
+    for copy in (copies[0], copies[2]):
         copy.wait()
-    for copy in copies[3:]:
+    for copy in (copies[1], *copies[3:]):
         copy.start()
     forward = flag[0] == 1
     piece = width // 4
@@ -241,6 +242,7 @@
 
     @pl.when(forward)
     def _():
+        copies[1].wait()
         taken = (first_rows, second_rows)[forward_from][...]
         gate_part = jnp.dot(taken, gate[...], preferred_element_type=jnp.float32)
         copies[3].wait()
@@ -259,6 +261,7 @@
         gate_part = jnp.dot(taken, gate[...], preferred_element_type=jnp.float32)
         copies[3].wait()
         up_part = jnp.dot(taken, up[...], preferred_element_type=jnp.float32)
+        copies[1].wait()
         copies[4].wait()
         hidden_grad = transposed(second_rows[...], down[...])
         sigmoid_part = jax.nn.sigmoid(gate_part)

time: 409 us -> 408 us (level)
  no operation moved by 1% of the time
where the time goes in v4:
time: 408 us; the launch traced here: 400 us
  waiting for transfers between devices  188 us (46%)
  starting transfers between devices  86.3 us (21%)
  Pallas kernels  60.6 us (15%)
  blocking collectives  44.9 us (11%)
  other arithmetic  8.43 us (2%)
  local copies, waits for them, and re-layouts  7.36 us (2%)
    ppermute x32, waiting for transfers between devices, step_ring(): lax.ppermute(block, RING, [(i, (i + step) % count) for i in range(count)])  102 us
    all_to_all x7, waiting for transfers between devices, exchange(): lax.all_to_all(parts, PLANE, split_axis=0, concat_axis=0, tiled=True)  81.9 us
    ppermute x32, starting transfers between devices, step_ring(): lax.ppermute(block, RING, [(i, (i + step) % count) for i in range(count)])  52.5 us
    all_to_all x1, blocking collectives, exchange(): lax.all_to_all(parts, PLANE, split_axis=0, concat_axis=0, tiled=True)  44.9 us
    pallas_call x4, Pallas kernels, apply_expert(): pl.pallas_call(functools.partial(expert_kernel, first_at, second_at, forw...  42.9 us
    all_to_all x7, starting transfers between devices, exchange(): lax.all_to_all(parts, PLANE, split_axis=0, concat_axis=0, tiled=True)  30.9 us
    pallas_call x2, Pallas kernels, pick_both(): pl.pallas_call(functools.partial(pick_kernel, top, ring, peers), in_specs...  9.04 us
  transfers between devices with their start and end apart: 40, of which 26 were waited for; matrix products, arithmetic and copies ran while one was open for 3% of the time, Pallas kernels for 8%

profile of v4, /device:TPU:96, one launch (start us, length us, event | category | flops | bytes accessed | tf_op | source)
XLA Modules:
  0.0 400.3 jit_solution(16599469455727303431)
XLA Ops:
  2.6 2.2 shard_map.82.refs_0_
  4.7 3.1 collective-permute-start
  7.9 11.8 %collective-permute-done.refs_1_ = bf16[64,4224]{1,0:T(8,128)(2,1)S(1)} collective-permute-done((bf16[64,4224]{1,0:T(8,128)(2,1)}, bf16[64,4224]{1,0:T(8,128)(2,1)S(1)}, u32[]{:S(2)}, u32[]{:S(2)}) %collective-permute-start) | collective-permute-done | bytes 540704 | tf_op jit(solution)/shard_map/ppermute | solution.py:24
  19.7 3.6 collective-permute-start.2
  23.4 10.6 %collective-permute-done.2.refs_3_ = bf16[64,4224]{1,0:T(8,128)(2,1)S(1)} collective-permute-done((bf16[64,4224]{1,0:T(8,128)(2,1)S(1)}, bf16[64,4224]{1,0:T(8,128)(2,1)S(1)}, u32[]{:S(2)}, u32[]{:S(2)}) %collective-permute-start.2) | collective-permute-done | bytes 540704 | tf_op jit(solution)/shard_map/ppermute | solution.py:24
  34.8 4.5 %shard_map.83 = (bf16[384,4096]{1,0:T(8,128)(2,1)}, bf16[384,256]{1,0:T(8,128)(2,1)}, bf16[384,256]{1,0:T(8,128)(2,1)}, bf16[384,256]{1,0:T(8,128)(2,1)}) custom-call(s32[2]{0:T(128)S(1)} %pad_add_fusion.told, bf16[64,4224]{1,0:T(8,128)(2,1)} %shard_map.82.refs_0_, bf16[64,4224]{1,0:T(8,128)(2,1)} %copy-done.25, bf16[64,4224]{1,0:T(8,128)(2,1)} %copy-done.26, ...), custom_call_target="tpu_custom_call" | custom-call | flops 805306368 | bytes 5832704 | tf_op jit(solution)/shard_map/pallas_call | solution.py:125
  40.1 7.0 %all-to-all-start = ((bf16[16,24,4096]{2,1,0:T(8,128)(2,1)}), bf16[16,24,4096]{2,1,0:T(8,128)(2,1)S(1)}, u32[]{:S(2)}, u32[]{:S(2)}) async-start(bf16[16,24,4096]{2,1,0:T(8,128)(2,1)} %bitcast.63), calls=%async_computation | async-start | bytes 6291456 | tf_op jit(solution)/shard_map/all_to_all | solution.py:62
  47.2 3.8 collective-permute-start.4
  51.0 12.9 %collective-permute-done.5.refs_2_ = bf16[64,4224]{1,0:T(8,128)(2,1)S(1)} collective-permute-done((bf16[64,4224]{1,0:T(8,128)(2,1)}, bf16[64,4224]{1,0:T(8,128)(2,1)S(1)}, u32[]{:S(2)}, u32[]{:S(2)}) %collective-permute-start.5) | collective-permute-done | bytes 540704 | tf_op jit(solution)/shard_map/ppermute | solution.py:24
  64.0 3.3 collective-permute-start.6
  67.3 6.1 %collective-permute-done.7 = bf16[32,4224]{1,0:T(8,128)(2,1)S(1)} collective-permute-done((bf16[32,4224]{1,0:T(8,128)(2,1)S(1)}, bf16[32,4224]{1,0:T(8,128)(2,1)S(1)}, u32[]{:S(2)}, u32[]{:S(2)}) %collective-permute-start.7) | collective-permute-done | bytes 270368 | tf_op jit(solution)/shard_map/ppermute | solution.py:24
  74.2 4.6 %shard_map.84 = (bf16[384,4096]{1,0:T(8,128)(2,1)}, bf16[384,256]{1,0:T(8,128)(2,1)}, bf16[384,256]{1,0:T(8,128)(2,1)}, bf16[384,256]{1,0:T(8,128)(2,1)}) custom-call(s32[2]{0:T(128)S(1)} %pad_add_fusion.told, bf16[64,4224]{1,0:T(8,128)(2,1)} %copy-done.23, bf16[64,4224]{1,0:T(8,128)(2,1)} %copy-done.22, bf16[64,4224]{1,0:T(8,128)(2,1)} %copy-done.21, ...), custom_call_target="tpu_custom_call" | custom-call | flops 805306368 | bytes 5832704 | tf_op jit(solution)/shard_map/pallas_call | solution.py:125
  78.8 8.9 %all-to-all-done = bf16[16,24,4096]{2,1,0:T(8,128)(2,1)S(1)} async-done(((bf16[16,24,4096]{2,1,0:T(8,128)(2,1)}), bf16[16,24,4096]{2,1,0:T(8,128)(2,1)S(1)}, u32[]{:S(2)}, u32[]{:S(2)}) %all-to-all-start) | async-done | bytes 3145760 | tf_op jit(solution)/shard_map/all_to_all | solution.py:62
  87.7 44.9 %all_to_all.40 = bf16[16,24,4096]{2,1,0:T(8,128)(2,1)} all-to-all(bf16[16,24,4096]{2,1,0:T(8,128)(2,1)} %bitcast.64), channel_id=1, replica_groups=mesh['segment'=2,'expert_0'=4,'expert_1'=2,'expert_2'=8,'expert_3'=2] {'..., dimensions={0} | all-to-all | bytes 6291456 | tf_op jit(solution)/shard_map/all_to_all | solution.py:62
  132.6 9.6 %shard_map.85 = bf16[384,2048]{1,0:T(8,128)(2,1)} custom-call(s32[1]{0:T(128)} %bitcast.3.forward.flag, bf16[384,4096]{1,0:T(8,128)(2,1)} %bitcast.60, bf16[384,4096]{1,0:T(8,128)(2,1)} %bitcast.61, bf16[2048,768]{1,0:T(8,128)(2,1)} %bitcast.71, bf16[2048,768]{1,0:T(8,128)(2,1)} %bitcast.75, bf16[768,2048]{1,0:T(8,128)(2,1)} %bitcast.79), custom_call_target="tpu_custom_call" | custom-call | flops 6039797760 | bytes 14155776 | tf_op jit(solution)/shard_map/pallas_call | solution.py:285
  142.2 3.7 all-to-all-start.2
  146.0 9.7 %shard_map.86 = bf16[384,2048]{1,0:T(8,128)(2,1)} custom-call(s32[1]{0:T(128)} %bitcast.3.forward.flag, bf16[384,4096]{1,0:T(8,128)(2,1)} %bitcast.57, bf16[384,4096]{1,0:T(8,128)(2,1)} %bitcast.58, bf16[2048,768]{1,0:T(8,128)(2,1)} %bitcast.72, bf16[2048,768]{1,0:T(8,128)(2,1)} %bitcast.76, bf16[768,2048]{1,0:T(8,128)(2,1)} %bitcast.80), custom_call_target="tpu_custom_call" | custom-call | flops 6039797760 | bytes 14155776 | tf_op jit(solution)/shard_map/pallas_call | solution.py:285
  155.7 13.9 %all-to-all-done.2 = bf16[16,24,2048]{2,1,0:T(8,128)(2,1)S(1)} async-done(((bf16[16,24,2048]{2,1,0:T(8,128)(2,1)}), bf16[16,24,2048]{2,1,0:T(8,128)(2,1)S(1)}, u32[]{:S(2)}, u32[]{:S(2)}) %all-to-all-start.2) | async-done | bytes 1572896 | tf_op jit(solution)/shard_map/all_to_all | solution.py:62
  169.6 1.6 shard_map.88
  171.2 3.7 collective-permute-start.8
  175.9 3.9 all-to-all-start.3
  179.9 3.3 collective-permute-start.9
  183.3 5.9 %collective-permute-done.9 = bf16[64,2048]{1,0:T(8,128)(2,1)S(1)} collective-permute-done((bf16[64,2048]{1,0:T(8,128)(2,1)S(1)}, bf16[64,2048]{1,0:T(8,128)(2,1)S(1)}, u32[]{:S(2)}, u32[]{:S(2)}) %collective-permute-start.9) | collective-permute-done | bytes 262176 | tf_op jit(solution)/shard_map/ppermute | solution.py:24
  189.3 3.8 collective-permute-start.10
  193.0 10.3 %all-to-all-done.3 = bf16[16,24,2048]{2,1,0:T(8,128)(2,1)S(1)} async-done(((bf16[16,24,2048]{2,1,0:T(8,128)(2,1)}), bf16[16,24,2048]{2,1,0:T(8,128)(2,1)S(1)}, u32[]{:S(2)}, u32[]{:S(2)}) %all-to-all-start.3) | async-done | bytes 1572896 | tf_op jit(solution)/shard_map/all_to_all | solution.py:62
  203.4 1.6 shard_map.87
  205.1 1.1 add_convert_fusion.5
  207.3 3.5 collective-permute-start.11
  210.8 4.7 %collective-permute-done.14 = bf16[64,2048]{1,0:T(8,128)(2,1)S(1)} collective-permute-done((bf16[64,2048]{1,0:T(8,128)(2,1)S(1)}, bf16[64,2048]{1,0:T(8,128)(2,1)S(1)}, u32[]{:S(2)}, u32[]{:S(2)}) %collective-permute-start.14) | collective-permute-done | bytes 262176 | tf_op jit(solution)/shard_map/ppermute | solution.py:24
  216.1 8.0 %collective-permute-done.15 = bf16[64,2048]{1,0:T(8,128)(2,1)S(1)} collective-permute-done((bf16[64,2048]{1,0:T(8,128)(2,1)S(1)}, bf16[64,2048]{1,0:T(8,128)(2,1)S(1)}, u32[]{:S(2)}, u32[]{:S(2)}) %collective-permute-start.15) | collective-permute-done | bytes 262176 | tf_op jit(solution)/shard_map/ppermute | solution.py:24
  224.9 2.9 collective-permute-start.16
  227.8 4.5 %collective-permute-done.16 = bf16[64,2048]{1,0:T(8,128)(2,1)S(1)} collective-permute-done((bf16[64,2048]{1,0:T(8,128)(2,1)S(1)}, bf16[64,2048]{1,0:T(8,128)(2,1)S(1)}, u32[]{:S(2)}, u32[]{:S(2)}) %collective-permute-start.16) | collective-permute-done | bytes 262176 | tf_op jit(solution)/shard_map/ppermute | solution.py:376
  232.9 2.0 collective-permute-start.18
  234.9 5.4 %collective-permute-done.17 = bf16[64,2048]{1,0:T(8,128)(2,1)S(1)} collective-permute-done((bf16[64,2048]{1,0:T(8,128)(2,1)S(1)}, bf16[64,2048]{1,0:T(8,128)(2,1)S(1)}, u32[]{:S(2)}, u32[]{:S(2)}) %collective-permute-start.17) | collective-permute-done | bytes 262176 | tf_op jit(solution)/shard_map/ppermute | solution.py:24
  240.5 1.8 collective-permute-start.20
  242.3 4.3 %collective-permute-done.19 = bf16[64,2048]{1,0:T(8,128)(2,1)S(1)} collective-permute-done((bf16[64,2048]{1,0:T(8,128)(2,1)S(1)}, bf16[64,2048]{1,0:T(8,128)(2,1)S(1)}, u32[]{:S(2)}, u32[]{:S(2)}) %collective-permute-start.19) | collective-permute-done | bytes 262176 | tf_op jit(solution)/shard_map/ppermute | solution.py:24
  246.6 1.8 convolution_convert_fusion.1
  248.5 4.4 %all-to-all-start.4 = ((bf16[16,24,2048]{2,1,0:T(8,128)(2,1)}), bf16[16,24,2048]{2,1,0:T(8,128)(2,1)S(1)}, u32[]{:S(2)}, u32[]{:S(2)}) async-start(bf16[16,24,2048]{2,1,0:T(8,128)(2,1)} %bitcast.68), calls=%async_computation.4 | async-start | bytes 3145728 | tf_op jit(solution)/shard_map/all_to_all | solution.py:62
  252.8 2.8 collective-permute-start.21
  255.6 6.1 %collective-permute-done.21 = bf16[64,2048]{1,0:T(8,128)(2,1)S(1)} collective-permute-done((bf16[64,2048]{1,0:T(8,128)(2,1)S(1)}, bf16[64,2048]{1,0:T(8,128)(2,1)S(1)}, u32[]{:S(2)}, u32[]{:S(2)}) %collective-permute-start.21) | collective-permute-done | bytes 262176 | tf_op jit(solution)/shard_map/ppermute | solution.py:24
  261.8 3.8 collective-permute-start.23
  265.7 2.4 collective-permute-done.23
  268.1 3.7 collective-permute-done.24
  271.8 1.8 convolution_convert_fusion
  273.6 2.9 all-to-all-done.4
  276.5 1.2 copy-done.9
  277.7 4.4 %all-to-all-start.5 = ((bf16[16,24,2048]{2,1,0:T(8,128)(2,1)}), bf16[16,24,2048]{2,1,0:T(8,128)(2,1)}, u32[]{:S(2)}, u32[]{:S(2)}) async-start(bf16[16,24,2048]{2,1,0:T(8,128)(2,1)} %bitcast.22), calls=%async_computation.5 | async-start | bytes 3145728 | tf_op jit(solution)/shard_map/all_to_all | solution.py:62
  282.2 23.7 %all-to-all-done.5 = bf16[16,24,2048]{2,1,0:T(8,128)(2,1)} async-done(((bf16[16,24,2048]{2,1,0:T(8,128)(2,1)}), bf16[16,24,2048]{2,1,0:T(8,128)(2,1)}, u32[]{:S(2)}, u32[]{:S(2)}) %all-to-all-start.5) | async-done | bytes 1572896 | tf_op jit(solution)/shard_map/all_to_all | solution.py:62
  305.9 11.8 %shard_map.89 = bf16[384,2048]{1,0:T(8,128)(2,1)} custom-call(s32[1]{0:T(128)S(6)} %sub.11.flag, bf16[384,4096]{1,0:T(8,128)(2,1)} %bitcast.62, bf16[384,2048]{1,0:T(8,128)(2,1)} %bitcast.23.second, bf16[2048,768]{1,0:T(8,128)(2,1)} %bitcast.73, bf16[2048,768]{1,0:T(8,128)(2,1)} %bitcast.77, bf16[768,2048]{1,0:T(8,128)(2,1)} %bitcast.81), custom_call_target="tpu_custom_call" | custom-call | flops 6039797760 | bytes 14155776 | tf_op jit(solution)/shard_map/pallas_call | solution.py:285
  317.6 3.7 all-to-all-start.6
  321.4 11.8 %shard_map.90 = bf16[384,2048]{1,0:T(8,128)(2,1)} custom-call(s32[1]{0:T(128)S(6)} %sub.11.flag, bf16[384,4096]{1,0:T(8,128)(2,1)} %bitcast.59, bf16[384,2048]{1,0:T(8,128)(2,1)} %bitcast.66, bf16[2048,768]{1,0:T(8,128)(2,1)} %bitcast.74, bf16[2048,768]{1,0:T(8,128)(2,1)} %bitcast.78, bf16[768,2048]{1,0:T(8,128)(2,1)} %bitcast.82), custom_call_target="tpu_custom_call" | custom-call | flops 6039797760 | bytes 14155776 | tf_op jit(solution)/shard_map/pallas_call | solution.py:285
  333.2 11.8 %all-to-all-done.6 = bf16[16,24,2048]{2,1,0:T(8,128)(2,1)S(1)} async-done(((bf16[16,24,2048]{2,1,0:T(8,128)(2,1)}), bf16[16,24,2048]{2,1,0:T(8,128)(2,1)S(1)}, u32[]{:S(2)}, u32[]{:S(2)}) %all-to-all-start.6) | async-done | bytes 1572896 | tf_op jit(solution)/shard_map/all_to_all | solution.py:62
  345.0 1.6 shard_map.92
  346.7 2.7 collective-permute-start.25
  350.3 3.9 all-to-all-start.7
  354.3 3.3 collective-permute-start.26
  357.8 5.9 %collective-permute-done.26 = bf16[64,2048]{1,0:T(8,128)(2,1)S(1)} collective-permute-done((bf16[64,2048]{1,0:T(8,128)(2,1)S(1)}, bf16[64,2048]{1,0:T(8,128)(2,1)S(1)}, u32[]{:S(2)}, u32[]{:S(2)}) %collective-permute-start.26) | collective-permute-done | bytes 262176 | tf_op jit(solution)/shard_map/ppermute | solution.py:24
  363.7 3.8 collective-permute-start.27
  367.5 10.3 %all-to-all-done.7 = bf16[16,24,2048]{2,1,0:T(8,128)(2,1)S(1)} async-done(((bf16[16,24,2048]{2,1,0:T(8,128)(2,1)}), bf16[16,24,2048]{2,1,0:T(8,128)(2,1)S(1)}, u32[]{:S(2)}, u32[]{:S(2)}) %all-to-all-start.7) | async-done | bytes 1572896 | tf_op jit(solution)/shard_map/all_to_all | solution.py:62
  377.8 1.6 shard_map.91
  381.7 3.3 collective-permute-start.28
  385.0 4.9 %collective-permute-done.31 = bf16[64,2048]{1,0:T(8,128)(2,1)S(1)} collective-permute-done((bf16[64,2048]{1,0:T(8,128)(2,1)S(1)}, bf16[64,2048]{1,0:T(8,128)(2,1)S(1)}, u32[]{:S(2)}, u32[]{:S(2)}) %collective-permute-start.31) | collective-permute-done | bytes 262176 | tf_op jit(solution)/shard_map/ppermute | solution.py:24
  390.3 8.2 %collective-permute-done.32 = bf16[64,2048]{1,0:T(8,128)(2,1)S(1)} collective-permute-done((bf16[64,2048]{1,0:T(8,128)(2,1)S(1)}, bf16[64,2048]{1,0:T(8,128)(2,1)S(1)}, u32[]{:S(2)}, u32[]{:S(2)}) %collective-permute-start.32) | collective-permute-done | bytes 262176 | tf_op jit(solution)/shard_map/ppermute | solution.py:24
  398.8 1.1 fusion.21
  (136 shorter events, 14.0 us)
Async XLA Ops:
  4.7 15.0 %collective-permute-start = (bf16[64,4224]{1,0:T(8,128)(2,1)}, bf16[64,4224]{1,0:T(8,128)(2,1)S(1)}, u32[]{:S(2)}, u32[]{:S(2)}) collective-permute-start(bf16[64,4224]{1,0:T(8,128)(2,1)} %shard_map.82.refs_0_), channel_id=1, source_target_pairs={{0,2},{2,4},{4,6},{6,8},{8,10},{10,12},{12,14},{14,0},{1,3},{3,5},... | collective-permute-start | bytes 1622024 | tf_op jit(solution)/shard_map/ppermute | solution.py:24
  7.9 15.4 %collective-permute-start.1 = (bf16[64,4224]{1,0:T(8,128)(2,1)}, bf16[64,4224]{1,0:T(8,128)(2,1)S(1)}, u32[]{:S(2)}, u32[]{:S(2)}) collective-permute-start(bf16[64,4224]{1,0:T(8,128)(2,1)} %shard_map.82.refs_0_), channel_id=1, source_target_pairs={{0,14},{2,0},{4,2},{6,4},{8,6},{10,8},{12,10},{14,12},{1,15},{3,1}... | collective-permute-start | bytes 1622024 | tf_op jit(solution)/shard_map/ppermute | solution.py:24
  19.7 14.3 %copy-start.25 = (bf16[64,4224]{1,0:T(8,128)(2,1)}, bf16[64,4224]{1,0:T(8,128)(2,1)S(1)}, u32[]{:S(2)}) copy-start(bf16[64,4224]{1,0:T(8,128)(2,1)S(1)} %collective-permute-done.refs_1_) | copy-start | bytes 1622020
  19.7 14.2 %collective-permute-start.2 = (bf16[64,4224]{1,0:T(8,128)(2,1)S(1)}, bf16[64,4224]{1,0:T(8,128)(2,1)S(1)}, u32[]{:S(2)}, u32[]{:S(2)}) collective-permute-start(bf16[64,4224]{1,0:T(8,128)(2,1)S(1)} %collective-permute-done.refs_1_), channel_id=1, source_target_pairs={{0,2},{2,4},{4,6},{6,8},{8,10},{10,12},{12,14},{14,0},{1,3},{3,5},... | collective-permute-start | bytes 1622024 | tf_op jit(solution)/shard_map/ppermute | solution.py:24
  23.3 10.7 %copy-start.26 = (bf16[64,4224]{1,0:T(8,128)(2,1)}, bf16[64,4224]{1,0:T(8,128)(2,1)S(1)}, u32[]{:S(2)}) copy-start(bf16[64,4224]{1,0:T(8,128)(2,1)S(1)} %collective-permute-done.1.refs_2_) | copy-start | bytes 1622020
  23.3 16.0 %collective-permute-start.3 = (bf16[64,4224]{1,0:T(8,128)(2,1)S(1)}, bf16[64,4224]{1,0:T(8,128)(2,1)S(1)}, u32[]{:S(2)}, u32[]{:S(2)}) collective-permute-start(bf16[64,4224]{1,0:T(8,128)(2,1)S(1)} %collective-permute-done.1.refs_2_), channel_id=1, source_target_pairs={{0,14},{2,0},{4,2},{6,4},{8,6},{10,8},{12,10},{14,12},{1,15},{3,1}... | collective-permute-start | bytes 1622024 | tf_op jit(solution)/shard_map/ppermute | solution.py:24
  40.1 47.6 %all-to-all-start = ((bf16[16,24,4096]{2,1,0:T(8,128)(2,1)}), bf16[16,24,4096]{2,1,0:T(8,128)(2,1)S(1)}, u32[]{:S(2)}, u32[]{:S(2)}) async-start(bf16[16,24,4096]{2,1,0:T(8,128)(2,1)} %bitcast.63), calls=%async_computation | async-start | bytes 6291456 | tf_op jit(solution)/shard_map/all_to_all | solution.py:62
  47.1 16.7 %collective-permute-start.5 = (bf16[64,4224]{1,0:T(8,128)(2,1)}, bf16[64,4224]{1,0:T(8,128)(2,1)S(1)}, u32[]{:S(2)}, u32[]{:S(2)}) collective-permute-start(bf16[64,4224]{1,0:T(8,128)(2,1)} %copy-done.23), channel_id=1, source_target_pairs={{0,14},{2,0},{4,2},{6,4},{8,6},{10,8},{12,10},{14,12},{1,15},{3,1}... | collective-permute-start | bytes 1622024 | tf_op jit(solution)/shard_map/ppermute | solution.py:24
  47.2 16.8 %collective-permute-start.4 = (bf16[64,4224]{1,0:T(8,128)(2,1)}, bf16[64,4224]{1,0:T(8,128)(2,1)S(1)}, u32[]{:S(2)}, u32[]{:S(2)}) collective-permute-start(bf16[64,4224]{1,0:T(8,128)(2,1)} %copy-done.24), channel_id=1, source_target_pairs={{0,2},{2,4},{4,6},{6,8},{8,10},{10,12},{12,14},{14,0},{1,3},{3,5},... | collective-permute-start | bytes 1622024 | tf_op jit(solution)/shard_map/ppermute | solution.py:24
  63.8 10.4 %copy-start.21 = (bf16[64,4224]{1,0:T(8,128)(2,1)}, bf16[64,4224]{1,0:T(8,128)(2,1)S(1)}, u32[]{:S(2)}) copy-start(bf16[64,4224]{1,0:T(8,128)(2,1)S(1)} %collective-permute-done.5.refs_2_) | copy-start | bytes 1622020
  63.9 9.5 %collective-permute-start.7 = (bf16[32,4224]{1,0:T(8,128)(2,1)S(1)}, bf16[32,4224]{1,0:T(8,128)(2,1)S(1)}, u32[]{:S(2)}, u32[]{:S(2)}) collective-permute-start(bf16[32,4224]{1,0:T(8,128)(2,1)S(1)} %slice.69), channel_id=1, source_target_pairs={{0,14},{2,0},{4,2},{6,4},{8,6},{10,8},{12,10},{14,12},{1,15},{3,1}... | collective-permute-start | bytes 811016 | tf_op jit(solution)/shard_map/ppermute | solution.py:24
  64.0 10.3 %copy-start.22 = (bf16[64,4224]{1,0:T(8,128)(2,1)}, bf16[64,4224]{1,0:T(8,128)(2,1)S(1)}, u32[]{:S(2)}) copy-start(bf16[64,4224]{1,0:T(8,128)(2,1)S(1)} %collective-permute-done.4.refs_1_) | copy-start | bytes 1622020
  64.0 9.4 %collective-permute-start.6 = (bf16[32,4224]{1,0:T(8,128)(2,1)S(1)}, bf16[32,4224]{1,0:T(8,128)(2,1)S(1)}, u32[]{:S(2)}, u32[]{:S(2)}) collective-permute-start(bf16[32,4224]{1,0:T(8,128)(2,1)S(1)} %slice.68), channel_id=1, source_target_pairs={{0,2},{2,4},{4,6},{6,8},{8,10},{10,12},{12,14},{14,0},{1,3},{3,5},... | collective-permute-start | bytes 811016 | tf_op jit(solution)/shard_map/ppermute | solution.py:24
  87.7 44.9 %copy-start.7 = (bf16[16,24,4096]{2,1,0:T(8,128)(2,1)}, bf16[16,24,4096]{2,1,0:T(8,128)(2,1)S(1)}, u32[]{:S(2)}) copy-start(bf16[16,24,4096]{2,1,0:T(8,128)(2,1)S(1)} %all-to-all-done) | copy-start | bytes 9437188
  142.2 27.4 %all-to-all-start.2 = ((bf16[16,24,2048]{2,1,0:T(8,128)(2,1)}), bf16[16,24,2048]{2,1,0:T(8,128)(2,1)S(1)}, u32[]{:S(2)}, u32[]{:S(2)}) async-start(bf16[16,24,2048]{2,1,0:T(8,128)(2,1)} %bitcast.70), calls=%async_computation.2 | async-start | bytes 3145728 | tf_op jit(solution)/shard_map/all_to_all | solution.py:62
  145.9 23.7 %copy-start.5 = (bf16[384,256]{1,0:T(8,128)(2,1)S(1)}, bf16[384,256]{1,0:T(8,128)(2,1)}, u32[]{:S(2)}) copy-start(bf16[384,256]{1,0:T(8,128)(2,1)} %get-tuple-element.53.weighing) | copy-start | bytes 589828
  171.2 8.5 %collective-permute-start.8 = (bf16[32,2048]{1,0:T(8,128)(2,1)}, bf16[32,2048]{1,0:T(8,128)(2,1)S(1)}, u32[]{:S(2)}, u32[]{:S(2)}) collective-permute-start(bf16[32,2048]{1,0:T(8,128)(2,1)} %get-tuple-element.57), channel_id=1, source_target_pairs={{0,2},{2,4},{4,6},{6,8},{8,10},{10,12},{12,14},{14,0},{1,3},{3,5},... | collective-permute-start | bytes 393224 | tf_op jit(solution)/shard_map/ppermute | solution.py:24
  174.9 8.2 %collective-permute-start.12 = (bf16[32,2048]{1,0:T(8,128)(2,1)}, bf16[32,2048]{1,0:T(8,128)(2,1)S(1)}, u32[]{:S(2)}, u32[]{:S(2)}) collective-permute-start(bf16[32,2048]{1,0:T(8,128)(2,1)} %get-tuple-element.61), channel_id=1, source_target_pairs={{0,14},{2,0},{4,2},{6,4},{8,6},{10,8},{12,10},{14,12},{1,15},{3,1}... | collective-permute-start | bytes 393224 | tf_op jit(solution)/shard_map/ppermute | solution.py:24
  175.8 3.9 copy-start.18
  175.9 7.3 %copy-start.16 = (bf16[64,2048]{1,0:T(8,128)(2,1)S(1)}, bf16[64,2048]{1,0:T(8,128)(2,1)}, u32[]{:S(2)}) copy-start(bf16[64,2048]{1,0:T(8,128)(2,1)} %get-tuple-element.60) | copy-start | bytes 786436
  175.9 27.5 %all-to-all-start.3 = ((bf16[16,24,2048]{2,1,0:T(8,128)(2,1)}), bf16[16,24,2048]{2,1,0:T(8,128)(2,1)S(1)}, u32[]{:S(2)}, u32[]{:S(2)}) async-start(bf16[16,24,2048]{2,1,0:T(8,128)(2,1)} %bitcast.17), calls=%async_computation.3 | async-start | bytes 3145728 | tf_op jit(solution)/shard_map/all_to_all | solution.py:62
  179.7 9.5 %copy-start.12 = (bf16[64,2048]{1,0:T(8,128)(2,1)S(1)}, bf16[64,2048]{1,0:T(8,128)(2,1)}, u32[]{:S(2)}) copy-start(bf16[64,2048]{1,0:T(8,128)(2,1)} %get-tuple-element.55) | copy-start | bytes 786436
  179.7 23.6 %copy-start.4 = (bf16[384,256]{1,0:T(8,128)(2,1)S(1)}, bf16[384,256]{1,0:T(8,128)(2,1)}, u32[]{:S(2)}) copy-start(bf16[384,256]{1,0:T(8,128)(2,1)} %get-tuple-element.42.weighing) | copy-start | bytes 589828
  179.9 9.3 %collective-permute-start.9 = (bf16[64,2048]{1,0:T(8,128)(2,1)S(1)}, bf16[64,2048]{1,0:T(8,128)(2,1)S(1)}, u32[]{:S(2)}, u32[]{:S(2)}) collective-permute-start(bf16[64,2048]{1,0:T(8,128)(2,1)S(1)} %pad_maximum_fusion.1), channel_id=1, source_target_pairs={{0,2},{2,4},{4,6},{6,8},{8,10},{10,12},{12,14},{14,0},{1,3},{3,5},... | collective-permute-start | bytes 786440 | tf_op jit(solution)/shard_map/ppermute | solution.py:24
  183.2 21.8 %collective-permute-start.13 = (bf16[64,2048]{1,0:T(8,128)(2,1)S(1)}, bf16[64,2048]{1,0:T(8,128)(2,1)S(1)}, u32[]{:S(2)}, u32[]{:S(2)}) collective-permute-start(bf16[64,2048]{1,0:T(8,128)(2,1)S(1)} %pad_maximum_fusion.2), channel_id=1, source_target_pairs={{0,14},{2,0},{4,2},{6,4},{8,6},{10,8},{12,10},{14,12},{1,15},{3,1}... | collective-permute-start | bytes 786440 | tf_op jit(solution)/shard_map/ppermute | solution.py:24
  189.3 17.0 %collective-permute-start.10 = (bf16[64,2048]{1,0:T(8,128)(2,1)S(1)}, bf16[64,2048]{1,0:T(8,128)(2,1)S(1)}, u32[]{:S(2)}, u32[]{:S(2)}) collective-permute-start(bf16[64,2048]{1,0:T(8,128)(2,1)S(1)} %add_convert_fusion.7), channel_id=1, source_target_pairs={{0,2},{2,4},{4,6},{6,8},{8,10},{10,12},{12,14},{14,0},{1,3},{3,5},... | collective-permute-start | bytes 786440 | tf_op jit(solution)/shard_map/ppermute | solution.py:24
  205.0 10.5 %copy-start.14 = (bf16[64,2048]{1,0:T(8,128)(2,1)S(1)}, bf16[64,2048]{1,0:T(8,128)(2,1)}, u32[]{:S(2)}) copy-start(bf16[64,2048]{1,0:T(8,128)(2,1)} %get-tuple-element.58) | copy-start | bytes 786436
  205.0 19.1 %copy-start.1 = (f32[1,2048]{1,0:T(1,128)S(1)}, f32[1,2048]{1,0:T(1,128)}, u32[]{:S(2)}) copy-start(f32[1,2048]{1,0:T(1,128)} %gain.1) | copy-start | bytes 24580
  205.0 19.1 %copy-start.6 = (bf16[1,64,2048]{2,1,0:T(8,128)(2,1)S(1)}, bf16[1,64,2048]{2,1,0:T(8,128)(2,1)}, u32[]{:S(2)}) copy-start(bf16[1,64,2048]{2,1,0:T(8,128)(2,1)} %param.9) | copy-start | bytes 786436
  205.0 19.1 %copy-start.8 = (bf16[1,64,2048]{2,1,0:T(8,128)(2,1)S(1)}, bf16[1,64,2048]{2,1,0:T(8,128)(2,1)}, u32[]{:S(2)}) copy-start(bf16[1,64,2048]{2,1,0:T(8,128)(2,1)} %param.8) | copy-start | bytes 786436
  205.0 19.1 %copy-start.10 = (bf16[64,2048]{1,0:T(8,128)(2,1)S(1)}, bf16[64,2048]{1,0:T(8,128)(2,1)}, u32[]{:S(2)}) copy-start(bf16[64,2048]{1,0:T(8,128)(2,1)} %get-tuple-element.51) | copy-start | bytes 786436
  206.2 9.4 %collective-permute-start.14 = (bf16[64,2048]{1,0:T(8,128)(2,1)S(1)}, bf16[64,2048]{1,0:T(8,128)(2,1)S(1)}, u32[]{:S(2)}, u32[]{:S(2)}) collective-permute-start(bf16[64,2048]{1,0:T(8,128)(2,1)S(1)} %add_convert_fusion.5), channel_id=1, source_target_pairs={{0,14},{2,0},{4,2},{6,4},{8,6},{10,8},{12,10},{14,12},{1,15},{3,1}... | collective-permute-start | bytes 786440 | tf_op jit(solution)/shard_map/ppermute | solution.py:24
  207.3 8.8 %collective-permute-start.11 = (bf16[64,2048]{1,0:T(8,128)(2,1)S(1)}, bf16[64,2048]{1,0:T(8,128)(2,1)S(1)}, u32[]{:S(2)}, u32[]{:S(2)}) collective-permute-start(bf16[64,2048]{1,0:T(8,128)(2,1)S(1)} %add_convert_fusion.6), channel_id=1, source_target_pairs={{0,2},{2,4},{4,6},{6,8},{8,10},{10,12},{12,14},{14,0},{1,3},{3,5},... | collective-permute-start | bytes 786440 | tf_op jit(solution)/shard_map/ppermute | solution.py:24
  215.6 8.5 %collective-permute-start.15 = (bf16[64,2048]{1,0:T(8,128)(2,1)S(1)}, bf16[64,2048]{1,0:T(8,128)(2,1)S(1)}, u32[]{:S(2)}, u32[]{:S(2)}) collective-permute-start(bf16[64,2048]{1,0:T(8,128)(2,1)S(1)} %add_convert_fusion.4), channel_id=1, source_target_pairs={{0,14},{2,0},{4,2},{6,4},{8,6},{10,8},{12,10},{14,12},{1,15},{3,1}... | collective-permute-start | bytes 786440 | tf_op jit(solution)/shard_map/ppermute | solution.py:24
  224.5 22.1 %copy-start.27 = (bf16[384,256]{1,0:T(8,128)(2,1)S(1)}, bf16[384,256]{1,0:T(8,128)(2,1)}, u32[]{:S(2)}) copy-start(bf16[384,256]{1,0:T(8,128)(2,1)} %get-tuple-element.63) | copy-start | bytes 589828
  224.9 7.4 %collective-permute-start.16 = (bf16[64,2048]{1,0:T(8,128)(2,1)S(1)}, bf16[64,2048]{1,0:T(8,128)(2,1)S(1)}, u32[]{:S(2)}, u32[]{:S(2)}) collective-permute-start(bf16[64,2048]{1,0:T(8,128)(2,1)S(1)} %fusion.8), channel_id=1, source_target_pairs={{0,128},{128,0},{1,129},{129,1},{2,130},{130,2},{3,131},{131,3},{4... | collective-permute-start | bytes 786440 | tf_op jit(solution)/shard_map/ppermute | solution.py:376
  232.8 7.5 %collective-permute-start.17 = (bf16[64,2048]{1,0:T(8,128)(2,1)S(1)}, bf16[64,2048]{1,0:T(8,128)(2,1)S(1)}, u32[]{:S(2)}, u32[]{:S(2)}) collective-permute-start(bf16[64,2048]{1,0:T(8,128)(2,1)S(1)} %fusion.22), channel_id=1, source_target_pairs={{0,2},{2,4},{4,6},{6,8},{8,10},{10,12},{12,14},{14,0},{1,3},{3,5},... | collective-permute-start | bytes 786440 | tf_op jit(solution)/shard_map/ppermute | solution.py:24
  232.9 7.7 %collective-permute-start.18 = (bf16[64,2048]{1,0:T(8,128)(2,1)S(1)}, bf16[64,2048]{1,0:T(8,128)(2,1)S(1)}, u32[]{:S(2)}, u32[]{:S(2)}) collective-permute-start(bf16[64,2048]{1,0:T(8,128)(2,1)S(1)} %fusion.22), channel_id=1, source_target_pairs={{0,14},{2,0},{4,2},{6,4},{8,6},{10,8},{12,10},{14,12},{1,15},{3,1}... | collective-permute-start | bytes 786440 | tf_op jit(solution)/shard_map/ppermute | solution.py:24
  240.3 6.4 %collective-permute-start.19 = (bf16[64,2048]{1,0:T(8,128)(2,1)S(1)}, bf16[64,2048]{1,0:T(8,128)(2,1)S(1)}, u32[]{:S(2)}, u32[]{:S(2)}) collective-permute-start(bf16[64,2048]{1,0:T(8,128)(2,1)S(1)} %collective-permute-done.17), channel_id=1, source_target_pairs={{0,2},{2,4},{4,6},{6,8},{8,10},{10,12},{12,14},{14,0},{1,3},{3,5},... | collective-permute-start | bytes 786440 | tf_op jit(solution)/shard_map/ppermute | solution.py:24
  240.5 15.1 %collective-permute-start.20 = (bf16[64,2048]{1,0:T(8,128)(2,1)S(1)}, bf16[64,2048]{1,0:T(8,128)(2,1)S(1)}, u32[]{:S(2)}, u32[]{:S(2)}) collective-permute-start(bf16[64,2048]{1,0:T(8,128)(2,1)S(1)} %collective-permute-done.18), channel_id=1, source_target_pairs={{0,14},{2,0},{4,2},{6,4},{8,6},{10,8},{12,10},{14,12},{1,15},{3,1}... | collective-permute-start | bytes 786440 | tf_op jit(solution)/shard_map/ppermute | solution.py:24
  248.5 28.1 %all-to-all-start.4 = ((bf16[16,24,2048]{2,1,0:T(8,128)(2,1)}), bf16[16,24,2048]{2,1,0:T(8,128)(2,1)S(1)}, u32[]{:S(2)}, u32[]{:S(2)}) async-start(bf16[16,24,2048]{2,1,0:T(8,128)(2,1)} %bitcast.68), calls=%async_computation.4 | async-start | bytes 3145728 | tf_op jit(solution)/shard_map/all_to_all | solution.py:62
  252.8 19.0 %copy-start.20 = (bf16[384,256]{1,0:T(8,128)(2,1)S(1)}, bf16[384,256]{1,0:T(8,128)(2,1)}, u32[]{:S(2)}) copy-start(bf16[384,256]{1,0:T(8,128)(2,1)} %get-tuple-element.64) | copy-start | bytes 589828
  252.8 8.9 %collective-permute-start.21 = (bf16[64,2048]{1,0:T(8,128)(2,1)S(1)}, bf16[64,2048]{1,0:T(8,128)(2,1)S(1)}, u32[]{:S(2)}, u32[]{:S(2)}) collective-permute-start(bf16[64,2048]{1,0:T(8,128)(2,1)S(1)} %collective-permute-done.19), channel_id=1, source_target_pairs={{0,2},{2,4},{4,6},{6,8},{8,10},{10,12},{12,14},{14,0},{1,3},{3,5},... | collective-permute-start | bytes 786440 | tf_op jit(solution)/shard_map/ppermute | solution.py:24
  255.6 9.9 %collective-permute-start.22 = (bf16[64,2048]{1,0:T(8,128)(2,1)S(1)}, bf16[64,2048]{1,0:T(8,128)(2,1)S(1)}, u32[]{:S(2)}, u32[]{:S(2)}) collective-permute-start(bf16[64,2048]{1,0:T(8,128)(2,1)S(1)} %collective-permute-done.20), channel_id=1, source_target_pairs={{0,14},{2,0},{4,2},{6,4},{8,6},{10,8},{12,10},{14,12},{1,15},{3,1}... | collective-permute-start | bytes 786440 | tf_op jit(solution)/shard_map/ppermute | solution.py:24
  261.8 6.3 %collective-permute-start.23 = (bf16[32,2048]{1,0:T(8,128)(2,1)S(1)}, bf16[32,2048]{1,0:T(8,128)(2,1)S(1)}, u32[]{:S(2)}, u32[]{:S(2)}) collective-permute-start(bf16[32,2048]{1,0:T(8,128)(2,1)S(1)} %slice.70), channel_id=1, source_target_pairs={{0,2},{2,4},{4,6},{6,8},{8,10},{10,12},{12,14},{14,0},{1,3},{3,5},... | collective-permute-start | bytes 393224 | tf_op jit(solution)/shard_map/ppermute | solution.py:24
  265.6 6.3 %collective-permute-start.24 = (bf16[32,2048]{1,0:T(8,128)(2,1)S(1)}, bf16[32,2048]{1,0:T(8,128)(2,1)S(1)}, u32[]{:S(2)}, u32[]{:S(2)}) collective-permute-start(bf16[32,2048]{1,0:T(8,128)(2,1)S(1)} %slice.71), channel_id=1, source_target_pairs={{0,14},{2,0},{4,2},{6,4},{8,6},{10,8},{12,10},{14,12},{1,15},{3,1}... | collective-permute-start | bytes 393224 | tf_op jit(solution)/shard_map/ppermute | solution.py:24
  277.7 28.1 %all-to-all-start.5 = ((bf16[16,24,2048]{2,1,0:T(8,128)(2,1)}), bf16[16,24,2048]{2,1,0:T(8,128)(2,1)}, u32[]{:S(2)}, u32[]{:S(2)}) async-start(bf16[16,24,2048]{2,1,0:T(8,128)(2,1)} %bitcast.22), calls=%async_computation.5 | async-start | bytes 3145728 | tf_op jit(solution)/shard_map/all_to_all | solution.py:62
  317.6 27.4 %all-to-all-start.6 = ((bf16[16,24,2048]{2,1,0:T(8,128)(2,1)}), bf16[16,24,2048]{2,1,0:T(8,128)(2,1)S(1)}, u32[]{:S(2)}, u32[]{:S(2)}) async-start(bf16[16,24,2048]{2,1,0:T(8,128)(2,1)} %bitcast.69), calls=%async_computation.6 | async-start | bytes 3145728 | tf_op jit(solution)/shard_map/all_to_all | solution.py:62
  321.4 23.7 %copy-start.3 = (bf16[384,256]{1,0:T(8,128)(2,1)S(1)}, bf16[384,256]{1,0:T(8,128)(2,1)}, u32[]{:S(2)}) copy-start(bf16[384,256]{1,0:T(8,128)(2,1)} %get-tuple-element.70.weighing) | copy-start | bytes 589828
  346.7 7.6 %collective-permute-start.25 = (bf16[32,2048]{1,0:T(8,128)(2,1)}, bf16[32,2048]{1,0:T(8,128)(2,1)S(1)}, u32[]{:S(2)}, u32[]{:S(2)}) collective-permute-start(bf16[32,2048]{1,0:T(8,128)(2,1)} %get-tuple-element.74), channel_id=1, source_target_pairs={{0,2},{2,4},{4,6},{6,8},{8,10},{10,12},{12,14},{14,0},{1,3},{3,5},... | collective-permute-start | bytes 393224 | tf_op jit(solution)/shard_map/ppermute | solution.py:24
  349.4 8.2 %collective-permute-start.29 = (bf16[32,2048]{1,0:T(8,128)(2,1)}, bf16[32,2048]{1,0:T(8,128)(2,1)S(1)}, u32[]{:S(2)}, u32[]{:S(2)}) collective-permute-start(bf16[32,2048]{1,0:T(8,128)(2,1)} %get-tuple-element.78), channel_id=1, source_target_pairs={{0,14},{2,0},{4,2},{6,4},{8,6},{10,8},{12,10},{14,12},{1,15},{3,1}... | collective-permute-start | bytes 393224 | tf_op jit(solution)/shard_map/ppermute | solution.py:24
  350.3 3.9 copy-start.19
  350.3 7.3 %copy-start.17 = (bf16[64,2048]{1,0:T(8,128)(2,1)S(1)}, bf16[64,2048]{1,0:T(8,128)(2,1)}, u32[]{:S(2)}) copy-start(bf16[64,2048]{1,0:T(8,128)(2,1)} %get-tuple-element.77) | copy-start | bytes 786436
  350.3 27.5 %all-to-all-start.7 = ((bf16[16,24,2048]{2,1,0:T(8,128)(2,1)}), bf16[16,24,2048]{2,1,0:T(8,128)(2,1)S(1)}, u32[]{:S(2)}, u32[]{:S(2)}) async-start(bf16[16,24,2048]{2,1,0:T(8,128)(2,1)} %bitcast.67), calls=%async_computation.7 | async-start | bytes 3145728 | tf_op jit(solution)/shard_map/all_to_all | solution.py:62
  354.2 9.5 %copy-start.13 = (bf16[64,2048]{1,0:T(8,128)(2,1)S(1)}, bf16[64,2048]{1,0:T(8,128)(2,1)}, u32[]{:S(2)}) copy-start(bf16[64,2048]{1,0:T(8,128)(2,1)} %get-tuple-element.72) | copy-start | bytes 786436
  354.2 23.6 %copy-start.2 = (bf16[384,256]{1,0:T(8,128)(2,1)S(1)}, bf16[384,256]{1,0:T(8,128)(2,1)}, u32[]{:S(2)}) copy-start(bf16[384,256]{1,0:T(8,128)(2,1)} %get-tuple-element.62.weighing) | copy-start | bytes 589828
  354.3 9.3 %collective-permute-start.26 = (bf16[64,2048]{1,0:T(8,128)(2,1)S(1)}, bf16[64,2048]{1,0:T(8,128)(2,1)S(1)}, u32[]{:S(2)}, u32[]{:S(2)}) collective-permute-start(bf16[64,2048]{1,0:T(8,128)(2,1)S(1)} %pad_maximum_fusion.3), channel_id=1, source_target_pairs={{0,2},{2,4},{4,6},{6,8},{8,10},{10,12},{12,14},{14,0},{1,3},{3,5},... | collective-permute-start | bytes 786440 | tf_op jit(solution)/shard_map/ppermute | solution.py:24
  357.7 21.8 %collective-permute-start.30 = (bf16[64,2048]{1,0:T(8,128)(2,1)S(1)}, bf16[64,2048]{1,0:T(8,128)(2,1)S(1)}, u32[]{:S(2)}, u32[]{:S(2)}) collective-permute-start(bf16[64,2048]{1,0:T(8,128)(2,1)S(1)} %pad_maximum_fusion.4), channel_id=1, source_target_pairs={{0,14},{2,0},{4,2},{6,4},{8,6},{10,8},{12,10},{14,12},{1,15},{3,1}... | collective-permute-start | bytes 786440 | tf_op jit(solution)/shard_map/ppermute | solution.py:24
  363.7 16.9 %collective-permute-start.27 = (bf16[64,2048]{1,0:T(8,128)(2,1)S(1)}, bf16[64,2048]{1,0:T(8,128)(2,1)S(1)}, u32[]{:S(2)}, u32[]{:S(2)}) collective-permute-start(bf16[64,2048]{1,0:T(8,128)(2,1)S(1)} %add_convert_fusion.3), channel_id=1, source_target_pairs={{0,2},{2,4},{4,6},{6,8},{8,10},{10,12},{12,14},{14,0},{1,3},{3,5},... | collective-permute-start | bytes 786440 | tf_op jit(solution)/shard_map/ppermute | solution.py:24
  379.4 10.5 %copy-start.15 = (bf16[64,2048]{1,0:T(8,128)(2,1)S(1)}, bf16[64,2048]{1,0:T(8,128)(2,1)}, u32[]{:S(2)}) copy-start(bf16[64,2048]{1,0:T(8,128)(2,1)} %get-tuple-element.75) | copy-start | bytes 786436
  379.4 19.0 %copy-start.11 = (bf16[64,2048]{1,0:T(8,128)(2,1)S(1)}, bf16[64,2048]{1,0:T(8,128)(2,1)}, u32[]{:S(2)}) copy-start(bf16[64,2048]{1,0:T(8,128)(2,1)} %get-tuple-element.68) | copy-start | bytes 786436
  380.5 9.4 %collective-permute-start.31 = (bf16[64,2048]{1,0:T(8,128)(2,1)S(1)}, bf16[64,2048]{1,0:T(8,128)(2,1)S(1)}, u32[]{:S(2)}, u32[]{:S(2)}) collective-permute-start(bf16[64,2048]{1,0:T(8,128)(2,1)S(1)} %add_convert_fusion.1), channel_id=1, source_target_pairs={{0,14},{2,0},{4,2},{6,4},{8,6},{10,8},{12,10},{14,12},{1,15},{3,1}... | collective-permute-start | bytes 786440 | tf_op jit(solution)/shard_map/ppermute | solution.py:24
  381.7 8.6 %collective-permute-start.28 = (bf16[64,2048]{1,0:T(8,128)(2,1)S(1)}, bf16[64,2048]{1,0:T(8,128)(2,1)S(1)}, u32[]{:S(2)}, u32[]{:S(2)}) collective-permute-start(bf16[64,2048]{1,0:T(8,128)(2,1)S(1)} %add_convert_fusion.2), channel_id=1, source_target_pairs={{0,2},{2,4},{4,6},{6,8},{8,10},{10,12},{12,14},{14,0},{1,3},{3,5},... | collective-permute-start | bytes 786440 | tf_op jit(solution)/shard_map/ppermute | solution.py:24
  390.0 8.5 %collective-permute-start.32 = (bf16[64,2048]{1,0:T(8,128)(2,1)S(1)}, bf16[64,2048]{1,0:T(8,128)(2,1)S(1)}, u32[]{:S(2)}, u32[]{:S(2)}) collective-permute-start(bf16[64,2048]{1,0:T(8,128)(2,1)S(1)} %add_convert_fusion), channel_id=1, source_target_pairs={{0,14},{2,0},{4,2},{6,4},{8,6},{10,8},{12,10},{14,12},{1,15},{3,1}... | collective-permute-start | bytes 786440 | tf_op jit(solution)/shard_map/ppermute | solution.py:24
  (4 other events, 3.5 us)

commit v5 on v4

--- a/solution.py
+++ b/solution.py
@@ -227,11 +227,11 @@
     copies = [
         pltpu.make_async_copy(source, target, done.at[i]) for i, (source, target) in enumerate(into)
     ]
-    for copy in (copies[0], copies[2]):
+    for copy in (copies[0], copies[2], copies[3]):
         copy.start()
     for copy in (copies[0], copies[2]):
         copy.wait()
-    for copy in (copies[1], *copies[3:]):
+    for copy in (copies[1], copies[4]):
         copy.start()
     forward = flag[0] == 1
     piece = width // 4

time: 408 us -> 407 us (level)
  no operation moved by 1% of the time
where the time goes in v5:
time: 407 us; the launch traced here: 399 us
  waiting for transfers between devices  189 us (46%)
  starting transfers between devices  84.7 us (21%)
  Pallas kernels  59.6 us (15%)
  blocking collectives  44.9 us (11%)
  other arithmetic  8.43 us (2%)
  local copies, waits for them, and re-layouts  7.36 us (2%)
    ppermute x32, waiting for transfers between devices, step_ring(): lax.ppermute(block, RING, [(i, (i + step) % count) for i in range(count)])  102 us
    all_to_all x7, waiting for transfers between devices, exchange(): lax.all_to_all(parts, PLANE, split_axis=0, concat_axis=0, tiled=True)  82.4 us
    ppermute x32, starting transfers between devices, step_ring(): lax.ppermute(block, RING, [(i, (i + step) % count) for i in range(count)])  52.4 us
    all_to_all x1, blocking collectives, exchange(): lax.all_to_all(parts, PLANE, split_axis=0, concat_axis=0, tiled=True)  44.9 us
    pallas_call x4, Pallas kernels, apply_expert(): pl.pallas_call(functools.partial(expert_kernel, first_at, second_at, forw...  41.8 us
    all_to_all x7, starting transfers between devices, exchange(): lax.all_to_all(parts, PLANE, split_axis=0, concat_axis=0, tiled=True)  30.5 us
    pallas_call x2, Pallas kernels, pick_both(): pl.pallas_call(functools.partial(pick_kernel, top, ring, peers), in_specs...  9.04 us
  transfers between devices with their start and end apart: 40, of which 26 were waited for; matrix products, arithmetic and copies ran while one was open for 3% of the time, Pallas kernels for 8%

profile of v5, /device:TPU:96, one launch (start us, length us, event | category | flops | bytes accessed | tf_op | source)
XLA Modules:
  0.0 398.8 jit_solution(14497642919019931195)
XLA Ops:
  2.6 2.2 shard_map.82.refs_0_
  4.7 3.1 collective-permute-start
  7.9 11.8 %collective-permute-done.refs_1_ = bf16[64,4224]{1,0:T(8,128)(2,1)S(1)} collective-permute-done((bf16[64,4224]{1,0:T(8,128)(2,1)}, bf16[64,4224]{1,0:T(8,128)(2,1)S(1)}, u32[]{:S(2)}, u32[]{:S(2)}) %collective-permute-start) | collective-permute-done | bytes 540704 | tf_op jit(solution)/shard_map/ppermute | solution.py:24
  19.7 3.6 collective-permute-start.2
  23.4 10.6 %collective-permute-done.2.refs_3_ = bf16[64,4224]{1,0:T(8,128)(2,1)S(1)} collective-permute-done((bf16[64,4224]{1,0:T(8,128)(2,1)S(1)}, bf16[64,4224]{1,0:T(8,128)(2,1)S(1)}, u32[]{:S(2)}, u32[]{:S(2)}) %collective-permute-start.2) | collective-permute-done | bytes 540704 | tf_op jit(solution)/shard_map/ppermute | solution.py:24
  34.8 4.5 %shard_map.83 = (bf16[384,4096]{1,0:T(8,128)(2,1)}, bf16[384,256]{1,0:T(8,128)(2,1)}, bf16[384,256]{1,0:T(8,128)(2,1)}, bf16[384,256]{1,0:T(8,128)(2,1)}) custom-call(s32[2]{0:T(128)S(1)} %pad_add_fusion.told, bf16[64,4224]{1,0:T(8,128)(2,1)} %shard_map.82.refs_0_, bf16[64,4224]{1,0:T(8,128)(2,1)} %copy-done.25, bf16[64,4224]{1,0:T(8,128)(2,1)} %copy-done.26, ...), custom_call_target="tpu_custom_call" | custom-call | flops 805306368 | bytes 5832704 | tf_op jit(solution)/shard_map/pallas_call | solution.py:125
  40.1 7.0 %all-to-all-start = ((bf16[16,24,4096]{2,1,0:T(8,128)(2,1)}), bf16[16,24,4096]{2,1,0:T(8,128)(2,1)S(1)}, u32[]{:S(2)}, u32[]{:S(2)}) async-start(bf16[16,24,4096]{2,1,0:T(8,128)(2,1)} %bitcast.63), calls=%async_computation | async-start | bytes 6291456 | tf_op jit(solution)/shard_map/all_to_all | solution.py:62
  47.2 3.8 collective-permute-start.4
  51.0 12.9 %collective-permute-done.5.refs_2_ = bf16[64,4224]{1,0:T(8,128)(2,1)S(1)} collective-permute-done((bf16[64,4224]{1,0:T(8,128)(2,1)}, bf16[64,4224]{1,0:T(8,128)(2,1)S(1)}, u32[]{:S(2)}, u32[]{:S(2)}) %collective-permute-start.5) | collective-permute-done | bytes 540704 | tf_op jit(solution)/shard_map/ppermute | solution.py:24
  64.0 3.3 collective-permute-start.6
  67.3 6.1 %collective-permute-done.7 = bf16[32,4224]{1,0:T(8,128)(2,1)S(1)} collective-permute-done((bf16[32,4224]{1,0:T(8,128)(2,1)S(1)}, bf16[32,4224]{1,0:T(8,128)(2,1)S(1)}, u32[]{:S(2)}, u32[]{:S(2)}) %collective-permute-start.7) | collective-permute-done | bytes 270368 | tf_op jit(solution)/shard_map/ppermute | solution.py:24
  74.2 4.6 %shard_map.84 = (bf16[384,4096]{1,0:T(8,128)(2,1)}, bf16[384,256]{1,0:T(8,128)(2,1)}, bf16[384,256]{1,0:T(8,128)(2,1)}, bf16[384,256]{1,0:T(8,128)(2,1)}) custom-call(s32[2]{0:T(128)S(1)} %pad_add_fusion.told, bf16[64,4224]{1,0:T(8,128)(2,1)} %copy-done.23, bf16[64,4224]{1,0:T(8,128)(2,1)} %copy-done.22, bf16[64,4224]{1,0:T(8,128)(2,1)} %copy-done.21, ...), custom_call_target="tpu_custom_call" | custom-call | flops 805306368 | bytes 5832704 | tf_op jit(solution)/shard_map/pallas_call | solution.py:125
  78.8 8.9 %all-to-all-done = bf16[16,24,4096]{2,1,0:T(8,128)(2,1)S(1)} async-done(((bf16[16,24,4096]{2,1,0:T(8,128)(2,1)}), bf16[16,24,4096]{2,1,0:T(8,128)(2,1)S(1)}, u32[]{:S(2)}, u32[]{:S(2)}) %all-to-all-start) | async-done | bytes 3145760 | tf_op jit(solution)/shard_map/all_to_all | solution.py:62
  87.7 44.9 %all_to_all.40 = bf16[16,24,4096]{2,1,0:T(8,128)(2,1)} all-to-all(bf16[16,24,4096]{2,1,0:T(8,128)(2,1)} %bitcast.64), channel_id=1, replica_groups=mesh['segment'=2,'expert_0'=4,'expert_1'=2,'expert_2'=8,'expert_3'=2] {'..., dimensions={0} | all-to-all | bytes 6291456 | tf_op jit(solution)/shard_map/all_to_all | solution.py:62
  132.6 9.8 %shard_map.85 = bf16[384,2048]{1,0:T(8,128)(2,1)} custom-call(s32[1]{0:T(128)} %bitcast.3.forward.flag, bf16[384,4096]{1,0:T(8,128)(2,1)} %bitcast.60, bf16[384,4096]{1,0:T(8,128)(2,1)} %bitcast.61, bf16[2048,768]{1,0:T(8,128)(2,1)} %bitcast.71, bf16[2048,768]{1,0:T(8,128)(2,1)} %bitcast.75, bf16[768,2048]{1,0:T(8,128)(2,1)} %bitcast.79), custom_call_target="tpu_custom_call" | custom-call | flops 6039797760 | bytes 14155776 | tf_op jit(solution)/shard_map/pallas_call | solution.py:285
  142.4 3.7 all-to-all-start.2
  146.2 9.9 %shard_map.86 = bf16[384,2048]{1,0:T(8,128)(2,1)} custom-call(s32[1]{0:T(128)} %bitcast.3.forward.flag, bf16[384,4096]{1,0:T(8,128)(2,1)} %bitcast.57, bf16[384,4096]{1,0:T(8,128)(2,1)} %bitcast.58, bf16[2048,768]{1,0:T(8,128)(2,1)} %bitcast.72, bf16[2048,768]{1,0:T(8,128)(2,1)} %bitcast.76, bf16[768,2048]{1,0:T(8,128)(2,1)} %bitcast.80), custom_call_target="tpu_custom_call" | custom-call | flops 6039797760 | bytes 14155776 | tf_op jit(solution)/shard_map/pallas_call | solution.py:285
  156.1 13.7 %all-to-all-done.2 = bf16[16,24,2048]{2,1,0:T(8,128)(2,1)S(1)} async-done(((bf16[16,24,2048]{2,1,0:T(8,128)(2,1)}), bf16[16,24,2048]{2,1,0:T(8,128)(2,1)S(1)}, u32[]{:S(2)}, u32[]{:S(2)}) %all-to-all-start.2) | async-done | bytes 1572896 | tf_op jit(solution)/shard_map/all_to_all | solution.py:62
  169.8 1.6 shard_map.88
  171.5 3.7 collective-permute-start.8
  176.1 3.9 all-to-all-start.3
  180.1 3.3 collective-permute-start.9
  183.5 5.9 %collective-permute-done.9 = bf16[64,2048]{1,0:T(8,128)(2,1)S(1)} collective-permute-done((bf16[64,2048]{1,0:T(8,128)(2,1)S(1)}, bf16[64,2048]{1,0:T(8,128)(2,1)S(1)}, u32[]{:S(2)}, u32[]{:S(2)}) %collective-permute-start.9) | collective-permute-done | bytes 262176 | tf_op jit(solution)/shard_map/ppermute | solution.py:24
  189.5 3.8 collective-permute-start.10
  193.2 10.3 %all-to-all-done.3 = bf16[16,24,2048]{2,1,0:T(8,128)(2,1)S(1)} async-done(((bf16[16,24,2048]{2,1,0:T(8,128)(2,1)}), bf16[16,24,2048]{2,1,0:T(8,128)(2,1)S(1)}, u32[]{:S(2)}, u32[]{:S(2)}) %all-to-all-start.3) | async-done | bytes 1572896 | tf_op jit(solution)/shard_map/all_to_all | solution.py:62
  203.6 1.6 shard_map.87
  205.3 1.1 add_convert_fusion.5
  207.5 3.5 collective-permute-start.11
  211.0 4.7 %collective-permute-done.14 = bf16[64,2048]{1,0:T(8,128)(2,1)S(1)} collective-permute-done((bf16[64,2048]{1,0:T(8,128)(2,1)S(1)}, bf16[64,2048]{1,0:T(8,128)(2,1)S(1)}, u32[]{:S(2)}, u32[]{:S(2)}) %collective-permute-start.14) | collective-permute-done | bytes 262176 | tf_op jit(solution)/shard_map/ppermute | solution.py:24
  216.3 8.0 %collective-permute-done.15 = bf16[64,2048]{1,0:T(8,128)(2,1)S(1)} collective-permute-done((bf16[64,2048]{1,0:T(8,128)(2,1)S(1)}, bf16[64,2048]{1,0:T(8,128)(2,1)S(1)}, u32[]{:S(2)}, u32[]{:S(2)}) %collective-permute-start.15) | collective-permute-done | bytes 262176 | tf_op jit(solution)/shard_map/ppermute | solution.py:24
  225.1 1.9 collective-permute-start.16
  227.1 4.5 %collective-permute-done.16 = bf16[64,2048]{1,0:T(8,128)(2,1)S(1)} collective-permute-done((bf16[64,2048]{1,0:T(8,128)(2,1)S(1)}, bf16[64,2048]{1,0:T(8,128)(2,1)S(1)}, u32[]{:S(2)}, u32[]{:S(2)}) %collective-permute-start.16) | collective-permute-done | bytes 262176 | tf_op jit(solution)/shard_map/ppermute | solution.py:376
  232.3 1.8 collective-permute-start.18
  234.1 5.9 %collective-permute-done.17 = bf16[64,2048]{1,0:T(8,128)(2,1)S(1)} collective-permute-done((bf16[64,2048]{1,0:T(8,128)(2,1)S(1)}, bf16[64,2048]{1,0:T(8,128)(2,1)S(1)}, u32[]{:S(2)}, u32[]{:S(2)}) %collective-permute-start.17) | collective-permute-done | bytes 262176 | tf_op jit(solution)/shard_map/ppermute | solution.py:24
  240.3 1.7 collective-permute-start.20
  242.0 4.3 %collective-permute-done.19 = bf16[64,2048]{1,0:T(8,128)(2,1)S(1)} collective-permute-done((bf16[64,2048]{1,0:T(8,128)(2,1)S(1)}, bf16[64,2048]{1,0:T(8,128)(2,1)S(1)}, u32[]{:S(2)}, u32[]{:S(2)}) %collective-permute-start.19) | collective-permute-done | bytes 262176 | tf_op jit(solution)/shard_map/ppermute | solution.py:24
  246.3 1.8 convolution_convert_fusion.1
  248.1 3.9 all-to-all-start.4
  252.1 2.8 collective-permute-start.21
  254.9 6.1 %collective-permute-done.21 = bf16[64,2048]{1,0:T(8,128)(2,1)S(1)} collective-permute-done((bf16[64,2048]{1,0:T(8,128)(2,1)S(1)}, bf16[64,2048]{1,0:T(8,128)(2,1)S(1)}, u32[]{:S(2)}, u32[]{:S(2)}) %collective-permute-start.21) | collective-permute-done | bytes 262176 | tf_op jit(solution)/shard_map/ppermute | solution.py:24
  261.0 3.8 collective-permute-start.23
  264.9 2.4 collective-permute-done.23
  267.4 3.7 collective-permute-done.24
  271.1 1.8 convolution_convert_fusion
  272.8 2.9 all-to-all-done.4
  275.7 1.2 copy-done.9
  277.0 4.4 %all-to-all-start.5 = ((bf16[16,24,2048]{2,1,0:T(8,128)(2,1)}), bf16[16,24,2048]{2,1,0:T(8,128)(2,1)}, u32[]{:S(2)}, u32[]{:S(2)}) async-start(bf16[16,24,2048]{2,1,0:T(8,128)(2,1)} %bitcast.22), calls=%async_computation.5 | async-start | bytes 3145728 | tf_op jit(solution)/shard_map/all_to_all | solution.py:62
  281.4 23.7 %all-to-all-done.5 = bf16[16,24,2048]{2,1,0:T(8,128)(2,1)} async-done(((bf16[16,24,2048]{2,1,0:T(8,128)(2,1)}), bf16[16,24,2048]{2,1,0:T(8,128)(2,1)}, u32[]{:S(2)}, u32[]{:S(2)}) %all-to-all-start.5) | async-done | bytes 1572896 | tf_op jit(solution)/shard_map/all_to_all | solution.py:62
  305.1 11.0 %shard_map.89 = bf16[384,2048]{1,0:T(8,128)(2,1)} custom-call(s32[1]{0:T(128)S(6)} %sub.11.flag, bf16[384,4096]{1,0:T(8,128)(2,1)} %bitcast.62, bf16[384,2048]{1,0:T(8,128)(2,1)} %bitcast.23.second, bf16[2048,768]{1,0:T(8,128)(2,1)} %bitcast.73, bf16[2048,768]{1,0:T(8,128)(2,1)} %bitcast.77, bf16[768,2048]{1,0:T(8,128)(2,1)} %bitcast.81), custom_call_target="tpu_custom_call" | custom-call | flops 6039797760 | bytes 14155776 | tf_op jit(solution)/shard_map/pallas_call | solution.py:285
  316.1 3.7 all-to-all-start.6
  319.8 11.1 %shard_map.90 = bf16[384,2048]{1,0:T(8,128)(2,1)} custom-call(s32[1]{0:T(128)S(6)} %sub.11.flag, bf16[384,4096]{1,0:T(8,128)(2,1)} %bitcast.59, bf16[384,2048]{1,0:T(8,128)(2,1)} %bitcast.66, bf16[2048,768]{1,0:T(8,128)(2,1)} %bitcast.74, bf16[2048,768]{1,0:T(8,128)(2,1)} %bitcast.78, bf16[768,2048]{1,0:T(8,128)(2,1)} %bitcast.82), custom_call_target="tpu_custom_call" | custom-call | flops 6039797760 | bytes 14155776 | tf_op jit(solution)/shard_map/pallas_call | solution.py:285
  330.9 12.6 %all-to-all-done.6 = bf16[16,24,2048]{2,1,0:T(8,128)(2,1)S(1)} async-done(((bf16[16,24,2048]{2,1,0:T(8,128)(2,1)}), bf16[16,24,2048]{2,1,0:T(8,128)(2,1)S(1)}, u32[]{:S(2)}, u32[]{:S(2)}) %all-to-all-start.6) | async-done | bytes 1572896 | tf_op jit(solution)/shard_map/all_to_all | solution.py:62
  343.5 1.6 shard_map.92
  345.1 2.7 collective-permute-start.25
  348.7 3.9 all-to-all-start.7
  352.7 3.3 collective-permute-start.26
  356.2 5.9 %collective-permute-done.26 = bf16[64,2048]{1,0:T(8,128)(2,1)S(1)} collective-permute-done((bf16[64,2048]{1,0:T(8,128)(2,1)S(1)}, bf16[64,2048]{1,0:T(8,128)(2,1)S(1)}, u32[]{:S(2)}, u32[]{:S(2)}) %collective-permute-start.26) | collective-permute-done | bytes 262176 | tf_op jit(solution)/shard_map/ppermute | solution.py:24
  362.1 3.8 collective-permute-start.27
  365.9 10.3 %all-to-all-done.7 = bf16[16,24,2048]{2,1,0:T(8,128)(2,1)S(1)} async-done(((bf16[16,24,2048]{2,1,0:T(8,128)(2,1)}), bf16[16,24,2048]{2,1,0:T(8,128)(2,1)S(1)}, u32[]{:S(2)}, u32[]{:S(2)}) %all-to-all-start.7) | async-done | bytes 1572896 | tf_op jit(solution)/shard_map/all_to_all | solution.py:62
  376.3 1.6 shard_map.91
  380.1 3.3 collective-permute-start.28
  383.4 4.9 %collective-permute-done.31 = bf16[64,2048]{1,0:T(8,128)(2,1)S(1)} collective-permute-done((bf16[64,2048]{1,0:T(8,128)(2,1)S(1)}, bf16[64,2048]{1,0:T(8,128)(2,1)S(1)}, u32[]{:S(2)}, u32[]{:S(2)}) %collective-permute-start.31) | collective-permute-done | bytes 262176 | tf_op jit(solution)/shard_map/ppermute | solution.py:24
  388.7 8.2 %collective-permute-done.32 = bf16[64,2048]{1,0:T(8,128)(2,1)S(1)} collective-permute-done((bf16[64,2048]{1,0:T(8,128)(2,1)S(1)}, bf16[64,2048]{1,0:T(8,128)(2,1)S(1)}, u32[]{:S(2)}, u32[]{:S(2)}) %collective-permute-start.32) | collective-permute-done | bytes 262176 | tf_op jit(solution)/shard_map/ppermute | solution.py:24
  397.2 1.1 fusion.21
  (136 shorter events, 14.3 us)
Async XLA Ops:
  4.7 15.0 %collective-permute-start = (bf16[64,4224]{1,0:T(8,128)(2,1)}, bf16[64,4224]{1,0:T(8,128)(2,1)S(1)}, u32[]{:S(2)}, u32[]{:S(2)}) collective-permute-start(bf16[64,4224]{1,0:T(8,128)(2,1)} %shard_map.82.refs_0_), channel_id=1, source_target_pairs={{0,2},{2,4},{4,6},{6,8},{8,10},{10,12},{12,14},{14,0},{1,3},{3,5},... | collective-permute-start | bytes 1622024 | tf_op jit(solution)/shard_map/ppermute | solution.py:24
  7.9 15.4 %collective-permute-start.1 = (bf16[64,4224]{1,0:T(8,128)(2,1)}, bf16[64,4224]{1,0:T(8,128)(2,1)S(1)}, u32[]{:S(2)}, u32[]{:S(2)}) collective-permute-start(bf16[64,4224]{1,0:T(8,128)(2,1)} %shard_map.82.refs_0_), channel_id=1, source_target_pairs={{0,14},{2,0},{4,2},{6,4},{8,6},{10,8},{12,10},{14,12},{1,15},{3,1}... | collective-permute-start | bytes 1622024 | tf_op jit(solution)/shard_map/ppermute | solution.py:24
  19.7 14.3 %copy-start.25 = (bf16[64,4224]{1,0:T(8,128)(2,1)}, bf16[64,4224]{1,0:T(8,128)(2,1)S(1)}, u32[]{:S(2)}) copy-start(bf16[64,4224]{1,0:T(8,128)(2,1)S(1)} %collective-permute-done.refs_1_) | copy-start | bytes 1622020
  19.7 14.2 %collective-permute-start.2 = (bf16[64,4224]{1,0:T(8,128)(2,1)S(1)}, bf16[64,4224]{1,0:T(8,128)(2,1)S(1)}, u32[]{:S(2)}, u32[]{:S(2)}) collective-permute-start(bf16[64,4224]{1,0:T(8,128)(2,1)S(1)} %collective-permute-done.refs_1_), channel_id=1, source_target_pairs={{0,2},{2,4},{4,6},{6,8},{8,10},{10,12},{12,14},{14,0},{1,3},{3,5},... | collective-permute-start | bytes 1622024 | tf_op jit(solution)/shard_map/ppermute | solution.py:24
  23.3 10.7 %copy-start.26 = (bf16[64,4224]{1,0:T(8,128)(2,1)}, bf16[64,4224]{1,0:T(8,128)(2,1)S(1)}, u32[]{:S(2)}) copy-start(bf16[64,4224]{1,0:T(8,128)(2,1)S(1)} %collective-permute-done.1.refs_2_) | copy-start | bytes 1622020
  23.3 16.0 %collective-permute-start.3 = (bf16[64,4224]{1,0:T(8,128)(2,1)S(1)}, bf16[64,4224]{1,0:T(8,128)(2,1)S(1)}, u32[]{:S(2)}, u32[]{:S(2)}) collective-permute-start(bf16[64,4224]{1,0:T(8,128)(2,1)S(1)} %collective-permute-done.1.refs_2_), channel_id=1, source_target_pairs={{0,14},{2,0},{4,2},{6,4},{8,6},{10,8},{12,10},{14,12},{1,15},{3,1}... | collective-permute-start | bytes 1622024 | tf_op jit(solution)/shard_map/ppermute | solution.py:24
  40.1 47.6 %all-to-all-start = ((bf16[16,24,4096]{2,1,0:T(8,128)(2,1)}), bf16[16,24,4096]{2,1,0:T(8,128)(2,1)S(1)}, u32[]{:S(2)}, u32[]{:S(2)}) async-start(bf16[16,24,4096]{2,1,0:T(8,128)(2,1)} %bitcast.63), calls=%async_computation | async-start | bytes 6291456 | tf_op jit(solution)/shard_map/all_to_all | solution.py:62
  47.1 16.7 %collective-permute-start.5 = (bf16[64,4224]{1,0:T(8,128)(2,1)}, bf16[64,4224]{1,0:T(8,128)(2,1)S(1)}, u32[]{:S(2)}, u32[]{:S(2)}) collective-permute-start(bf16[64,4224]{1,0:T(8,128)(2,1)} %copy-done.23), channel_id=1, source_target_pairs={{0,14},{2,0},{4,2},{6,4},{8,6},{10,8},{12,10},{14,12},{1,15},{3,1}... | collective-permute-start | bytes 1622024 | tf_op jit(solution)/shard_map/ppermute | solution.py:24
  47.2 16.8 %collective-permute-start.4 = (bf16[64,4224]{1,0:T(8,128)(2,1)}, bf16[64,4224]{1,0:T(8,128)(2,1)S(1)}, u32[]{:S(2)}, u32[]{:S(2)}) collective-permute-start(bf16[64,4224]{1,0:T(8,128)(2,1)} %copy-done.24), channel_id=1, source_target_pairs={{0,2},{2,4},{4,6},{6,8},{8,10},{10,12},{12,14},{14,0},{1,3},{3,5},... | collective-permute-start | bytes 1622024 | tf_op jit(solution)/shard_map/ppermute | solution.py:24
  63.8 10.4 %copy-start.21 = (bf16[64,4224]{1,0:T(8,128)(2,1)}, bf16[64,4224]{1,0:T(8,128)(2,1)S(1)}, u32[]{:S(2)}) copy-start(bf16[64,4224]{1,0:T(8,128)(2,1)S(1)} %collective-permute-done.5.refs_2_) | copy-start | bytes 1622020
  63.9 9.5 %collective-permute-start.7 = (bf16[32,4224]{1,0:T(8,128)(2,1)S(1)}, bf16[32,4224]{1,0:T(8,128)(2,1)S(1)}, u32[]{:S(2)}, u32[]{:S(2)}) collective-permute-start(bf16[32,4224]{1,0:T(8,128)(2,1)S(1)} %slice.69), channel_id=1, source_target_pairs={{0,14},{2,0},{4,2},{6,4},{8,6},{10,8},{12,10},{14,12},{1,15},{3,1}... | collective-permute-start | bytes 811016 | tf_op jit(solution)/shard_map/ppermute | solution.py:24
  64.0 10.3 %copy-start.22 = (bf16[64,4224]{1,0:T(8,128)(2,1)}, bf16[64,4224]{1,0:T(8,128)(2,1)S(1)}, u32[]{:S(2)}) copy-start(bf16[64,4224]{1,0:T(8,128)(2,1)S(1)} %collective-permute-done.4.refs_1_) | copy-start | bytes 1622020
  64.0 9.4 %collective-permute-start.6 = (bf16[32,4224]{1,0:T(8,128)(2,1)S(1)}, bf16[32,4224]{1,0:T(8,128)(2,1)S(1)}, u32[]{:S(2)}, u32[]{:S(2)}) collective-permute-start(bf16[32,4224]{1,0:T(8,128)(2,1)S(1)} %slice.68), channel_id=1, source_target_pairs={{0,2},{2,4},{4,6},{6,8},{8,10},{10,12},{12,14},{14,0},{1,3},{3,5},... | collective-permute-start | bytes 811016 | tf_op jit(solution)/shard_map/ppermute | solution.py:24
  87.7 44.9 %copy-start.7 = (bf16[16,24,4096]{2,1,0:T(8,128)(2,1)}, bf16[16,24,4096]{2,1,0:T(8,128)(2,1)S(1)}, u32[]{:S(2)}) copy-start(bf16[16,24,4096]{2,1,0:T(8,128)(2,1)S(1)} %all-to-all-done) | copy-start | bytes 9437188
  142.4 27.4 %all-to-all-start.2 = ((bf16[16,24,2048]{2,1,0:T(8,128)(2,1)}), bf16[16,24,2048]{2,1,0:T(8,128)(2,1)S(1)}, u32[]{:S(2)}, u32[]{:S(2)}) async-start(bf16[16,24,2048]{2,1,0:T(8,128)(2,1)} %bitcast.70), calls=%async_computation.2 | async-start | bytes 3145728 | tf_op jit(solution)/shard_map/all_to_all | solution.py:62
  146.2 23.7 %copy-start.5 = (bf16[384,256]{1,0:T(8,128)(2,1)S(1)}, bf16[384,256]{1,0:T(8,128)(2,1)}, u32[]{:S(2)}) copy-start(bf16[384,256]{1,0:T(8,128)(2,1)} %get-tuple-element.53.weighing) | copy-start | bytes 589828
  171.5 8.5 %collective-permute-start.8 = (bf16[32,2048]{1,0:T(8,128)(2,1)}, bf16[32,2048]{1,0:T(8,128)(2,1)S(1)}, u32[]{:S(2)}, u32[]{:S(2)}) collective-permute-start(bf16[32,2048]{1,0:T(8,128)(2,1)} %get-tuple-element.57), channel_id=1, source_target_pairs={{0,2},{2,4},{4,6},{6,8},{8,10},{10,12},{12,14},{14,0},{1,3},{3,5},... | collective-permute-start | bytes 393224 | tf_op jit(solution)/shard_map/ppermute | solution.py:24
  175.1 8.2 %collective-permute-start.12 = (bf16[32,2048]{1,0:T(8,128)(2,1)}, bf16[32,2048]{1,0:T(8,128)(2,1)S(1)}, u32[]{:S(2)}, u32[]{:S(2)}) collective-permute-start(bf16[32,2048]{1,0:T(8,128)(2,1)} %get-tuple-element.61), channel_id=1, source_target_pairs={{0,14},{2,0},{4,2},{6,4},{8,6},{10,8},{12,10},{14,12},{1,15},{3,1}... | collective-permute-start | bytes 393224 | tf_op jit(solution)/shard_map/ppermute | solution.py:24
  176.1 3.9 copy-start.18
  176.1 7.3 %copy-start.16 = (bf16[64,2048]{1,0:T(8,128)(2,1)S(1)}, bf16[64,2048]{1,0:T(8,128)(2,1)}, u32[]{:S(2)}) copy-start(bf16[64,2048]{1,0:T(8,128)(2,1)} %get-tuple-element.60) | copy-start | bytes 786436
  176.1 27.5 %all-to-all-start.3 = ((bf16[16,24,2048]{2,1,0:T(8,128)(2,1)}), bf16[16,24,2048]{2,1,0:T(8,128)(2,1)S(1)}, u32[]{:S(2)}, u32[]{:S(2)}) async-start(bf16[16,24,2048]{2,1,0:T(8,128)(2,1)} %bitcast.17), calls=%async_computation.3 | async-start | bytes 3145728 | tf_op jit(solution)/shard_map/all_to_all | solution.py:62
  179.9 9.5 %copy-start.12 = (bf16[64,2048]{1,0:T(8,128)(2,1)S(1)}, bf16[64,2048]{1,0:T(8,128)(2,1)}, u32[]{:S(2)}) copy-start(bf16[64,2048]{1,0:T(8,128)(2,1)} %get-tuple-element.55) | copy-start | bytes 786436
  180.0 23.6 %copy-start.4 = (bf16[384,256]{1,0:T(8,128)(2,1)S(1)}, bf16[384,256]{1,0:T(8,128)(2,1)}, u32[]{:S(2)}) copy-start(bf16[384,256]{1,0:T(8,128)(2,1)} %get-tuple-element.42.weighing) | copy-start | bytes 589828
  180.1 9.3 %collective-permute-start.9 = (bf16[64,2048]{1,0:T(8,128)(2,1)S(1)}, bf16[64,2048]{1,0:T(8,128)(2,1)S(1)}, u32[]{:S(2)}, u32[]{:S(2)}) collective-permute-start(bf16[64,2048]{1,0:T(8,128)(2,1)S(1)} %pad_maximum_fusion.1), channel_id=1, source_target_pairs={{0,2},{2,4},{4,6},{6,8},{8,10},{10,12},{12,14},{14,0},{1,3},{3,5},... | collective-permute-start | bytes 786440 | tf_op jit(solution)/shard_map/ppermute | solution.py:24
  183.5 21.8 %collective-permute-start.13 = (bf16[64,2048]{1,0:T(8,128)(2,1)S(1)}, bf16[64,2048]{1,0:T(8,128)(2,1)S(1)}, u32[]{:S(2)}, u32[]{:S(2)}) collective-permute-start(bf16[64,2048]{1,0:T(8,128)(2,1)S(1)} %pad_maximum_fusion.2), channel_id=1, source_target_pairs={{0,14},{2,0},{4,2},{6,4},{8,6},{10,8},{12,10},{14,12},{1,15},{3,1}... | collective-permute-start | bytes 786440 | tf_op jit(solution)/shard_map/ppermute | solution.py:24
  189.5 17.0 %collective-permute-start.10 = (bf16[64,2048]{1,0:T(8,128)(2,1)S(1)}, bf16[64,2048]{1,0:T(8,128)(2,1)S(1)}, u32[]{:S(2)}, u32[]{:S(2)}) collective-permute-start(bf16[64,2048]{1,0:T(8,128)(2,1)S(1)} %add_convert_fusion.7), channel_id=1, source_target_pairs={{0,2},{2,4},{4,6},{6,8},{8,10},{10,12},{12,14},{14,0},{1,3},{3,5},... | collective-permute-start | bytes 786440 | tf_op jit(solution)/shard_map/ppermute | solution.py:24
  205.2 10.5 %copy-start.14 = (bf16[64,2048]{1,0:T(8,128)(2,1)S(1)}, bf16[64,2048]{1,0:T(8,128)(2,1)}, u32[]{:S(2)}) copy-start(bf16[64,2048]{1,0:T(8,128)(2,1)} %get-tuple-element.58) | copy-start | bytes 786436
  205.2 19.1 %copy-start.1 = (f32[1,2048]{1,0:T(1,128)S(1)}, f32[1,2048]{1,0:T(1,128)}, u32[]{:S(2)}) copy-start(f32[1,2048]{1,0:T(1,128)} %gain.1) | copy-start | bytes 24580
  205.2 19.1 %copy-start.6 = (bf16[1,64,2048]{2,1,0:T(8,128)(2,1)S(1)}, bf16[1,64,2048]{2,1,0:T(8,128)(2,1)}, u32[]{:S(2)}) copy-start(bf16[1,64,2048]{2,1,0:T(8,128)(2,1)} %param.9) | copy-start | bytes 786436
  205.2 19.1 %copy-start.8 = (bf16[1,64,2048]{2,1,0:T(8,128)(2,1)S(1)}, bf16[1,64,2048]{2,1,0:T(8,128)(2,1)}, u32[]{:S(2)}) copy-start(bf16[1,64,2048]{2,1,0:T(8,128)(2,1)} %param.8) | copy-start | bytes 786436
  205.3 19.1 %copy-start.10 = (bf16[64,2048]{1,0:T(8,128)(2,1)S(1)}, bf16[64,2048]{1,0:T(8,128)(2,1)}, u32[]{:S(2)}) copy-start(bf16[64,2048]{1,0:T(8,128)(2,1)} %get-tuple-element.51) | copy-start | bytes 786436
  206.4 9.4 %collective-permute-start.14 = (bf16[64,2048]{1,0:T(8,128)(2,1)S(1)}, bf16[64,2048]{1,0:T(8,128)(2,1)S(1)}, u32[]{:S(2)}, u32[]{:S(2)}) collective-permute-start(bf16[64,2048]{1,0:T(8,128)(2,1)S(1)} %add_convert_fusion.5), channel_id=1, source_target_pairs={{0,14},{2,0},{4,2},{6,4},{8,6},{10,8},{12,10},{14,12},{1,15},{3,1}... | collective-permute-start | bytes 786440 | tf_op jit(solution)/shard_map/ppermute | solution.py:24
  207.5 8.8 %collective-permute-start.11 = (bf16[64,2048]{1,0:T(8,128)(2,1)S(1)}, bf16[64,2048]{1,0:T(8,128)(2,1)S(1)}, u32[]{:S(2)}, u32[]{:S(2)}) collective-permute-start(bf16[64,2048]{1,0:T(8,128)(2,1)S(1)} %add_convert_fusion.6), channel_id=1, source_target_pairs={{0,2},{2,4},{4,6},{6,8},{8,10},{10,12},{12,14},{14,0},{1,3},{3,5},... | collective-permute-start | bytes 786440 | tf_op jit(solution)/shard_map/ppermute | solution.py:24
  215.8 8.5 %collective-permute-start.15 = (bf16[64,2048]{1,0:T(8,128)(2,1)S(1)}, bf16[64,2048]{1,0:T(8,128)(2,1)S(1)}, u32[]{:S(2)}, u32[]{:S(2)}) collective-permute-start(bf16[64,2048]{1,0:T(8,128)(2,1)S(1)} %add_convert_fusion.4), channel_id=1, source_target_pairs={{0,14},{2,0},{4,2},{6,4},{8,6},{10,8},{12,10},{14,12},{1,15},{3,1}... | collective-permute-start | bytes 786440 | tf_op jit(solution)/shard_map/ppermute | solution.py:24
  224.7 21.6 %copy-start.27 = (bf16[384,256]{1,0:T(8,128)(2,1)S(1)}, bf16[384,256]{1,0:T(8,128)(2,1)}, u32[]{:S(2)}) copy-start(bf16[384,256]{1,0:T(8,128)(2,1)} %get-tuple-element.63) | copy-start | bytes 589828
  225.1 6.5 %collective-permute-start.16 = (bf16[64,2048]{1,0:T(8,128)(2,1)S(1)}, bf16[64,2048]{1,0:T(8,128)(2,1)S(1)}, u32[]{:S(2)}, u32[]{:S(2)}) collective-permute-start(bf16[64,2048]{1,0:T(8,128)(2,1)S(1)} %fusion.8), channel_id=1, source_target_pairs={{0,128},{128,0},{1,129},{129,1},{2,130},{130,2},{3,131},{131,3},{4... | collective-permute-start | bytes 786440 | tf_op jit(solution)/shard_map/ppermute | solution.py:376
  232.0 8.0 %collective-permute-start.17 = (bf16[64,2048]{1,0:T(8,128)(2,1)S(1)}, bf16[64,2048]{1,0:T(8,128)(2,1)S(1)}, u32[]{:S(2)}, u32[]{:S(2)}) collective-permute-start(bf16[64,2048]{1,0:T(8,128)(2,1)S(1)} %fusion.22), channel_id=1, source_target_pairs={{0,2},{2,4},{4,6},{6,8},{8,10},{10,12},{12,14},{14,0},{1,3},{3,5},... | collective-permute-start | bytes 786440 | tf_op jit(solution)/shard_map/ppermute | solution.py:24
  232.3 8.0 %collective-permute-start.18 = (bf16[64,2048]{1,0:T(8,128)(2,1)S(1)}, bf16[64,2048]{1,0:T(8,128)(2,1)S(1)}, u32[]{:S(2)}, u32[]{:S(2)}) collective-permute-start(bf16[64,2048]{1,0:T(8,128)(2,1)S(1)} %fusion.22), channel_id=1, source_target_pairs={{0,14},{2,0},{4,2},{6,4},{8,6},{10,8},{12,10},{14,12},{1,15},{3,1}... | collective-permute-start | bytes 786440 | tf_op jit(solution)/shard_map/ppermute | solution.py:24
  239.9 6.4 %collective-permute-start.19 = (bf16[64,2048]{1,0:T(8,128)(2,1)S(1)}, bf16[64,2048]{1,0:T(8,128)(2,1)S(1)}, u32[]{:S(2)}, u32[]{:S(2)}) collective-permute-start(bf16[64,2048]{1,0:T(8,128)(2,1)S(1)} %collective-permute-done.17), channel_id=1, source_target_pairs={{0,2},{2,4},{4,6},{6,8},{8,10},{10,12},{12,14},{14,0},{1,3},{3,5},... | collective-permute-start | bytes 786440 | tf_op jit(solution)/shard_map/ppermute | solution.py:24
  240.3 14.6 %collective-permute-start.20 = (bf16[64,2048]{1,0:T(8,128)(2,1)S(1)}, bf16[64,2048]{1,0:T(8,128)(2,1)S(1)}, u32[]{:S(2)}, u32[]{:S(2)}) collective-permute-start(bf16[64,2048]{1,0:T(8,128)(2,1)S(1)} %collective-permute-done.18), channel_id=1, source_target_pairs={{0,14},{2,0},{4,2},{6,4},{8,6},{10,8},{12,10},{14,12},{1,15},{3,1}... | collective-permute-start | bytes 786440 | tf_op jit(solution)/shard_map/ppermute | solution.py:24
  248.1 27.6 %all-to-all-start.4 = ((bf16[16,24,2048]{2,1,0:T(8,128)(2,1)}), bf16[16,24,2048]{2,1,0:T(8,128)(2,1)S(1)}, u32[]{:S(2)}, u32[]{:S(2)}) async-start(bf16[16,24,2048]{2,1,0:T(8,128)(2,1)} %bitcast.68), calls=%async_computation.4 | async-start | bytes 3145728 | tf_op jit(solution)/shard_map/all_to_all | solution.py:62
  252.0 19.0 %copy-start.20 = (bf16[384,256]{1,0:T(8,128)(2,1)S(1)}, bf16[384,256]{1,0:T(8,128)(2,1)}, u32[]{:S(2)}) copy-start(bf16[384,256]{1,0:T(8,128)(2,1)} %get-tuple-element.64) | copy-start | bytes 589828
  252.1 8.9 %collective-permute-start.21 = (bf16[64,2048]{1,0:T(8,128)(2,1)S(1)}, bf16[64,2048]{1,0:T(8,128)(2,1)S(1)}, u32[]{:S(2)}, u32[]{:S(2)}) collective-permute-start(bf16[64,2048]{1,0:T(8,128)(2,1)S(1)} %collective-permute-done.19), channel_id=1, source_target_pairs={{0,2},{2,4},{4,6},{6,8},{8,10},{10,12},{12,14},{14,0},{1,3},{3,5},... | collective-permute-start | bytes 786440 | tf_op jit(solution)/shard_map/ppermute | solution.py:24
  254.8 9.9 %collective-permute-start.22 = (bf16[64,2048]{1,0:T(8,128)(2,1)S(1)}, bf16[64,2048]{1,0:T(8,128)(2,1)S(1)}, u32[]{:S(2)}, u32[]{:S(2)}) collective-permute-start(bf16[64,2048]{1,0:T(8,128)(2,1)S(1)} %collective-permute-done.20), channel_id=1, source_target_pairs={{0,14},{2,0},{4,2},{6,4},{8,6},{10,8},{12,10},{14,12},{1,15},{3,1}... | collective-permute-start | bytes 786440 | tf_op jit(solution)/shard_map/ppermute | solution.py:24
  261.0 6.3 %collective-permute-start.23 = (bf16[32,2048]{1,0:T(8,128)(2,1)S(1)}, bf16[32,2048]{1,0:T(8,128)(2,1)S(1)}, u32[]{:S(2)}, u32[]{:S(2)}) collective-permute-start(bf16[32,2048]{1,0:T(8,128)(2,1)S(1)} %slice.70), channel_id=1, source_target_pairs={{0,2},{2,4},{4,6},{6,8},{8,10},{10,12},{12,14},{14,0},{1,3},{3,5},... | collective-permute-start | bytes 393224 | tf_op jit(solution)/shard_map/ppermute | solution.py:24
  264.8 6.3 %collective-permute-start.24 = (bf16[32,2048]{1,0:T(8,128)(2,1)S(1)}, bf16[32,2048]{1,0:T(8,128)(2,1)S(1)}, u32[]{:S(2)}, u32[]{:S(2)}) collective-permute-start(bf16[32,2048]{1,0:T(8,128)(2,1)S(1)} %slice.71), channel_id=1, source_target_pairs={{0,14},{2,0},{4,2},{6,4},{8,6},{10,8},{12,10},{14,12},{1,15},{3,1}... | collective-permute-start | bytes 393224 | tf_op jit(solution)/shard_map/ppermute | solution.py:24
  277.0 28.1 %all-to-all-start.5 = ((bf16[16,24,2048]{2,1,0:T(8,128)(2,1)}), bf16[16,24,2048]{2,1,0:T(8,128)(2,1)}, u32[]{:S(2)}, u32[]{:S(2)}) async-start(bf16[16,24,2048]{2,1,0:T(8,128)(2,1)} %bitcast.22), calls=%async_computation.5 | async-start | bytes 3145728 | tf_op jit(solution)/shard_map/all_to_all | solution.py:62
  316.1 27.4 %all-to-all-start.6 = ((bf16[16,24,2048]{2,1,0:T(8,128)(2,1)}), bf16[16,24,2048]{2,1,0:T(8,128)(2,1)S(1)}, u32[]{:S(2)}, u32[]{:S(2)}) async-start(bf16[16,24,2048]{2,1,0:T(8,128)(2,1)} %bitcast.69), calls=%async_computation.6 | async-start | bytes 3145728 | tf_op jit(solution)/shard_map/all_to_all | solution.py:62
  319.8 23.7 %copy-start.3 = (bf16[384,256]{1,0:T(8,128)(2,1)S(1)}, bf16[384,256]{1,0:T(8,128)(2,1)}, u32[]{:S(2)}) copy-start(bf16[384,256]{1,0:T(8,128)(2,1)} %get-tuple-element.70.weighing) | copy-start | bytes 589828
  345.1 7.6 %collective-permute-start.25 = (bf16[32,2048]{1,0:T(8,128)(2,1)}, bf16[32,2048]{1,0:T(8,128)(2,1)S(1)}, u32[]{:S(2)}, u32[]{:S(2)}) collective-permute-start(bf16[32,2048]{1,0:T(8,128)(2,1)} %get-tuple-element.74), channel_id=1, source_target_pairs={{0,2},{2,4},{4,6},{6,8},{8,10},{10,12},{12,14},{14,0},{1,3},{3,5},... | collective-permute-start | bytes 393224 | tf_op jit(solution)/shard_map/ppermute | solution.py:24
  347.8 8.2 %collective-permute-start.29 = (bf16[32,2048]{1,0:T(8,128)(2,1)}, bf16[32,2048]{1,0:T(8,128)(2,1)S(1)}, u32[]{:S(2)}, u32[]{:S(2)}) collective-permute-start(bf16[32,2048]{1,0:T(8,128)(2,1)} %get-tuple-element.78), channel_id=1, source_target_pairs={{0,14},{2,0},{4,2},{6,4},{8,6},{10,8},{12,10},{14,12},{1,15},{3,1}... | collective-permute-start | bytes 393224 | tf_op jit(solution)/shard_map/ppermute | solution.py:24
  348.7 3.9 copy-start.19
  348.7 7.3 %copy-start.17 = (bf16[64,2048]{1,0:T(8,128)(2,1)S(1)}, bf16[64,2048]{1,0:T(8,128)(2,1)}, u32[]{:S(2)}) copy-start(bf16[64,2048]{1,0:T(8,128)(2,1)} %get-tuple-element.77) | copy-start | bytes 786436
  348.7 27.5 %all-to-all-start.7 = ((bf16[16,24,2048]{2,1,0:T(8,128)(2,1)}), bf16[16,24,2048]{2,1,0:T(8,128)(2,1)S(1)}, u32[]{:S(2)}, u32[]{:S(2)}) async-start(bf16[16,24,2048]{2,1,0:T(8,128)(2,1)} %bitcast.67), calls=%async_computation.7 | async-start | bytes 3145728 | tf_op jit(solution)/shard_map/all_to_all | solution.py:62
  352.6 9.5 %copy-start.13 = (bf16[64,2048]{1,0:T(8,128)(2,1)S(1)}, bf16[64,2048]{1,0:T(8,128)(2,1)}, u32[]{:S(2)}) copy-start(bf16[64,2048]{1,0:T(8,128)(2,1)} %get-tuple-element.72) | copy-start | bytes 786436
  352.6 23.6 %copy-start.2 = (bf16[384,256]{1,0:T(8,128)(2,1)S(1)}, bf16[384,256]{1,0:T(8,128)(2,1)}, u32[]{:S(2)}) copy-start(bf16[384,256]{1,0:T(8,128)(2,1)} %get-tuple-element.62.weighing) | copy-start | bytes 589828
  352.7 9.3 %collective-permute-start.26 = (bf16[64,2048]{1,0:T(8,128)(2,1)S(1)}, bf16[64,2048]{1,0:T(8,128)(2,1)S(1)}, u32[]{:S(2)}, u32[]{:S(2)}) collective-permute-start(bf16[64,2048]{1,0:T(8,128)(2,1)S(1)} %pad_maximum_fusion.3), channel_id=1, source_target_pairs={{0,2},{2,4},{4,6},{6,8},{8,10},{10,12},{12,14},{14,0},{1,3},{3,5},... | collective-permute-start | bytes 786440 | tf_op jit(solution)/shard_map/ppermute | solution.py:24
  356.1 21.8 %collective-permute-start.30 = (bf16[64,2048]{1,0:T(8,128)(2,1)S(1)}, bf16[64,2048]{1,0:T(8,128)(2,1)S(1)}, u32[]{:S(2)}, u32[]{:S(2)}) collective-permute-start(bf16[64,2048]{1,0:T(8,128)(2,1)S(1)} %pad_maximum_fusion.4), channel_id=1, source_target_pairs={{0,14},{2,0},{4,2},{6,4},{8,6},{10,8},{12,10},{14,12},{1,15},{3,1}... | collective-permute-start | bytes 786440 | tf_op jit(solution)/shard_map/ppermute | solution.py:24
  362.1 16.9 %collective-permute-start.27 = (bf16[64,2048]{1,0:T(8,128)(2,1)S(1)}, bf16[64,2048]{1,0:T(8,128)(2,1)S(1)}, u32[]{:S(2)}, u32[]{:S(2)}) collective-permute-start(bf16[64,2048]{1,0:T(8,128)(2,1)S(1)} %add_convert_fusion.3), channel_id=1, source_target_pairs={{0,2},{2,4},{4,6},{6,8},{8,10},{10,12},{12,14},{14,0},{1,3},{3,5},... | collective-permute-start | bytes 786440 | tf_op jit(solution)/shard_map/ppermute | solution.py:24
  377.9 10.5 %copy-start.15 = (bf16[64,2048]{1,0:T(8,128)(2,1)S(1)}, bf16[64,2048]{1,0:T(8,128)(2,1)}, u32[]{:S(2)}) copy-start(bf16[64,2048]{1,0:T(8,128)(2,1)} %get-tuple-element.75) | copy-start | bytes 786436
  377.9 19.0 %copy-start.11 = (bf16[64,2048]{1,0:T(8,128)(2,1)S(1)}, bf16[64,2048]{1,0:T(8,128)(2,1)}, u32[]{:S(2)}) copy-start(bf16[64,2048]{1,0:T(8,128)(2,1)} %get-tuple-element.68) | copy-start | bytes 786436
  379.0 9.4 %collective-permute-start.31 = (bf16[64,2048]{1,0:T(8,128)(2,1)S(1)}, bf16[64,2048]{1,0:T(8,128)(2,1)S(1)}, u32[]{:S(2)}, u32[]{:S(2)}) collective-permute-start(bf16[64,2048]{1,0:T(8,128)(2,1)S(1)} %add_convert_fusion.1), channel_id=1, source_target_pairs={{0,14},{2,0},{4,2},{6,4},{8,6},{10,8},{12,10},{14,12},{1,15},{3,1}... | collective-permute-start | bytes 786440 | tf_op jit(solution)/shard_map/ppermute | solution.py:24
  380.1 8.6 %collective-permute-start.28 = (bf16[64,2048]{1,0:T(8,128)(2,1)S(1)}, bf16[64,2048]{1,0:T(8,128)(2,1)S(1)}, u32[]{:S(2)}, u32[]{:S(2)}) collective-permute-start(bf16[64,2048]{1,0:T(8,128)(2,1)S(1)} %add_convert_fusion.2), channel_id=1, source_target_pairs={{0,2},{2,4},{4,6},{6,8},{8,10},{10,12},{12,14},{14,0},{1,3},{3,5},... | collective-permute-start | bytes 786440 | tf_op jit(solution)/shard_map/ppermute | solution.py:24
  388.4 8.5 %collective-permute-start.32 = (bf16[64,2048]{1,0:T(8,128)(2,1)S(1)}, bf16[64,2048]{1,0:T(8,128)(2,1)S(1)}, u32[]{:S(2)}, u32[]{:S(2)}) collective-permute-start(bf16[64,2048]{1,0:T(8,128)(2,1)S(1)} %add_convert_fusion), channel_id=1, source_target_pairs={{0,14},{2,0},{4,2},{6,4},{8,6},{10,8},{12,10},{14,12},{1,15},{3,1}... | collective-permute-start | bytes 786440 | tf_op jit(solution)/shard_map/ppermute | solution.py:24
  (4 other events, 3.5 us)
